TPU v7x, 32 devices: a whole 2x2x4 slice. The times are simulated.
32 devices in a mesh: dp: 8 (over y, x, core), tensor: 4 (over z).
Axes of the slice: x: 2, y: 2, z: 4, core: 2. Of those that a mesh axis runs over, the one named last changes fastest.
Arguments:
- block_in: bfloat16 [2, 8, 1024, 1280], P(None, 'dp', 'tensor'), may hold values from -6 to 6
- out_grad: float32 [2, 8, 1024, 1280], P(None, 'dp', 'tensor'), may hold values from -6 to 6
- global_pos: int32 [2, 8, 64], P(None, 'dp'), may hold values from 0 to 1023, as said below
- w_query: bfloat16 [1280, 1280], P('dp', 'tensor'), may hold values from -0.15625 to 0.15625
- w_key: bfloat16 [1280, 1280], P('dp', 'tensor'), may hold values from -0.15625 to 0.15625
- w_value: bfloat16 [1280, 1280], P('dp', 'tensor'), may hold values from -0.15625 to 0.15625
- w_out: bfloat16 [1280, 1280], P('dp', 'tensor'), may hold values from -0.15625 to 0.15625
- w_up: bfloat16 [1280, 5120], P('dp', 'tensor'), may hold values from -0.15625 to 0.15625
- w_gate: bfloat16 [1280, 5120], P('dp', 'tensor'), may hold values from -0.15625 to 0.15625
- w_down: bfloat16 [1280, 5120], P('dp', 'tensor'), may hold values from -0.078125 to 0.078125
- qk_gain: float32 [1280], P('tensor'), may hold values from 0.8 to 1.6
- up_gain: float32 [5120], P('tensor'), may hold values from 0.5 to 1.5
- gate_gain: float32 [5120], P('tensor'), may hold values from 0.5 to 1.5
- att_rate: float32 [1280], replicated, may hold values from 0.2 to 0.8
- mlp_rate: float32 [1280], replicated, may hold values from 0.2 to 0.8
Outputs:
- block_out: float32 [2, 8, 1024, 1280], P(None, 'dp', 'tensor')
- in_grad: float32 [2, 8, 1024, 1280], P(None, 'dp', 'tensor')
- grad_query: float32 [1280, 1280], P('dp', 'tensor')
- grad_key: float32 [1280, 1280], P('dp', 'tensor')
- grad_value: float32 [1280, 1280], P('dp', 'tensor')
- grad_out: float32 [1280, 1280], P('dp', 'tensor')
- grad_up: float32 [1280, 5120], P('dp', 'tensor')
- grad_gate: float32 [1280, 5120], P('dp', 'tensor')
- grad_down: float32 [1280, 5120], P('dp', 'tensor')
- grad_qk_gain: float32 [1280], P('tensor')
- grad_up_gain: float32 [5120], P('tensor')
- grad_gate_gain: float32 [5120], P('tensor')
- grad_att_rate: float32 [1280], replicated
- grad_mlp_rate: float32 [1280], replicated
Inputs may be any that keep to these rules, and one draw needn't show every extreme that they name: `global_pos`: each row holds 64 distinct positions of its sequence.
All inputs are finite; a program needn't handle non-finite values.
Results may differ from a plain program's by a relative error of at most 0.023.
Values may be sent and summed in bfloat16 or wider, within the bound.
No kernel may reach another device: no remote copies, remote signals or barrier semaphores. Data moves between devices by JAX's collectives and lax.ppermute only.
A program may use at most 256 MiB of HBM per device.

v0:
```python
import math

import jax
import jax.numpy as jnp
from jax import lax
from jax.sharding import PartitionSpec as P

HD = 64
WINDOW = 512


epsilon = 1e-06
blocked = -1e30


def row_norm(values):
    return values * lax.rsqrt(jnp.mean(values * values, axis=-1, keepdims=True) + epsilon)


def head_norm(values, gain):
    shaped = values.reshape(values.shape[:-1] + (values.shape[-1] // HD, HD))
    normed = shaped * lax.rsqrt(jnp.mean(shaped * shaped, axis=-1, keepdims=True) + epsilon)
    return normed.reshape(values.shape) * gain


def both_heads(query_raw, key_raw, gain):
    return (head_norm(query_raw, gain), head_norm(key_raw, gain))


def settle(base, branch, rate):
    return row_norm(base + rate * (row_norm(branch) - base))


def swish_gate(up_raw, gate_raw, up_gain, gate_gain):
    lifted = gate_gain * gate_raw
    return up_gain * up_raw * (lifted * jax.nn.sigmoid(lifted))


def window_mask(global_flags, row_start, row_count):
    places = jnp.arange(global_flags.shape[0], dtype=jnp.int32)
    row_ids = row_start + jnp.arange(row_count, dtype=jnp.int32)
    in_window = row_ids[:, None] - places[None, :] < WINDOW
    causal = places[None, :] <= row_ids[:, None]
    row_flags = global_flags[row_start : row_start + row_count]
    return causal & (in_window | row_flags[:, None] | global_flags[None, :])


def attend_forward(queries, key_rows, value_rows, global_flags):
    seq_len = queries.shape[0]
    block_rows = min(512, seq_len)
    outputs = []
    log_totals = []
    for block_start in range(0, seq_len, block_rows):
        query_block = queries[block_start : block_start + block_rows]
        scores = jnp.einsum(
            "qhd,khd->hqk", query_block, key_rows, preferred_element_type=jnp.float32
        ) / math.sqrt(HD)
        allow_mask = window_mask(global_flags, block_start, block_rows)
        masked = jnp.where(allow_mask[None], scores, blocked)
        row_peak = jnp.max(masked, axis=-1, keepdims=True)
        raised = jnp.exp(masked - row_peak)
        row_total = jnp.sum(raised, axis=-1, keepdims=True)
        probs_low = (raised / row_total).astype(jnp.bfloat16)
        outputs.append(
            jnp.einsum("hqk,khd->qhd", probs_low, value_rows, preferred_element_type=jnp.float32)
        )
        log_totals.append(row_peak + jnp.log(row_total))
    return (jnp.concatenate(outputs, axis=0), jnp.concatenate(log_totals, axis=1))


def attend_backward(queries, key_rows, value_rows, log_totals, mixed_grad, global_flags):
    seq_len = queries.shape[0]
    block_rows = min(512, seq_len)
    query_parts = []
    key_total = jnp.zeros(key_rows.shape, jnp.float32)
    value_total = jnp.zeros(value_rows.shape, jnp.float32)
    for block_start in range(0, seq_len, block_rows):
        query_block = queries[block_start : block_start + block_rows]
        grad_block = mixed_grad[block_start : block_start + block_rows]
        scores = jnp.einsum(
            "qhd,khd->hqk", query_block, key_rows, preferred_element_type=jnp.float32
        ) / math.sqrt(HD)
        allow_mask = window_mask(global_flags, block_start, block_rows)
        block_totals = log_totals[:, block_start : block_start + block_rows]
        probs = jnp.where(
            allow_mask[None],
            jnp.exp(jnp.where(allow_mask[None], scores, blocked) - block_totals),
            0.0,
        )
        prob_grad = jnp.einsum(
            "qhd,khd->hqk", grad_block, value_rows, preferred_element_type=jnp.float32
        )
        inner = jnp.sum(probs * prob_grad, axis=-1, keepdims=True)
        score_grad = (probs * (prob_grad - inner)).astype(jnp.bfloat16)
        query_parts.append(
            jnp.einsum("hqk,khd->qhd", score_grad, key_rows, preferred_element_type=jnp.float32)
            / math.sqrt(HD)
        )
        key_total = key_total + jnp.einsum(
            "hqk,qhd->khd", score_grad, query_block, preferred_element_type=jnp.float32
        ) / math.sqrt(HD)
        value_total = value_total + jnp.einsum(
            "hqk,qhd->khd",
            probs.astype(jnp.bfloat16),
            grad_block,
            preferred_element_type=jnp.float32,
        )
    return (jnp.concatenate(query_parts, axis=0), key_total, value_total)


def fetch_attn(w_query, w_key, w_value, w_out):
    return (
        lax.all_gather(w_query, "dp", axis=0, tiled=True),
        lax.all_gather(w_key, "dp", axis=0, tiled=True),
        lax.all_gather(w_value, "dp", axis=0, tiled=True),
        lax.all_gather(w_out, "dp", axis=0, tiled=True),
    )


def fetch_mlp(w_up, w_gate, w_down):
    return (
        lax.all_gather(w_up, "dp", axis=0, tiled=True),
        lax.all_gather(w_gate, "dp", axis=0, tiled=True),
        lax.all_gather(w_down, "dp", axis=0, tiled=True),
    )


def project(tokens, weight):
    return jnp.einsum("bsd,de->bse", tokens, weight, preferred_element_type=jnp.float32)


def project_back(tokens, weight):
    return jnp.einsum("bse,de->bsd", tokens, weight, preferred_element_type=jnp.float32)


def weight_grad(left_rows, right_rows):
    return jnp.einsum("bsd,bse->de", left_rows, right_rows, preferred_element_type=jnp.float32)


def per_device(
    block_in,
    out_grad,
    global_pos,
    w_query,
    w_key,
    w_value,
    w_out,
    w_up,
    w_gate,
    w_down,
    qk_gain,
    up_gain,
    gate_gain,
    att_rate,
    mlp_rate,
):
    micro_count = block_in.shape[0]
    tensor_count = lax.axis_size("tensor")
    local_rows = block_in.shape[2]
    seq_len = local_rows * tensor_count
    model_width = block_in.shape[3]
    head_width = w_query.shape[1]
    unit_width = w_up.shape[1]
    tensor_rank = lax.axis_index("tensor")
    places = jnp.arange(seq_len, dtype=jnp.int32)
    attn_zero = jnp.zeros((model_width, head_width), jnp.float32)
    mlp_zero = jnp.zeros((model_width, unit_width), jnp.float32)
    attn_sums = [attn_zero, attn_zero, attn_zero, attn_zero]
    mlp_sums = [mlp_zero, mlp_zero, mlp_zero]
    qk_total = jnp.zeros((head_width,), jnp.float32)
    up_total = jnp.zeros((unit_width,), jnp.float32)
    gate_total = jnp.zeros((unit_width,), jnp.float32)
    att_total = jnp.zeros((model_width,), jnp.float32)
    mlp_total = jnp.zeros((model_width,), jnp.float32)
    block_outs = []
    input_grads = []
    for micro_step in range(micro_count):
        tokens_in = block_in[micro_step]
        rows_in = tokens_in.astype(jnp.float32)
        global_flags = jnp.any(global_pos[micro_step][:, :, None] == places[None, None, :], axis=1)
        attn_weights = fetch_attn(w_query, w_key, w_value, w_out)
        query_full, key_full, value_full, out_full = attn_weights
        gathered_in = lax.all_gather(tokens_in, "tensor", axis=1, tiled=True)
        query_raw = project(gathered_in, query_full)
        key_raw = project(gathered_in, key_full)
        value_raw = project(gathered_in, value_full)
        (query_norm, key_norm), norm_pull = jax.vjp(both_heads, query_raw, key_raw, qk_gain)
        head_shape = (query_raw.shape[0], seq_len, head_width // HD, HD)
        queries = query_norm.astype(jnp.bfloat16).reshape(head_shape)
        key_rows = key_norm.astype(jnp.bfloat16).reshape(head_shape)
        value_rows = value_raw.astype(jnp.bfloat16).reshape(head_shape)
        mixed_heads, log_totals = jax.vmap(attend_forward)(
            queries, key_rows, value_rows, global_flags
        )
        mixed = mixed_heads.reshape(query_raw.shape).astype(jnp.bfloat16)
        partial_att = project_back(mixed, out_full)
        att_branch = lax.psum_scatter(
            partial_att.astype(jnp.bfloat16), "tensor", scatter_dimension=1, tiled=True
        ).astype(jnp.float32)
        hidden_one, att_pull = jax.vjp(settle, rows_in, att_branch, att_rate)
        gathered_mid = lax.all_gather(hidden_one.astype(jnp.bfloat16), "tensor", axis=1, tiled=True)
        mlp_weights = fetch_mlp(w_up, w_gate, w_down)
        up_full, gate_full, down_full = mlp_weights
        up_raw = project(gathered_mid, up_full)
        gate_raw = project(gathered_mid, gate_full)
        activated_wide, act_pull = jax.vjp(swish_gate, up_raw, gate_raw, up_gain, gate_gain)
        activated = activated_wide.astype(jnp.bfloat16)
        mlp_branch = lax.psum_scatter(
            project_back(activated, down_full).astype(jnp.bfloat16),
            "tensor",
            scatter_dimension=1,
            tiled=True,
        ).astype(jnp.float32)
        block_result, mlp_pull = jax.vjp(settle, hidden_one, mlp_branch, mlp_rate)
        block_outs.append(block_result)
        hidden_grad, branch_grad, mlp_rate_term = mlp_pull(out_grad[micro_step])
        mlp_total = mlp_total + mlp_rate_term
        up_full, gate_full, down_full = fetch_mlp(w_up, w_gate, w_down)
        branch_full = lax.all_gather(branch_grad.astype(jnp.bfloat16), "tensor", axis=1, tiled=True)
        mlp_sums[2] = mlp_sums[2] + weight_grad(branch_full, activated)
        act_grad = project(branch_full, down_full)
        up_grad, gate_grad, up_gain_term, gate_gain_term = act_pull(act_grad)
        up_total = up_total + up_gain_term
        gate_total = gate_total + gate_gain_term
        up_low = up_grad.astype(jnp.bfloat16)
        gate_low = gate_grad.astype(jnp.bfloat16)
        mlp_sums[0] = mlp_sums[0] + weight_grad(gathered_mid, up_low)
        mlp_sums[1] = mlp_sums[1] + weight_grad(gathered_mid, gate_low)
        mid_part = project_back(up_low, up_full) + project_back(gate_low, gate_full)
        hidden_total = hidden_grad + lax.psum_scatter(
            mid_part.astype(jnp.bfloat16), "tensor", scatter_dimension=1, tiled=True
        ).astype(jnp.float32)
        input_direct, att_grad, att_rate_term = att_pull(hidden_total)
        att_total = att_total + att_rate_term
        query_full, key_full, value_full, out_full = fetch_attn(w_query, w_key, w_value, w_out)
        att_full = lax.all_gather(att_grad.astype(jnp.bfloat16), "tensor", axis=1, tiled=True)
        attn_sums[3] = attn_sums[3] + weight_grad(att_full, mixed)
        mixed_grad = project(att_full, out_full).astype(jnp.bfloat16).reshape(head_shape)
        query_grad, key_grad, value_grad = jax.vmap(attend_backward)(
            queries, key_rows, value_rows, log_totals, mixed_grad, global_flags
        )
        qraw_grad, kraw_grad, qk_gain_term = norm_pull(
            (query_grad.reshape(query_raw.shape), key_grad.reshape(key_raw.shape))
        )
        qk_total = qk_total + qk_gain_term
        qraw_low = qraw_grad.astype(jnp.bfloat16)
        kraw_low = kraw_grad.astype(jnp.bfloat16)
        vraw_low = value_grad.reshape(value_raw.shape).astype(jnp.bfloat16)
        attn_sums[0] = attn_sums[0] + weight_grad(gathered_in, qraw_low)
        attn_sums[1] = attn_sums[1] + weight_grad(gathered_in, kraw_low)
        attn_sums[2] = attn_sums[2] + weight_grad(gathered_in, vraw_low)
        in_part = (
            project_back(qraw_low, query_full)
            + project_back(kraw_low, key_full)
            + project_back(vraw_low, value_full)
        )
        input_grads.append(
            input_direct
            + lax.psum_scatter(
                in_part.astype(jnp.bfloat16), "tensor", scatter_dimension=1, tiled=True
            ).astype(jnp.float32)
        )
    weight_sums = (
        lax.psum_scatter(attn_sums[0], "dp", scatter_dimension=0, tiled=True),
        lax.psum_scatter(attn_sums[1], "dp", scatter_dimension=0, tiled=True),
        lax.psum_scatter(attn_sums[2], "dp", scatter_dimension=0, tiled=True),
        lax.psum_scatter(attn_sums[3], "dp", scatter_dimension=0, tiled=True),
        lax.psum_scatter(mlp_sums[0], "dp", scatter_dimension=0, tiled=True),
        lax.psum_scatter(mlp_sums[1], "dp", scatter_dimension=0, tiled=True),
        lax.psum_scatter(mlp_sums[2], "dp", scatter_dimension=0, tiled=True),
    )
    qk_padded = lax.dynamic_update_slice_in_dim(
        jnp.zeros((head_width * tensor_count,), jnp.float32), qk_total, tensor_rank * head_width, 0
    )
    up_padded = lax.dynamic_update_slice_in_dim(
        jnp.zeros((unit_width * tensor_count,), jnp.float32), up_total, tensor_rank * unit_width, 0
    )
    gate_padded = lax.dynamic_update_slice_in_dim(
        jnp.zeros((unit_width * tensor_count,), jnp.float32),
        gate_total,
        tensor_rank * unit_width,
        0,
    )
    small_sums = lax.psum(
        (qk_padded, up_padded, gate_padded, att_total, mlp_total), ("dp", "tensor")
    )
    grad_qk_gain = lax.dynamic_slice_in_dim(small_sums[0], tensor_rank * head_width, head_width)
    grad_up_gain = lax.dynamic_slice_in_dim(small_sums[1], tensor_rank * unit_width, unit_width)
    grad_gate_gain = lax.dynamic_slice_in_dim(small_sums[2], tensor_rank * unit_width, unit_width)
    return (
        jnp.stack(block_outs),
        jnp.stack(input_grads),
        weight_sums[0],
        weight_sums[1],
        weight_sums[2],
        weight_sums[3],
        weight_sums[4],
        weight_sums[5],
        weight_sums[6],
        grad_qk_gain,
        grad_up_gain,
        grad_gate_gain,
        small_sums[3],
        small_sums[4],
    )


def solution(mesh):
    in_specs = (
        P(None, "dp", "tensor", None),
        P(None, "dp", "tensor", None),
        P(None, "dp", None),
        P("dp", "tensor"),
        P("dp", "tensor"),
        P("dp", "tensor"),
        P("dp", "tensor"),
        P("dp", "tensor"),
        P("dp", "tensor"),
        P("dp", "tensor"),
        P("tensor"),
        P("tensor"),
        P("tensor"),
        P(),
        P(),
    )
    out_specs = (
        P(None, "dp", "tensor", None),
        P(None, "dp", "tensor", None),
        P("dp", "tensor"),
        P("dp", "tensor"),
        P("dp", "tensor"),
        P("dp", "tensor"),
        P("dp", "tensor"),
        P("dp", "tensor"),
        P("dp", "tensor"),
        P("tensor"),
        P("tensor"),
        P("tensor"),
        P(),
        P(),
    )
    return jax.shard_map(
        per_device, mesh=mesh, in_specs=in_specs, out_specs=out_specs, check_vma=False
    )
```

profile of v0, /device:TPU:0, one launch (start us, length us, event | category | flops | bytes accessed | tf_op | source)
XLA Modules:
  0.0 1546.7 jit_solution(10572056599478299863)
XLA Ops:
  11.7 13.3 all_gather.32
  25.1 11.9 all_gather.33
  37.0 10.8 all_gather.31
  47.8 11.9 all_gather.34
  71.8 52.5 %all-gather.34.cloned.1.call-done = bf16[1,1,1024,1280]{3,2,1,0:T(8,128)(2,1)} async-done(((bf16[1,1,256,1280]{3,2,1,0:T(8,128)(2,1)}), bf16[1,1,1024,1280]{3,2,1,0:T(8,128)(2,1)}) %all-gather.34.cloned.1.call-update) | async-done | bytes 2621456 | tf_op jit(solution)/shard_map/all_gather | solution.py:183
  143.1 12.6 fusion.3
  210.3 18.0 %reduce-scatter.26.cloned.1.call-done = bf16[1,256,1280]{2,1,0:T(8,128)(2,1)} async-done(((bf16[1,1024,1280]{2,1,0:T(8,128)(2,1)}), bf16[1,256,1280]{2,1,0:T(8,128)(2,1)}) %reduce-scatter.26.cloned.1.call-update) | async-done | bytes 655376 | tf_op jit(solution)/shard_map/reduce_scatter | solution.py:197
  229.7 53.2 %reduce-scatter.22.cloned.1.call-done = bf16[1,256,1280]{2,1,0:T(8,128)(2,1)} async-done(((bf16[1,1024,1280]{2,1,0:T(8,128)(2,1)}), bf16[1,256,1280]{2,1,0:T(8,128)(2,1)}) %reduce-scatter.22.cloned.1.call-update) | async-done | bytes 655376 | tf_op jit(solution)/shard_map/reduce_scatter | solution.py:197
  291.4 51.8 %all-gather.14.cloned.1.call-done = bf16[1,1024,1280]{2,1,0:T(8,128)(2,1)} async-done(((bf16[1,256,1280]{2,1,0:T(8,128)(2,1)}), bf16[1,1024,1280]{2,1,0:T(8,128)(2,1)}) %all-gather.14.cloned.1.call-update) | async-done | bytes 2621456 | tf_op jit(solution)/shard_map/all_gather | solution.py:201
  343.3 8.7 fusion.70
  351.9 24.6 %all-gather.16.cloned.1.call-done = bf16[1280,1280]{1,0:T(8,128)(2,1)} async-done(((bf16[160,1280]{1,0:T(8,128)(2,1)}), bf16[1280,1280]{1,0:T(8,128)(2,1)}) %all-gather.16.cloned.1.call-update) | async-done | bytes 3276816 | tf_op jit(solution)/shard_map/all_gather | solution.py:122
  385.2 48.2 %all-gather.22.cloned.1.call-done = bf16[1,1024,1280]{2,1,0:T(8,128)(2,1)} async-done(((bf16[1,256,1280]{2,1,0:T(8,128)(2,1)}), bf16[1,1024,1280]{2,1,0:T(8,128)(2,1)}) %all-gather.22.cloned.1.call-update) | async-done | bytes 2621456 | tf_op jit(solution)/shard_map/all_gather | solution.py:201
  442.1 9.8 multiply_convert_fusion.8
  451.9 14.9 all-gather.20.cloned.1.call-done
  482.5 44.3 %reduce-scatter.28.cloned.1.call-done = bf16[1,256,1280]{2,1,0:T(8,128)(2,1)} async-done(((bf16[1,1024,1280]{2,1,0:T(8,128)(2,1)}), bf16[1,256,1280]{2,1,0:T(8,128)(2,1)}) %reduce-scatter.28.cloned.1.call-update) | async-done | bytes 655376 | tf_op jit(solution)/shard_map/reduce_scatter | solution.py:208
  528.2 52.7 %reduce-scatter.24.cloned.1.call-done = bf16[1,256,1280]{2,1,0:T(8,128)(2,1)} async-done(((bf16[1,1024,1280]{2,1,0:T(8,128)(2,1)}), bf16[1,256,1280]{2,1,0:T(8,128)(2,1)}) %reduce-scatter.24.cloned.1.call-update) | async-done | bytes 655376 | tf_op jit(solution)/shard_map/reduce_scatter | solution.py:208
  590.5 54.4 %all-gather.24.cloned.1.call-done = bf16[1,1024,1280]{2,1,0:T(8,128)(2,1)} async-done(((bf16[1,256,1280]{2,1,0:T(8,128)(2,1)}), bf16[1,1024,1280]{2,1,0:T(8,128)(2,1)}) %all-gather.24.cloned.1.call-update) | async-done | bytes 2621456 | tf_op jit(solution)/shard_map/all_gather | solution.py:219
  644.9 12.1 multiply_reduce_fusion.5
  666.3 51.0 %reduce-scatter.30.cloned.1.call-done = bf16[1,256,1280]{2,1,0:T(8,128)(2,1)} async-done(((bf16[1,1024,1280]{2,1,0:T(8,128)(2,1)}), bf16[1,256,1280]{2,1,0:T(8,128)(2,1)}) %reduce-scatter.30.cloned.1.call-update) | async-done | bytes 655376 | tf_op jit(solution)/shard_map/reduce_scatter | solution.py:230
  724.3 54.4 %all-gather.28.cloned.1.call-done = bf16[1,1024,1280]{2,1,0:T(8,128)(2,1)} async-done(((bf16[1,256,1280]{2,1,0:T(8,128)(2,1)}), bf16[1,1024,1280]{2,1,0:T(8,128)(2,1)}) %all-gather.28.cloned.1.call-update) | async-done | bytes 2621456 | tf_op jit(solution)/shard_map/all_gather | solution.py:219
  778.6 12.3 multiply_reduce_fusion.4
  800.9 50.3 %reduce-scatter.34.cloned.1.call-done = bf16[1,256,1280]{2,1,0:T(8,128)(2,1)} async-done(((bf16[1,1024,1280]{2,1,0:T(8,128)(2,1)}), bf16[1,256,1280]{2,1,0:T(8,128)(2,1)}) %reduce-scatter.34.cloned.1.call-update) | async-done | bytes 655376 | tf_op jit(solution)/shard_map/reduce_scatter | solution.py:230
  862.5 50.9 %all-gather.26.cloned.1.call-done = bf16[1,1024,1280]{2,1,0:T(8,128)(2,1)} async-done(((bf16[1,256,1280]{2,1,0:T(8,128)(2,1)}), bf16[1,1024,1280]{2,1,0:T(8,128)(2,1)}) %all-gather.26.cloned.1.call-update) | async-done | bytes 2621456 | tf_op jit(solution)/shard_map/all_gather | solution.py:236
  932.3 36.2 %all-gather.30.cloned.1.call-done = bf16[1,1024,1280]{2,1,0:T(8,128)(2,1)} async-done(((bf16[1,256,1280]{2,1,0:T(8,128)(2,1)}), bf16[1,1024,1280]{2,1,0:T(8,128)(2,1)}) %all-gather.30.cloned.1.call-update) | async-done | bytes 2621456 | tf_op jit(solution)/shard_map/all_gather | solution.py:236
  1157.1 40.7 %all-reduce = (f32[1280]{0:T(1024)S(1)}, f32[5120]{0:T(1024)S(1)}, f32[5120]{0:T(1024)S(1)}, f32[1280]{0:T(1024)}, f32[1280]{0:T(1024)}) all-reduce(f32[1280]{0:T(1024)S(1)} %add_dynamic-update-slice_fusion.2, f32[5120]{0:T(1024)S(1)} %add_dynamic-update-slice_fusion.1, ...), channel_id=1, replica_groups=mesh['dp'=8,'tensor'=4] {'dp','tensor'}, use_global_device_ids=true, to_apply=%region_57.58 | all-reduce | flops 14080 | bytes 112640 | tf_op jit(solution)/shard_map/psum | solution.py:284
  1203.2 24.3 %reduce-scatter.44.cloned.1.call-done = f32[160,1280]{1,0:T(8,128)} async-done(((f32[1280,1280]{1,0:T(8,128)}), f32[160,1280]{1,0:T(8,128)}) %reduce-scatter.44.cloned.1.call-update) | async-done | bytes 819216 | tf_op jit(solution)/shard_map/reduce_scatter | solution.py:270
  1227.5 67.3 %reduce-scatter.42.cloned.1.call-done = f32[160,1280]{1,0:T(8,128)} async-done(((f32[1280,1280]{1,0:T(8,128)}), f32[160,1280]{1,0:T(8,128)}) %reduce-scatter.42.cloned.1.call-update) | async-done | bytes 819216 | tf_op jit(solution)/shard_map/reduce_scatter | solution.py:269
  1294.8 66.7 %reduce-scatter.40.cloned.1.call-done = f32[160,1280]{1,0:T(8,128)} async-done(((f32[1280,1280]{1,0:T(8,128)}), f32[160,1280]{1,0:T(8,128)}) %reduce-scatter.40.cloned.1.call-update) | async-done | bytes 819216 | tf_op jit(solution)/shard_map/reduce_scatter | solution.py:268
  1361.5 44.6 %reduce-scatter.38.cloned.1.call-done = f32[160,320]{1,0:T(8,128)} async-done(((f32[1280,320]{1,0:T(8,128)}), f32[160,320]{1,0:T(8,128)}) %reduce-scatter.38.cloned.1.call-update) | async-done | bytes 204816 | tf_op jit(solution)/shard_map/reduce_scatter | solution.py:267
  1406.1 44.2 %reduce-scatter.50.cloned.1.call-done = f32[160,320]{1,0:T(8,128)} async-done(((f32[1280,320]{1,0:T(8,128)}), f32[160,320]{1,0:T(8,128)}) %reduce-scatter.50.cloned.1.call-update) | async-done | bytes 204816
  1450.4 44.6 %reduce-scatter.48.cloned.1.call-done = f32[160,320]{1,0:T(8,128)} async-done(((f32[1280,320]{1,0:T(8,128)}), f32[160,320]{1,0:T(8,128)}) %reduce-scatter.48.cloned.1.call-update) | async-done | bytes 204816
  1494.9 44.2 %reduce-scatter.46.cloned.1.call-done = f32[160,320]{1,0:T(8,128)} async-done(((f32[1280,320]{1,0:T(8,128)}), f32[160,320]{1,0:T(8,128)}) %reduce-scatter.46.cloned.1.call-update) | async-done | bytes 204816
  (616 shorter events, 390.8 us)
Async XLA Ops:
  8.1 60.5 %all-gather.32.cloned.1.call-start = ((), (), s32[]{:S(2)}) async-start(), calls=%async_computation.36 | async-start | bytes 3276800 | tf_op jit(solution)/shard_map/all_gather | solution.py:183
  10.7 113.7 %all-gather.34.cloned.1.call-start = ((), (), s32[]{:S(2)}) async-start(), calls=%async_computation.37 | async-start | bytes 3276800 | tf_op jit(solution)/shard_map/all_gather | solution.py:183
  11.4 216.9 %reduce-scatter.26.cloned.1.call-start = ((), (), s32[]{:S(2)}) async-start(), calls=%async_computation.21 | async-start | bytes 3276800 | tf_op jit(solution)/shard_map/reduce_scatter | solution.py:197
  47.8 137.5 %copy-start.30 = (bf16[1280,320]{1,0:T(8,128)(2,1)}, bf16[1280,320]{1,0:T(8,128)(2,1)S(1)}, u32[]{:S(2)}) copy-start(bf16[1280,320]{1,0:T(8,128)(2,1)S(1)} %all_gather.31) | copy-start | bytes 2457604
  62.9 137.0 %copy-start.40 = (pred[512,1024]{1,0:T(8,128)(4,1)}, pred[512,1024]{1,0:T(8,128)(4,1)S(1)}, u32[]{:S(2)}) copy-start(pred[512,1024]{1,0:T(8,128)(4,1)S(1)} %get-tuple-element.134) | copy-start | bytes 1572868
  177.3 105.6 %reduce-scatter.22.cloned.1.call-start = ((), (), s32[]{:S(2)}) async-start(), calls=%async_computation.15 | async-start | bytes 3276800 | tf_op jit(solution)/shard_map/reduce_scatter | solution.py:197
  209.7 75.1 %copy-start.73 = (f32[1280]{0:T(1024)S(1)}, f32[1280]{0:T(1024)}, u32[]{:S(2)}) copy-start(f32[1280]{0:T(1024)} %param.28) | copy-start | bytes 15364
  209.7 81.7 %all-gather.18.cloned.1.call-start = ((), (), s32[]{:S(2)}) async-start(), calls=%async_computation.18 | async-start | bytes 3686400 | tf_op jit(solution)/shard_map/all_gather | solution.py:123
  210.3 133.0 %all-gather.14.cloned.1.call-start = ((), (), s32[]{:S(2)}) async-start(), calls=%async_computation.16 | async-start | bytes 3276800 | tf_op jit(solution)/shard_map/all_gather | solution.py:201
  288.9 87.7 %all-gather.16.cloned.1.call-start = ((), (), s32[]{:S(2)}) async-start(), calls=%async_computation.17 | async-start | bytes 3686400 | tf_op jit(solution)/shard_map/all_gather | solution.py:122
  289.4 143.9 %all-gather.22.cloned.1.call-start = ((), (), s32[]{:S(2)}) async-start(), calls=%async_computation.22 | async-start | bytes 3276800 | tf_op jit(solution)/shard_map/all_gather | solution.py:201
  290.2 176.6 %all-gather.20.cloned.1.call-start = ((), (), s32[]{:S(2)}) async-start(), calls=%async_computation.19 | async-start | bytes 3686400 | tf_op jit(solution)/shard_map/all_gather | solution.py:124
  290.9 235.9 %reduce-scatter.28.cloned.1.call-start = ((), (), s32[]{:S(2)}) async-start(), calls=%async_computation.23 | async-start | bytes 3276800 | tf_op jit(solution)/shard_map/reduce_scatter | solution.py:208
  474.6 106.3 %reduce-scatter.24.cloned.1.call-start = ((), (), s32[]{:S(2)}) async-start(), calls=%async_computation.20 | async-start | bytes 3276800 | tf_op jit(solution)/shard_map/reduce_scatter | solution.py:208
  482.4 99.7 %copy-start.75 = (f32[1280]{0:T(1024)S(1)}, f32[1280]{0:T(1024)}, u32[]{:S(2)}) copy-start(f32[1280]{0:T(1024)} %param.29) | copy-start | bytes 15364
  482.5 162.4 %all-gather.24.cloned.1.call-start = ((), (), s32[]{:S(2)}) async-start(), calls=%async_computation.24 | async-start | bytes 3276800 | tf_op jit(solution)/shard_map/all_gather | solution.py:219
  590.4 126.9 %reduce-scatter.30.cloned.1.call-start = ((), (), s32[]{:S(2)}) async-start(), calls=%async_computation.25 | async-start | bytes 3276800 | tf_op jit(solution)/shard_map/reduce_scatter | solution.py:230
  666.3 112.4 %all-gather.28.cloned.1.call-start = ((), (), s32[]{:S(2)}) async-start(), calls=%async_computation.28 | async-start | bytes 3276800 | tf_op jit(solution)/shard_map/all_gather | solution.py:219
  724.2 127.0 %reduce-scatter.34.cloned.1.call-start = ((), (), s32[]{:S(2)}) async-start(), calls=%async_computation.29 | async-start | bytes 3276800 | tf_op jit(solution)/shard_map/reduce_scatter | solution.py:230
  800.2 113.1 %all-gather.26.cloned.1.call-start = ((), (), s32[]{:S(2)}) async-start(), calls=%async_computation.26 | async-start | bytes 3276800 | tf_op jit(solution)/shard_map/all_gather | solution.py:236
  858.8 109.7 %all-gather.30.cloned.1.call-start = ((), (), s32[]{:S(2)}) async-start(), calls=%async_computation.30 | async-start | bytes 3276800 | tf_op jit(solution)/shard_map/all_gather | solution.py:236
  859.0 119.6 %copy-start.124 = (f32[5,512]{1,0:T(8,128)}, f32[5,512]{1,0:T(8,128)S(1)}, u32[]{:S(2)}) copy-start(f32[5,512]{1,0:T(8,128)S(1)} %log_add_fusion) | copy-start | bytes 30724
  861.7 338.1 %reduce-scatter.36.cloned.1.call-start = ((), (), s32[]{:S(2)}) async-start(), calls=%async_computation.31 | async-start | bytes 3276800 | tf_op jit(solution)/shard_map/reduce_scatter | solution.py:259
  861.8 130.9 %copy-start.126 = (f32[5,512]{1,0:T(8,128)}, f32[5,512]{1,0:T(8,128)S(1)}, u32[]{:S(2)}) copy-start(f32[5,512]{1,0:T(8,128)S(1)} %log_add_fusion.1) | copy-start | bytes 30724
  1055.5 144.3 %reduce-scatter.32.cloned.1.call-start = ((), (), s32[]{:S(2)}) async-start(), calls=%async_computation.27 | async-start | bytes 3276800 | tf_op jit(solution)/shard_map/reduce_scatter | solution.py:259
  1075.9 151.6 %reduce-scatter.44.cloned.1.call-start = ((), (), s32[]{:S(2)}) async-start(), calls=%async_computation.35 | async-start | bytes 7372800 | tf_op jit(solution)/shard_map/reduce_scatter | solution.py:270
  1088.3 206.5 %reduce-scatter.42.cloned.1.call-start = ((), (), s32[]{:S(2)}) async-start(), calls=%async_computation.34 | async-start | bytes 7372800 | tf_op jit(solution)/shard_map/reduce_scatter | solution.py:269
  1104.6 257.0 %reduce-scatter.40.cloned.1.call-start = ((), (), s32[]{:S(2)}) async-start(), calls=%async_computation.33 | async-start | bytes 7372800 | tf_op jit(solution)/shard_map/reduce_scatter | solution.py:268
  1117.2 288.9 %reduce-scatter.38.cloned.1.call-start = ((), (), s32[]{:S(2)}) async-start(), calls=%async_computation.32 | async-start | bytes 2211840 | tf_op jit(solution)/shard_map/reduce_scatter | solution.py:267
  1124.7 325.6 %reduce-scatter.50.cloned.1.call-start = ((), (), s32[]{:S(2)}) async-start(), calls=%async_computation.40 | async-start | bytes 2211840
  1132.9 362.0 %reduce-scatter.48.cloned.1.call-start = ((), (), s32[]{:S(2)}) async-start(), calls=%async_computation.39 | async-start | bytes 2211840
  1141.3 397.8 %reduce-scatter.46.cloned.1.call-start = ((), (), s32[]{:S(2)}) async-start(), calls=%async_computation.38 | async-start | bytes 2211840
  (195 other events, 1978.6 us)
Sparse Core Ops, SparseCore 0:
  11.0 57.4 all-gather.31
  70.7 53.5 all-gather.33
  177.4 50.8 reduce-scatter.25
  231.0 51.7 reduce-scatter.21
  474.7 52.1 reduce-scatter.27
  529.0 51.7 reduce-scatter.23
  666.4 50.8 reduce-scatter.29
  858.9 54.3 all-gather.25
  914.9 53.5 all-gather.29
Sparse Core Ops, SparseCore 1:
  212.1 31.6 all-gather.17
  288.9 54.3 all-gather.13
  345.0 31.4 all-gather.15
  378.7 54.6 all-gather.21
  435.3 31.4 all-gather.19
  590.5 54.3 all-gather.23
  724.3 54.3 all-gather.27
  800.3 50.9 reduce-scatter.33
  1055.5 50.9 reduce-scatter.35
  1108.8 51.7 reduce-scatter.31
  1164.4 63.0 reduce-scatter.43
  1231.9 62.8 reduce-scatter.41
  1298.7 62.8 reduce-scatter.39
  1365.9 40.2 reduce-scatter.37
  1410.1 40.2 reduce-scatter.49
  1454.7 40.1 reduce-scatter.47
  1498.9 40.2 reduce-scatter.45
where the time goes:
time: 1550 us
  waiting for transfers between devices  1000 us (65%)
  matrix products  294 us (19%)
  other arithmetic  107 us (7%)
  blocking collectives  88.7 us (6%)
  local copies, waits for them, and re-layouts  34.1 us (2%)
  between operations  18.5 us (1%)
    unnamed x29, waiting for transfers between devices  136 us
    all_gather x2, waiting for transfers between devices, per_device(): lax.all_gather(branch_grad.astype(jnp.bfloat16), 'tensor', axis=1, tiled=...  109 us
    reduce_scatter x2, waiting for transfers between devices, per_device(): lax.psum_scatter(mid_part.astype(jnp.bfloat16), 'tensor', scatter_dimensi...  101 us
    all_gather x2, waiting for transfers between devices, per_device(): lax.all_gather(hidden_one.astype(jnp.bfloat16), 'tensor', axis=1, tiled=T...  100 us
    reduce_scatter x2, waiting for transfers between devices, per_device(): lax.psum_scatter(project_back(activated, down_full).astype(jnp.bfloat16),...  97 us
    all_gather x2, waiting for transfers between devices, per_device(): lax.all_gather(att_grad.astype(jnp.bfloat16), 'tensor', axis=1, tiled=True)  87.1 us
    dot_general x14, matrix products, project(): jnp.einsum('bsd,de->bse', tokens, weight, preferred_element_type=jnp.floa...  74.2 us
    reduce_scatter x2, waiting for transfers between devices, per_device(): lax.psum_scatter(partial_att.astype(jnp.bfloat16), 'tensor', scatter_dime...  71.1 us
  transfers between devices with their start and end apart: 26, of which 23 were waited for; matrix products, arithmetic and copies ran while one was open for 13% of the time, Pallas kernels for 0%

commit v1 on v0

v1 whole, which is shorter than its diff:
```python
import math

import jax
import jax.numpy as jnp
from jax import lax
from jax.experimental import pallas as pl
from jax.experimental.pallas import tpu as pltpu
from jax.sharding import Mesh, PartitionSpec as P

HD = 64
WINDOW = 512
CHIPS = 4
LANES = 128
HALF = 64
EXTRA = 32
BLOCK = 256
VMEM_LIMIT = 48 * 2**20

DP = ("outer", "chip", "core")
ALL = DP + ("tensor",)

epsilon = 1e-06
blocked = -1e30
low = jnp.bfloat16
wide = jnp.float32


def swap(value, bit):
    count = lax.axis_size(DP)
    return lax.ppermute(value, DP, [(i, i ^ bit) for i in range(count)])


def pick(flag, when_true, when_false):
    return jnp.where(flag, when_true, when_false)


def outer_gather(value):
    me = lax.axis_index(DP)
    bit = 8
    while bit < lax.axis_size(DP):
        other = swap(value, bit)
        upper = (me & bit) != 0
        value = pick(
            upper, jnp.concatenate([other, value]), jnp.concatenate([value, other])
        )
        bit *= 2
    return value


def outer_scatter(value):
    me = lax.axis_index(DP)
    bit = lax.axis_size(DP) // 2
    while bit >= 8:
        rows = value.shape[0] // 2
        upper = (me & bit) != 0
        keep = pick(upper, value[rows:], value[:rows])
        send = pick(upper, value[:rows], value[rows:])
        value = (keep.astype(wide) + swap(send, bit).astype(wide)).astype(value.dtype)
        bit //= 2
    return value


def full_rows(value):
    outer = lax.axis_size(DP) // 8
    count, rows, columns = value.shape
    if outer > 1:
        value = value.reshape(count, outer, rows // outer, columns).transpose(1, 0, 2, 3)
    return value.reshape(count * rows, columns)


def plane_rows(value):
    outer = lax.axis_size(DP) // 8
    total, columns = value.shape
    if outer > 1:
        value = value.reshape(outer, 8, total // 8 // outer, columns).transpose(1, 0, 2, 3)
    return value.reshape(8, total // 8, columns)


def plane_first(value):
    return value, swap(value, 2), swap(value, 4)


def plane_second(first):
    value, along_x, along_y = first
    half = value.shape[0] // 2
    return value, along_x, along_y, swap(along_y[:half], 2), swap(along_x[half:], 4)


def scatter_first(blocks):
    own, along_x, along_y, diagonal = blocks
    half = own.shape[0] // 2
    first = swap(jnp.concatenate([along_x[:half], diagonal[:half]]), 2)
    second = swap(jnp.concatenate([along_y[half:], diagonal[half:]]), 4)
    return blocks, first, second


def scatter_second(sent):
    (own, along_x, along_y, _), first, second = sent
    half = own.shape[0] // 2
    next_y = (along_y[:half].astype(wide) + first[half:].astype(wide)).astype(low)
    next_x = (along_x[half:].astype(wide) + second[half:].astype(wide)).astype(low)
    top = own[:half].astype(wide) + first[:half].astype(wide) + swap(next_y, 4).astype(wide)
    bottom = own[half:].astype(wide) + second[:half].astype(wide) + swap(next_x, 2).astype(wide)
    return jnp.concatenate([top, bottom])


def row_norm(values):
    return values * lax.rsqrt(jnp.mean(values * values, axis=-1, keepdims=True) + epsilon)


def settle(base, branch, rate):
    return row_norm(base + rate * (row_norm(branch) - base))


def nt(left, right):
    return lax.dot_general(left, right, (((1,), (1,)), ((), ())), preferred_element_type=wide)


def nn(left, right):
    return lax.dot_general(left, right, (((1,), (0,)), ((), ())), preferred_element_type=wide)


def tn(left, right):
    return lax.dot_general(left, right, (((0,), (0,)), ((), ())), preferred_element_type=wide)


def params():
    return pltpu.CompilerParams(vmem_limit_bytes=VMEM_LIMIT)


def cost(flops, moved):
    return pl.CostEstimate(flops=int(flops), bytes_accessed=int(moved), transcendentals=0)


def head_means(width):
    rows = lax.broadcasted_iota(jnp.int32, (width, width), 0) // HD
    columns = lax.broadcasted_iota(jnp.int32, (width, width), 1) // HD
    return jnp.where(rows == columns, 1.0 / HD, 0.0).astype(low)


def head_scale(raw, means):
    return lax.rsqrt(nn((raw * raw).astype(low), means) + epsilon)


def project_heads(rows, weight, gain):
    n, depth = rows.shape
    width = weight.shape[1]
    tile = 2 * LANES
    block = 256

    def kernel(rows_ref, weight_ref, gain_ref, out_ref, raw_ref):
        means = head_means(tile)
        for start in range(0, n, block):
            span = slice(start, start + block)
            raw = nn(rows_ref[span, :], weight_ref[...])
            raw_ref[span, :] = raw.astype(low)
            out_ref[span, :] = (raw * head_scale(raw, means) * gain_ref[...]).astype(low)

    out = pl.BlockSpec((n, tile), lambda j: (0, j))
    return pl.pallas_call(
        kernel,
        grid=(width // tile,),
        in_specs=[
            pl.BlockSpec((n, depth), lambda j: (0, 0)),
            pl.BlockSpec((depth, tile), lambda j: (0, j)),
            pl.BlockSpec((1, tile), lambda j: (0, j)),
        ],
        out_specs=[out, out],
        out_shape=[jax.ShapeDtypeStruct((n, width), low)] * 2,
        compiler_params=params(),
        cost_estimate=cost(2 * n * depth * width, 2 * (n * depth + depth * width + 2 * n * width)),
    )(rows, weight, gain[None])


def fill_bias(bias, flag_row, flag_col):
    @pl.when(pl.program_id(0) == 0)
    def _():
        for i in range(bias.shape[0] // BLOCK):
            for j in range(i + 1):
                keys = slice(j * BLOCK, (j + 1) * BLOCK)
                rows = slice(i * BLOCK, (i + 1) * BLOCK)
                key_ids = j * BLOCK + lax.broadcasted_iota(jnp.int32, (BLOCK, BLOCK), 0)
                row_ids = i * BLOCK + lax.broadcasted_iota(jnp.int32, (BLOCK, BLOCK), 1)
                flagged = jnp.maximum(flag_row[:, rows], flag_col[keys, :]) > 0.5
                allow = (key_ids <= row_ids) & ((row_ids - key_ids < WINDOW) | flagged)
                bias[keys, rows] = jnp.where(allow, 0.0, blocked)


def head_lanes(value, head):
    lane = lax.broadcasted_iota(jnp.int32, value.shape, 1)
    mine = (lane < HD) if head == 0 else (lane >= HD)
    return jnp.where(mine, value, jnp.zeros_like(value))


def flag_specs(seq_len):
    return [pl.BlockSpec((1, seq_len), lambda h: (0, 0)), pl.BlockSpec((seq_len, 1), lambda h: (0, 0))]


def attend_forward(heads, value_rows, flag_row, flag_col):
    seq_len, width = value_rows.shape
    pairs = width // LANES

    def kernel(q_ref, k_ref, v_ref, row_ref, col_ref, out_ref, lse_ref, bias, turned):
        fill_bias(bias, row_ref, col_ref)
        turned[...] = v_ref[...].astype(wide).T.astype(low)
        for i in range(seq_len // BLOCK):
            rows = slice(i * BLOCK, (i + 1) * BLOCK)
            reach = (i + 1) * BLOCK
            block = q_ref[rows, :] * jnp.asarray(1.0 / math.sqrt(HD), low)
            halves = []
            for head in range(2):
                scores = nt(k_ref[:reach, :], head_lanes(block, head)) + bias[:reach, rows]
                raised = jnp.exp(scores)
                total = jnp.sum(raised, axis=0, keepdims=True)
                mixed = nn(turned[head * HD : (head + 1) * HD, :reach], raised.astype(low))
                halves.append(mixed / total)
                lse_ref[0, head : head + 1, rows] = jnp.log(total)
            out_ref[rows, :] = jnp.concatenate(halves, axis=0).T.astype(low)

    block = pl.BlockSpec((seq_len, LANES), lambda h: (0, h))
    keys = pl.BlockSpec((seq_len, LANES), lambda h: (0, pairs + h))
    return pl.pallas_call(
        kernel,
        grid=(pairs,),
        in_specs=[block, keys, block] + flag_specs(seq_len),
        out_specs=[block, pl.BlockSpec((1, 8, seq_len), lambda h: (h, 0, 0))],
        out_shape=[
            jax.ShapeDtypeStruct((seq_len, width), low),
            jax.ShapeDtypeStruct((pairs, 8, seq_len), wide),
        ],
        scratch_shapes=[pltpu.VMEM((seq_len, seq_len), wide), pltpu.VMEM((LANES, seq_len), low)],
        compiler_params=params(),
        cost_estimate=cost(16 * seq_len * seq_len * width, 10 * seq_len * width),
    )(heads, heads, value_rows, flag_row, flag_col)


def attend_backward(heads, raw, value_rows, mixed, mixed_grad, lse, gain, flag_row, flag_col):
    seq_len, width = value_rows.shape
    pairs = width // LANES
    scale = 1.0 / math.sqrt(HD)

    def unnorm(grad, raw_block, gain_row, means):
        raw_block = raw_block.astype(wide)
        factor = head_scale(raw_block, means)
        normed = raw_block * factor
        term = jnp.sum(grad * normed, axis=0, keepdims=True)
        grad = grad * gain_row
        inner = nn((grad * normed).astype(low), means)
        return (factor * (grad - normed * inner)).astype(low), term

    def kernel(
        q_ref, k_ref, v_ref, qraw_ref, kraw_ref, m_ref, g_ref, lse_ref, gain_ref, row_ref, col_ref,
        heads_ref, dv_ref, term_ref, bias, turned, key_total, value_total, dq_ref, dk_ref, sems,
    ):
        step = pl.program_id(0)

        def stores(pair):
            return [
                pltpu.make_async_copy(
                    ref, heads_ref.at[:, pl.ds(pl.multiple_of((side * pairs + pair) * LANES, LANES), LANES)], sems.at[side]
                )
                for side, ref in enumerate((dq_ref, dk_ref))
            ]

        @pl.when(step > 0)
        def _():
            for store in stores(step - 1):
                store.wait()

        fill_bias(bias, row_ref, col_ref)
        turned[...] = k_ref[...].astype(wide).T.astype(low)
        means = head_means(LANES)
        gain_row = gain_ref[...]
        query_term = key_term = jnp.zeros((1, LANES), wide)
        count = seq_len // BLOCK
        for i in reversed(range(count)):
            rows = slice(i * BLOCK, (i + 1) * BLOCK)
            reach = (i + 1) * BLOCK
            block = q_ref[rows, :] * jnp.asarray(scale, low)
            grads = g_ref[rows, :]
            products = (grads.astype(wide) * m_ref[rows, :].astype(wide)).T
            halves = []
            key_parts = value_parts = None
            for head in range(2):
                inner = jnp.sum(products[head * HD : (head + 1) * HD], axis=0, keepdims=True)
                query = head_lanes(block, head)
                grad = head_lanes(grads, head)
                scores = nt(k_ref[:reach, :], query) + bias[:reach, rows]
                probs = jnp.exp(scores - lse_ref[0, head : head + 1, rows])
                prob_grad = nt(v_ref[:reach, :], grad)
                score_grad = (probs * (prob_grad - inner)).astype(low)
                halves.append(nn(turned[head * HD : (head + 1) * HD, :reach], score_grad))
                key_part = nn(score_grad, query)
                value_part = nn(probs.astype(low), grad)
                key_parts = key_part if key_parts is None else key_parts + key_part
                value_parts = value_part if value_parts is None else value_parts + value_part
            if i == count - 1:
                key_total[...] = key_parts
                value_total[...] = value_parts
            else:
                key_total[:reach, :] += key_parts
                value_total[:reach, :] += value_parts
            query_grad = jnp.concatenate(halves, axis=0).T * scale
            dq_ref[rows, :], term = unnorm(query_grad, qraw_ref[rows, :], gain_row, means)
            query_term = query_term + term
        dv_ref[...] = value_total[...].astype(low)
        for i in range(count):
            rows = slice(i * BLOCK, (i + 1) * BLOCK)
            dk_ref[rows, :], term = unnorm(key_total[rows, :], kraw_ref[rows, :], gain_row, means)
            key_term = key_term + term
        term_ref[...] = jnp.concatenate([query_term, key_term, jnp.zeros((6, LANES), wide)], axis=0)
        for store in stores(step):
            store.start()

        @pl.when(step == pairs - 1)
        def _():
            for store in stores(step):
                store.wait()

    block = pl.BlockSpec((seq_len, LANES), lambda h: (0, h))
    keys = pl.BlockSpec((seq_len, LANES), lambda h: (0, pairs + h))
    return pl.pallas_call(
        kernel,
        grid=(pairs,),
        in_specs=[block, keys, block, block, keys, block, block]
        + [pl.BlockSpec((1, 8, seq_len), lambda h: (h, 0, 0)), pl.BlockSpec((1, LANES), lambda h: (0, h))]
        + flag_specs(seq_len),
        out_specs=[pl.BlockSpec(memory_space=pl.ANY), block, pl.BlockSpec((8, LANES), lambda h: (0, h))],
        out_shape=[
            jax.ShapeDtypeStruct((seq_len, 2 * width), low),
            jax.ShapeDtypeStruct((seq_len, width), low),
            jax.ShapeDtypeStruct((8, width), wide),
        ],
        scratch_shapes=[
            pltpu.VMEM((seq_len, seq_len), wide),
            pltpu.VMEM((LANES, seq_len), low),
            pltpu.VMEM((seq_len, LANES), wide),
            pltpu.VMEM((seq_len, LANES), wide),
            pltpu.VMEM((seq_len, LANES), low),
            pltpu.VMEM((seq_len, LANES), low),
            pltpu.SemaphoreType.DMA((2,)),
        ],
        compiler_params=params(),
        cost_estimate=cost(32 * seq_len * seq_len * width, 20 * seq_len * width),
    )(heads, heads, value_rows, raw, raw, mixed, mixed_grad, lse, gain[None], flag_row, flag_col)


def sum_back(lefts, rights, n=None, first=0):
    n = n or lefts[0][0].shape[0]
    out_width = rights[0][0].shape[0]
    block = 256
    count = len(lefts)
    skip = first * n // block

    def kernel(*refs):
        total = nt(refs[0][...], refs[count][...])
        for i in range(1, count):
            total = total + nt(refs[i][...], refs[count + i][...])
        refs[2 * count][...] = total.astype(low)

    depth = sum(columns for _, _, columns in lefts)
    return pl.pallas_call(
        kernel,
        grid=(n // block,),
        in_specs=[
            pl.BlockSpec((block, columns), lambda r, at=at: (r + skip, at)) for _, at, columns in lefts
        ]
        + [pl.BlockSpec((out_width, columns), lambda r, at=at: (0, at)) for _, at, columns in rights],
        out_specs=pl.BlockSpec((block, out_width), lambda r: (r, 0)),
        out_shape=jax.ShapeDtypeStruct((n, out_width), low),
        compiler_params=params(),
        cost_estimate=cost(2 * n * out_width * depth, 2 * (n + out_width) * depth + 2 * n * out_width),
    )(*(matrix for matrix, _, _ in lefts + rights))


def rows_product(pairs):
    n, depth = pairs[0][0].shape
    width = pairs[0][1].shape[1]
    tile = 2 * LANES
    steps = depth // tile
    count = len(pairs)

    def kernel(*refs):
        for k in range(count):

            @pl.when(pl.program_id(0) // steps == k)
            def _():
                refs[2 * count][...] = tn(refs[2 * k][...], refs[2 * k + 1][...]).astype(low)

    def left_tile(k):
        return lambda j: (0, jnp.clip(j - k * steps, 0, steps - 1))

    specs = []
    for k in range(count):
        specs += [pl.BlockSpec((n, tile), left_tile(k)), pl.BlockSpec((n, width), lambda j: (0, 0))]
    return pl.pallas_call(
        kernel,
        grid=(count * steps,),
        in_specs=specs,
        out_specs=pl.BlockSpec((tile, width), lambda j: (j % steps, j // steps)),
        out_shape=jax.ShapeDtypeStruct((depth, count * width), low),
        compiler_params=params(),
        cost_estimate=cost(2 * n * depth * width * count, 2 * count * (n * (depth + width) + depth * width)),
    )(*(member for pair in pairs for member in pair))


def chunk_specs(blocks, width):
    return [pl.BlockSpec(block.shape, lambda j: (0, 0)) for block in blocks]


def mlp_forward(blocks, up_w, gate_w, scales, chunk, earlier):
    n = sum(block.shape[0] for block in blocks)
    depth, units = up_w.shape
    tile = 2 * LANES
    span = 512
    count = len(blocks)

    def kernel(*refs):
        ins, rest = refs[:count], refs[count:]
        up_ref, gate_ref, scale_ref = rest[:3]
        mid_ref, up_out, gate_out, act_out = rest[-4:]

        @pl.when(pl.program_id(0) == 0)
        def _():
            at = 0
            for ref in ins:
                mid_ref[at : at + ref.shape[0], :] = ref[...]
                at += ref.shape[0]

        for start in range(0, n, span):
            rows = slice(start, start + span)
            left = mid_ref[rows, :]
            up = nn(left, up_ref[...])
            gate = nn(left, gate_ref[...])
            lifted = scale_ref[1:2, :] * gate
            up_out[rows, :] = up.astype(low)
            gate_out[rows, :] = gate.astype(low)
            act_out[rows, :] = (scale_ref[0:1, :] * up * (lifted * jax.nn.sigmoid(lifted))).astype(low)

    weight = pl.BlockSpec((depth, tile), lambda j: (0, j))
    whole = pl.BlockSpec((n, depth), lambda j: (chunk, 0))
    tiles = pl.BlockSpec((n, tile), lambda j: (chunk, j))
    big = jax.ShapeDtypeStruct((2 * n, depth), low)
    wide_units = jax.ShapeDtypeStruct((2 * n, units), low)
    return pl.pallas_call(
        kernel,
        grid=(units // tile,),
        in_specs=chunk_specs(blocks, depth)
        + [weight] * 2
        + [pl.BlockSpec((2, tile), lambda j: (0, j))]
        + [pl.BlockSpec(memory_space=pl.ANY)] * len(earlier),
        out_specs=[whole, tiles, tiles, tiles],
        out_shape=[big, wide_units, wide_units, wide_units],
        input_output_aliases={count + 3 + i: i for i in range(len(earlier))},
        compiler_params=params(),
        cost_estimate=cost(4 * n * depth * units, 2 * (2 * n * depth + 2 * depth * units + 3 * n * units)),
    )(*blocks, up_w, gate_w, scales, *earlier)


def mlp_backward(blocks, up_w, gate_w, down_w, scales, up_raw, gate_raw, chunk, earlier):
    n = sum(block.shape[0] for block in blocks)
    depth, units = up_w.shape
    tile = 2 * LANES
    span = 512
    count = len(blocks)
    steps = units // tile

    def kernel(*refs):
        ins, rest = refs[:count], refs[count:]
        down_ref, scale_ref, up_raw_ref, gate_raw_ref, up_ref, gate_ref = rest[:6]
        branch_ref, up_out, gate_out, part_ref, gain_ref, kept, weights, sems = rest[-8:]
        step = pl.program_id(0)
        fetches = [
            pltpu.make_async_copy(ref, weights.at[i], sems.at[i]) for i, ref in enumerate((up_ref, gate_ref))
        ]

        @pl.when(step == 0)
        def _():
            for fetch in fetches:
                fetch.start()
            at = 0
            for ref in ins:
                branch_ref[at : at + ref.shape[0], :] = ref[...]
                at += ref.shape[0]

        up_gain, gate_gain = scale_ref[0:1, :], scale_ref[1:2, :]
        up_term = gate_term = jnp.zeros((1, tile), wide)
        for start in range(0, n, span):
            rows = slice(start, start + span)
            grad = nn(branch_ref[rows, :], down_ref[...])
            up = up_raw_ref[rows, :].astype(wide)
            gate = gate_raw_ref[rows, :].astype(wide)
            lifted = gate_gain * gate
            slope = jax.nn.sigmoid(lifted)
            swished = lifted * slope
            up_part = grad * swished
            lifted_grad = grad * up * (up_gain * (slope + swished * (1.0 - slope)))
            up_term = up_term + jnp.sum(up_part * up, axis=0, keepdims=True)
            gate_term = gate_term + jnp.sum(lifted_grad * gate, axis=0, keepdims=True)
            up_low = (up_part * up_gain).astype(low)
            gate_low = (lifted_grad * gate_gain).astype(low)
            up_out[rows, :] = up_low
            gate_out[rows, :] = gate_low
            kept[0, step, rows, :] = up_low
            kept[1, step, rows, :] = gate_low
        gain_ref[...] = jnp.concatenate([up_term, gate_term, jnp.zeros((6, tile), wide)], axis=0)

        @pl.when(step == steps - 1)
        def _():
            for fetch in fetches:
                fetch.wait()
            for start in range(0, n, span):
                rows = slice(start, start + span)
                ups, gates = (
                    jnp.concatenate([kept[i, k, rows, :] for k in range(steps)], axis=1) for i in range(2)
                )
                for at in range(0, depth, tile):
                    part = nt(ups, weights[0, at : at + tile, :]) + nt(gates, weights[1, at : at + tile, :])
                    part_ref[rows, at : at + tile] = part.astype(low)

    weight = pl.BlockSpec((depth, tile), lambda j: (0, j))
    anywhere = pl.BlockSpec(memory_space=pl.ANY)
    whole = pl.BlockSpec((n, depth), lambda j: (chunk, 0))
    tiles = pl.BlockSpec((n, tile), lambda j: (chunk, j))
    big = jax.ShapeDtypeStruct((2 * n, depth), low)
    wide_units = jax.ShapeDtypeStruct((2 * n, units), low)
    return pl.pallas_call(
        kernel,
        grid=(steps,),
        in_specs=chunk_specs(blocks, depth)
        + [weight, pl.BlockSpec((2, tile), lambda j: (0, j)), tiles, tiles, anywhere, anywhere]
        + [anywhere] * len(earlier),
        out_specs=[
            whole, tiles, tiles,
            pl.BlockSpec((n, depth), lambda j: (0, 0)), pl.BlockSpec((8, tile), lambda j: (0, j)),
        ],
        out_shape=[
            big, wide_units, wide_units,
            jax.ShapeDtypeStruct((n, depth), low), jax.ShapeDtypeStruct((8, units), wide),
        ],
        scratch_shapes=[
            pltpu.VMEM((2, steps, n, tile), low), pltpu.VMEM((2, depth, units), low),
            pltpu.SemaphoreType.DMA((2,)),
        ],
        input_output_aliases={count + 6 + i: i for i in range(len(earlier))},
        compiler_params=params(),
        cost_estimate=cost(6 * n * depth * units, 2 * (2 * n * depth + 3 * depth * units + 4 * n * units)),
    )(*blocks, down_w, scales, up_raw, gate_raw, up_w, gate_w, *earlier)


def dot(left, right):
    return jnp.dot(left, right, preferred_element_type=wide)


def dot_rows(left, right):
    return tn(left, right).astype(low)


def place(blocks, indices):
    ndim = min(block.ndim for block in blocks)
    n = len(indices)
    count = len(blocks)
    pieces = [
        (i, at) for i, block in enumerate(blocks) for at in ([None] if block.ndim == ndim else range(block.shape[0]))
    ]
    shape = blocks[-1].shape[-ndim:]
    where_to = jnp.stack([jnp.asarray(i, jnp.int32) for i in indices])

    def kernel(index_ref, *refs):
        out, sems = refs[count], refs[count + 1]
        copies = []
        for k, (i, at) in enumerate(pieces):
            source = refs[i] if at is None else refs[i].at[at]
            copies.append(pltpu.make_async_copy(source, out.at[index_ref[k]], sems.at[k]))
        for copy in copies:
            copy.start()
        for copy in copies:
            copy.wait()

    anywhere = pl.BlockSpec(memory_space=pl.ANY)
    out = jax.ShapeDtypeStruct((n,) + shape, blocks[0].dtype)
    return pl.pallas_call(
        kernel,
        in_specs=[pl.BlockSpec(memory_space=pltpu.SMEM)] + [anywhere] * count,
        out_specs=pl.BlockSpec(memory_space=pltpu.VMEM),
        out_shape=out,
        scratch_shapes=[pltpu.SemaphoreType.DMA((n,))],
        compiler_params=params(),
        cost_estimate=cost(0, 2 * out.size * out.dtype.itemsize),
    )(where_to, *blocks)


def half_tiles(first, second, first_upper, second_upper):
    first, second = first.astype(wide), second.astype(wide)
    axis = first.ndim - 1
    first = jnp.where(first_upper, pltpu.roll(first, HALF, axis), first)
    second = jnp.where(second_upper, second, pltpu.roll(second, HALF, axis))
    lane = lax.broadcasted_iota(jnp.int32, first.shape, axis)
    return jnp.where(lane < HALF, first, second).astype(low)


def unit_pack(weights):
    rows, units = weights[0].shape
    main = units // CHIPS // LANES * LANES
    n = len(weights)

    def kernel(*refs):
        out = refs[n]
        target = pl.program_id(0)
        for i in range(n):
            start = pl.multiple_of(target * main, LANES)
            out[0, :, i * main : (i + 1) * main] = refs[i][:, pl.ds(start, main)]
        tile = pl.multiple_of(CHIPS * main + (target // 2) * LANES, LANES)
        upper = (target & 1) == 1
        rests = [refs[i][:, pl.ds(tile, LANES)] for i in range(n)]
        out[0, :, n * main :] = half_tiles(rests[0], rests[-1], upper, upper)

    whole = pl.BlockSpec((rows, units), lambda k: (0, 0))
    return pl.pallas_call(
        kernel,
        grid=(CHIPS,),
        in_specs=[whole] * n,
        out_specs=pl.BlockSpec((1, rows, n * main + LANES), lambda k: (k, 0, 0)),
        out_shape=jax.ShapeDtypeStruct((CHIPS, rows, n * main + LANES), weights[0].dtype),
    )(*weights)


def unit_lay(n, mine, theirs, core):
    count, _, rows, columns = mine.shape
    main = (columns - LANES) // n
    units = count * main + count // 2 * LANES

    def kernel(core_ref, *refs):
        outs = refs[2:]
        for side in range(2):
            slot = core_ref[0] ^ side
            blocks = refs[side]
            for i in range(n):
                for k in range(count):
                    outs[i][slot, :, k * main : (k + 1) * main] = blocks[k, 0, :, i * main : (i + 1) * main]
                tile = n * main
                upper = i == 1
                for k in range(0, count, 2):
                    at = count * main + k // 2 * LANES
                    outs[i][slot, :, at : at + LANES] = half_tiles(
                        blocks[k, 0, :, tile : tile + LANES],
                        blocks[k + 1, 0, :, tile : tile + LANES],
                        upper,
                        upper,
                    )

    block = pl.BlockSpec((count, 1, rows, columns), lambda q: (0, q, 0, 0))
    out = pl.BlockSpec((2, rows, units), lambda q: (q, 0, 0))
    return pl.pallas_call(
        kernel,
        grid=(CHIPS,),
        in_specs=[pl.BlockSpec(memory_space=pltpu.SMEM)] + [block] * 2,
        out_specs=[out] * n,
        out_shape=[jax.ShapeDtypeStruct((2 * CHIPS, rows, units), low)] * n,
        compiler_params=params(),
        cost_estimate=cost(0, 14 * n * 8 * rows * units // 4),
    )(core.reshape(1), mine, theirs)


def unit_unlay(grads, core):
    count = lax.axis_size("tensor")
    _, rows, units = grads[0].shape
    n = len(grads)
    main = units // count // LANES * LANES
    columns = n * main + (n + 1) // 2 * LANES

    def kernel(core_ref, *refs):
        for side in range(2):
            slot = core_ref[0] ^ side
            out = refs[n + side]
            for k in range(count):
                for i in range(n):
                    out[k, 0, :, i * main : (i + 1) * main] = refs[i][slot, :, k * main : (k + 1) * main]
                at = count * main + k // 2 * LANES
                upper = k % 2 == 1
                rests = [refs[i][slot, :, at : at + LANES] for i in range(n)]
                for i in range(0, n, 2):
                    to = n * main + i // 2 * LANES
                    out[k, 0, :, to : to + LANES] = half_tiles(
                        rests[i], rests[min(i + 1, n - 1)], upper, upper
                    )

    block = pl.BlockSpec((2, rows, units), lambda q: (q, 0, 0))
    return pl.pallas_call(
        kernel,
        grid=(CHIPS,),
        in_specs=[pl.BlockSpec(memory_space=pltpu.SMEM)] + [block] * n,
        out_specs=[pl.BlockSpec((count, 1, rows, columns), lambda q: (0, q, 0, 0))] * 2,
        out_shape=[jax.ShapeDtypeStruct((count, CHIPS, rows, columns), low)] * 2,
        compiler_params=params(),
        cost_estimate=cost(0, 14 * n * 8 * rows * units // 4),
    )(core.reshape(1), *grads)


def unit_unpack(n, blocks):
    _, rows, columns = blocks.shape
    main = (columns - (n + 1) // 2 * LANES) // n
    units = CHIPS * main + CHIPS // 2 * LANES

    def kernel(block_ref, *outs):
        for i in range(n):
            for j in range(CHIPS):
                outs[i][:, j * main : (j + 1) * main] = block_ref[j, :, i * main : (i + 1) * main].astype(wide)
            tile = n * main + i // 2 * LANES
            upper = i % 2 == 1
            for j in range(0, CHIPS, 2):
                at = CHIPS * main + j // 2 * LANES
                outs[i][:, at : at + LANES] = half_tiles(
                    block_ref[j, :, tile : tile + LANES], block_ref[j + 1, :, tile : tile + LANES], upper, upper
                ).astype(wide)

    return pl.pallas_call(
        kernel,
        out_shape=[jax.ShapeDtypeStruct((rows, units), wide)] * n,
        compiler_params=params(),
    )(blocks)


def per_device(
    block_in, out_grad, global_pos,
    w_query, w_key, w_value, w_out, w_up, w_gate, w_down,
    qk_gain, up_gain, gate_gain, att_rate, mlp_rate,
):
    count = lax.axis_size("tensor")
    plane = lax.axis_size(DP)
    micro_count, _, local_rows, model_width = block_in.shape
    assert micro_count == 2 and count == 4
    seq_len = local_rows * count
    head_width = w_query.shape[1]
    core_heads = head_width * 2
    unit_width = w_up.shape[1]
    plane_unit = unit_width // CHIPS
    main = plane_unit // LANES * LANES
    rest = plane_unit - main
    me = lax.axis_index(DP)
    z = lax.axis_index("tensor")
    core = me & 1
    chip = (me >> 1) & 3
    early = z < 2

    def across(value, pairs):
        return lax.ppermute(
            value, ALL, [(a * count + b, c * count + d) for (a, b), (c, d) in pairs]
        )

    def home(far):
        return [
            ((p, t), ((p & ~1) | (t & 1), ((t & 2) ^ (2 if far else 0)) | (p & 1)))
            for p in range(plane)
            for t in range(count)
        ]

    def seq_near(value):
        return across(lax.dynamic_index_in_dim(value, z >> 1, 0, keepdims=False), home(False))

    def seq_far(value):
        return across(lax.dynamic_index_in_dim(value, 1 - (z >> 1), 0, keepdims=False), home(True))

    def seq_join(near, far):
        return pick(early, near, far), pick(early, far, near)

    def from_sequence(first, second):
        near = across(pick(early, first, second), [(b, a) for a, b in home(False)])
        far = across(pick(early, second, first), [(b, a) for a, b in home(True)])
        return pick(early, jnp.stack([near, far]), jnp.stack([far, near]))

    def both_cores(first, second):
        return place(
            [first, second, swap(first, 1), swap(second, 1)], [core, core + 2, 1 - core, 3 - core]
        ).reshape(seq_len, model_width)

    def core_scatter(partial):
        split = partial.reshape(2, 2, local_rows, model_width)
        got = swap(lax.dynamic_index_in_dim(split, 1 - core, 1, keepdims=False), 1)
        mine = lax.dynamic_index_in_dim(split, core, 1, keepdims=False)
        return tuple(mine[i].astype(wide) + got[i].astype(wide) for i in range(2))

    def head_pairs(other_core, second):
        return [
            ((p ^ other_core, (t + 2 * (p & 1) + second) % count), (p, t))
            for p in range(plane)
            for t in range(count)
        ]

    def paired(a, b):
        return jnp.concatenate(
            [a[:, :head_width], b[:, :head_width], a[:, head_width:], b[:, head_width:]], axis=1
        )

    def attn_fetch(first, second):
        packed = outer_gather(jnp.concatenate([first, second], axis=1))
        groups = [[across(packed, head_pairs(side, which)) for which in range(2)] for side in range(2)]
        return jnp.stack([paired(*group) for group in groups])

    def attn_first(sides):
        return sides, swap(sides, 2), swap(sides, 4)

    def attn_second(first):
        sides, along_x, along_y = first
        return sides, along_x, along_y, swap(along_y[0], 2), swap(along_x[1], 4)

    def attn_lay(gathered):
        sides, along_x, along_y, d_own, d_other = gathered
        return full_rows(
            place(
                [sides, along_x, along_y, d_own, d_other],
                [2 * (chip ^ (i // 2)) + (core ^ (i % 2)) for i in range(8)],
            )
        )

    def attn_spread(packed, extra):
        columns = packed.shape[1]
        by_chip = plane_rows(packed).reshape(CHIPS, -1, columns)
        pieces = []
        for k in range(CHIPS):
            block = lax.dynamic_index_in_dim(by_chip, chip ^ k, 0, keepdims=False)
            pieces.append(jnp.concatenate([block, extra.astype(low)]))
        return scatter_second(scatter_first(pieces)).astype(low)

    def attn_scatter(spread):
        rows = (spread.shape[0] - EXTRA) // 2
        cores = spread[: 2 * rows].reshape(2, rows, -1)
        got = []
        for other_core in range(2):
            side = lax.dynamic_index_in_dim(cores, core ^ other_core, 0, keepdims=False)
            side = jnp.concatenate([side, spread[2 * rows :]])
            for which in range(2):
                at = which * head_width
                piece = jnp.concatenate(
                    [side[:, at : at + head_width], side[:, core_heads + at : core_heads + at + head_width]],
                    axis=1,
                )
                pairs = [(b, a) for a, b in head_pairs(other_core, which)]
                got.append(across(piece, pairs).astype(wide))
        grads = outer_scatter(sum(piece[:rows] for piece in got))
        small = jnp.stack([piece[rows:] for piece in got])
        total = jnp.zeros(small.shape[1:], wide)
        for t in range(count):
            back = (z - t) % count
            index = 2 * ((back >> 1) ^ core) + (back & 1)
            total = total + lax.dynamic_index_in_dim(small, index, 0, keepdims=False)
        bit = 8
        while bit < plane:
            total = total + swap(total, bit)
            bit *= 2
        return grads[:, :head_width], grads[:, head_width:], total

    def unit_send(weights):
        packed = unit_pack([outer_gather(w) for w in weights])
        return lax.all_to_all(packed, "chip", 0, 0, tiled=True)

    def unit_join(n, mine):
        return [full_rows(w) for w in unit_lay(n, mine, swap(mine, 1), core)]

    def unit_collect(grads):
        keep, send = unit_unlay([plane_rows(g) for g in grads], core)
        return (keep.astype(wide) + swap(send, 1).astype(wide)).astype(low)

    def unit_return(n, total):
        return [outer_scatter(g) for g in unit_unpack(n, lax.all_to_all(total, "chip", 0, 0, tiled=True))]

    tie = lax.optimization_barrier

    def shifted(value, step):
        return lax.ppermute(value, "tensor", [((i + step) % count, i) for i in range(count)])

    qk_sides = attn_fetch(w_query, w_key)
    far = seq_far(block_in[:, 0])
    ug_laid = unit_send([w_up, w_gate])
    down_laid = unit_send([w_down])
    qk_sides, ug_laid, block_in, qk_gain, global_pos = tie((qk_sides, ug_laid, block_in, qk_gain, global_pos))
    qk_first = attn_first(qk_sides)
    near = seq_near(block_in[:, 0])
    mains = lax.dynamic_slice_in_dim(jnp.stack([up_gain, gate_gain]), chip * main, main, 1)
    rests = lax.dynamic_slice_in_dim(jnp.stack([up_gain, gate_gain]), CHIPS * main + chip * rest, rest, 1)
    gains = jnp.concatenate([jnp.concatenate([mains, rests], axis=1).reshape(1, -1), qk_gain[None]], axis=1)
    gains = [gains] + [shifted(gains, k) for k in range(1, count)]
    places_here = global_pos[:, 0]
    places_there = swap(places_here, 1)
    qk_first, near, far, w_value, w_out, gains, places_there = tie(
        (qk_first, near, far, w_value, w_out, gains, places_there)
    )
    vo_sides = attn_fetch(w_value, w_out)
    qk_gathered = attn_second(qk_first)
    tokens = seq_join(near, far)
    sequence = both_cores(*tokens)
    vo_sides, qk_gathered, sequence, ug_laid, down_laid, gains = tie(
        (vo_sides, qk_gathered, sequence, ug_laid, down_laid, gains)
    )
    ug_shifted = lax.all_gather(ug_laid, "tensor")
    down_shifted = lax.all_gather(down_laid, "tensor")
    vo_first = attn_first(vo_sides)
    qk_w = attn_lay(qk_gathered)
    gains = jnp.concatenate(gains)
    gains = lax.dynamic_slice_in_dim(jnp.concatenate([gains, gains]), count - z, count, 0)
    unit_gains = gains[:, : 2 * plane_unit].reshape(count, 2, plane_unit).transpose(1, 0, 2)
    scales = jnp.concatenate(
        [unit_gains[..., :main].reshape(2, -1), unit_gains[..., main:].reshape(2, -1)], axis=1
    )
    head_gain = gains[:, 2 * plane_unit :]
    head_gain = lax.dynamic_slice_in_dim(
        jnp.concatenate([head_gain, head_gain]), z + 2 * core, 2, 0
    ).reshape(core_heads)
    places = lax.dynamic_index_in_dim(
        pick((z & 1) == core, places_here, places_there), z >> 1, 0, keepdims=False
    )
    flags = jnp.any(places[:, None] == jnp.arange(seq_len, dtype=jnp.int32)[None, :], axis=0).astype(wide)
    flag_row, flag_col = flags[None], flags[:, None]

    heads, raw = project_heads(sequence, qk_w, jnp.concatenate([head_gain, head_gain]))
    vo_w = attn_lay(attn_second(vo_first))
    value_w, out_w = vo_w[:, :core_heads], vo_w[:, core_heads:]
    value_rows = dot(sequence, value_w).astype(low)
    mixed, lse = attend_forward(heads, value_rows, flag_row, flag_col)
    att_branch = core_scatter(sum_back([(mixed, 0, core_heads)], [(vo_w, 1, core_heads)]))
    hidden, att_pull = zip(
        *(jax.vjp(settle, tokens[i].astype(wide), att_branch[i], att_rate) for i in range(2))
    )

    first_mid = plane_first(hidden[0].astype(low))
    first_mid, second_hidden = tie((first_mid, hidden[1]))
    mids = [plane_second(first_mid), plane_second(plane_first(second_hidden.astype(low)))]
    up_w, gate_w = unit_join(2, ug_shifted)
    laid = ()
    for i in range(2):
        laid = mlp_forward(mids[i], up_w, gate_w, scales, i, laid)
    laid, out_grad, down_shifted = tie((laid, out_grad, down_shifted))
    mid, up_raw, gate_raw, activated = laid
    units, chunk_rows = activated.shape[1], CHIPS * local_rows
    cotangent = seq_join(seq_near(out_grad[:, 0].astype(low)), seq_far(out_grad[:, 0].astype(low)))
    (down_w,) = unit_join(1, down_shifted)

    def by_chip(value):
        return [value[k * local_rows : (k + 1) * local_rows] for k in range(CHIPS)]

    def back(i):
        return sum_back([(activated, 0, units)], [(down_w, 0, units)], chunk_rows, i)

    def turn(i, sent):
        rows, pull = jax.vjp(settle, hidden[i], scatter_second(sent), mlp_rate)
        direct, branch_grad, term = pull(cotangent[i].astype(wide))
        return rows, direct, term, plane_first(branch_grad.astype(low))

    sent = scatter_first(by_chip(back(0)))
    sent, second_part = tie((sent, back(1)))
    second_sent = scatter_first(by_chip(second_part))
    rows_a, direct_a, term_a, first_a = turn(0, sent)
    rows_b, direct_b, term_b, first_b = turn(1, second_sent)

    branch_a = plane_second(first_a)
    branch_a, first_b = tie((branch_a, first_b))
    branch_b = plane_second(first_b)
    weights = (up_w, gate_w, down_w, scales, up_raw, gate_raw)
    *laid, part, unit_term_a = mlp_backward(branch_a, *weights, 0, ())
    sent = scatter_first(by_chip(part))
    laid, rows_a, rows_b = tie((laid, rows_a, rows_b))
    *laid, part, unit_term_b = mlp_backward(branch_b, *weights, 1, laid)
    block_out = from_sequence(rows_a.astype(low), rows_b.astype(low)).astype(wide)
    branch, up_low, gate_low = laid
    sent, part = tie((sent, part))
    second_sent = scatter_first(by_chip(part))
    down_grad = dot_rows(branch, activated)
    sent, second_sent, down_grad, mid = tie((sent, second_sent, down_grad, mid))
    hidden_total = [direct_a + scatter_second(sent), direct_b + scatter_second(second_sent)]
    up_w_grad, gate_w_grad = dot_rows(mid, up_low), dot_rows(mid, gate_low)
    input_direct, att_grad, att_rate_terms = zip(*(att_pull[i](hidden_total[i]) for i in range(2)))
    att_low = both_cores(*(grad.astype(low) for grad in att_grad))
    unit_blocks = unit_collect([up_w_grad, gate_w_grad, down_grad])
    att_low, unit_blocks = tie((att_low, unit_blocks))
    units_back = lax.psum_scatter(unit_blocks, "tensor", scatter_dimension=0)
    mixed_grad = dot(att_low, out_w).astype(low)
    heads_low, vraw_low, head_terms = attend_backward(
        heads, raw, value_rows, mixed, mixed_grad, lse, head_gain, flag_row, flag_col
    )
    in_part = sum_back(
        [(heads_low, 0, 2 * core_heads), (vraw_low, 0, core_heads)],
        [(qk_w, 0, 2 * core_heads), (vo_w, 0, core_heads)],
    )
    in_rows = [input_direct[i] + part for i, part in enumerate(core_scatter(in_part))]
    in_grad = from_sequence(*(rows.astype(low) for rows in in_rows)).astype(wide)
    unit_terms = [unit_term_a[:2], unit_term_b[:2]]
    mlp_rate_terms = [term_a, term_b]

    small = jnp.concatenate(
        [
            unit_terms[0] + unit_terms[1],
            (att_rate_terms[0] + att_rate_terms[1])[None],
            (mlp_rate_terms[0] + mlp_rate_terms[1])[None],
        ]
    )
    small = small + swap(small, 1)
    unit_rows = jnp.concatenate(
        [small[:2, : count * main].reshape(2, count, main), small[:2, count * main :].reshape(2, count, rest)],
        axis=2,
    )
    unit_rows = lax.dynamic_slice_in_dim(
        jnp.concatenate([unit_rows, unit_rows], axis=1), z + 2 * core, 2, 1
    ).reshape(1, 4 * plane_unit)
    rate_rows = jnp.broadcast_to(small[2:].reshape(4, 2, 1, head_width), (4, 2, 2, head_width))
    rate_rows = rate_rows.reshape(1, 4, 4 * head_width)
    own_chip = jnp.arange(CHIPS)[:, None] == chip
    vo_extra = jnp.concatenate(
        [
            jnp.where(own_chip, unit_rows, 0.0),
            jnp.where(own_chip[..., None], rate_rows, 0.0).reshape(4 * CHIPS, -1),
            jnp.zeros((EXTRA - 5 * CHIPS, 4 * head_width), wide),
        ]
    )
    qk_extra = jnp.concatenate(
        [
            jnp.where(own_chip, head_terms[:2].reshape(1, 4 * head_width), 0.0),
            jnp.zeros((EXTRA - CHIPS, 4 * head_width), wide),
        ]
    )
    vo_spread = attn_spread(rows_product([(sequence, vraw_low), (att_low, mixed)]), vo_extra)
    qk_spread = attn_spread(dot_rows(sequence, heads_low), qk_extra)
    grad_value, grad_out, vo_small = attn_scatter(vo_spread)
    grad_query, grad_key, qk_small = attn_scatter(qk_spread)
    grad_up, grad_gate, grad_down = unit_return(3, units_back)

    units = vo_small[:CHIPS].reshape(CHIPS, 2, plane_unit).transpose(1, 0, 2)
    units = jnp.concatenate([units[..., :main].reshape(2, -1), units[..., main:].reshape(2, -1)], axis=1)
    rates = jnp.sum(vo_small[CHIPS : 5 * CHIPS].reshape(CHIPS, 2, model_width), axis=0)
    head_sums = jnp.sum(qk_small[:CHIPS], axis=0)
    grad_qk_gain = head_sums[:head_width] + head_sums[head_width:]
    return (
        block_out[:, None], in_grad[:, None],
        grad_query, grad_key, grad_value, grad_out, grad_up, grad_gate, grad_down,
        grad_qk_gain, units[0], units[1], rates[0], rates[1],
    )


def solution(mesh):
    shape = dict(mesh.shape)
    plane, count = shape["dp"], shape["tensor"]
    split = Mesh(mesh.devices.reshape(plane // 8, CHIPS, 2, count), ALL)
    tokens = P(None, DP, "tensor", None)
    matrix = P(DP, "tensor")
    in_specs = (tokens, tokens, P(None, DP, None)) + (matrix,) * 7 + (P("tensor"),) * 3 + (P(), P())
    out_specs = (tokens, tokens) + (matrix,) * 7 + (P("tensor"),) * 3 + (P(), P())
    return jax.shard_map(
        per_device, mesh=split, in_specs=in_specs, out_specs=out_specs, check_vma=False
    )
```

time: 1550 us -> 781 us (0.50)
  waiting for transfers between devices: 1000 us -> 231 us
  matrix products: 294 us -> 39.4 us
  Pallas kernels: 0 us -> 189 us
  starting transfers between devices: 2.47 us -> 161 us
  blocking collectives: 88.7 us -> 0 us
  other arithmetic: 107 us -> 75.1 us
  local copies, waits for them, and re-layouts: 34.1 us -> 56 us
    reduce_scatter x12 -> x1, waiting for transfers between devices: 472 us -> 0.01 us  [per_device(): units_back = lax.psum_scatter(unit_blocks, 'tensor', scatter_dimension=0)]
    all_gather x11 -> x2, waiting for transfers between devices: 394 us -> 0.02 us  [the longest x1 0.02 us: per_device(): ug_shifted = lax.all_gather(ug_laid, 'tensor')]
    dot_general x66 -> x6, matrix products: 294 us -> 39.4 us  [the longest x4 32 us: tn(): lax.dot_general(left, right, (((0,), (0,)), ((), ())), preferred_element_...]
    ppermute x0 -> x86, waiting for transfers between devices: none -> 216 us  [the longest x59 143 us: swap(): return lax.ppermute(value, DP, [(i, i ^ bit) for i in range(count)])]
    pallas_call x0 -> x22, Pallas kernels: none -> 189 us  [the longest x2 39 us: mlp_backward(): pl.pallas_call(kernel, grid=(steps,), in_specs=chunk_specs(blocks, depth)...]
    ppermute x0 -> x86, starting transfers between devices: none -> 149 us  [the longest x59 77.3 us: swap(): return lax.ppermute(value, DP, [(i, i ^ bit) for i in range(count)])]
    unnamed x29 -> x3, waiting for transfers between devices: 136 us -> 0.05 us
    all_gather x4 -> x0, blocking collectives: 48 us -> none  [the longest x1 13.3 us: fetch_attn(): lax.all_gather(w_query, 'dp', axis=0, tiled=True)]
  transfers between devices with their start and end apart: 26 -> 92, of which waited for: 23 -> 30; matrix products, arithmetic and copies ran while one was open for 13% -> 14% of each run, Pallas kernels for 0% -> 17%
where the time goes in v1:
time: 781 us; the launch traced here: 768 us
  waiting for transfers between devices  231 us (30%)
  Pallas kernels  189 us (24%)
  starting transfers between devices  161 us (21%)
  other arithmetic  75.1 us (10%)
  local copies, waits for them, and re-layouts  56 us (7%)
  matrix products  39.4 us (5%)
  between operations  16.1 us (2%)
    ppermute x59, waiting for transfers between devices, swap(): return lax.ppermute(value, DP, [(i, i ^ bit) for i in range(count)])  143 us
    ppermute x59, starting transfers between devices, swap(): return lax.ppermute(value, DP, [(i, i ^ bit) for i in range(count)])  77.3 us
    ppermute x24, starting transfers between devices, across(): lax.ppermute(value, ALL, [(a * count + b, c * count + d) for (a, b), (c,...  70.7 us
    ppermute x24, waiting for transfers between devices, across(): lax.ppermute(value, ALL, [(a * count + b, c * count + d) for (a, b), (c,...  64.6 us
    pallas_call x2, Pallas kernels, mlp_backward(): pl.pallas_call(kernel, grid=(steps,), in_specs=chunk_specs(blocks, depth)...  39 us
    dot_general x4, matrix products, tn(): lax.dot_general(left, right, (((0,), (0,)), ((), ())), preferred_element_...  32 us
    pallas_call x1, Pallas kernels, attend_backward(): pl.pallas_call(kernel, grid=(pairs,), in_specs=[block, keys, block, block...  28.9 us
    pallas_call x4, Pallas kernels, sum_back(): pl.pallas_call(kernel, grid=(n // block,), in_specs=[pl.BlockSpec((block,...  24.4 us
  transfers between devices with their start and end apart: 92, of which 30 were waited for; matrix products, arithmetic and copies ran while one was open for 14% of the time, Pallas kernels for 17%

profile of v1, /device:TPU:0, one launch (start us, length us, event | category | flops | bytes accessed | tf_op | source)
XLA Modules:
  0.0 767.7 jit_solution(2245345713040271334)
XLA Ops:
  29.5 8.5 %all-to-all-done = bf16[4,160,640]{2,1,0:T(8,128)(2,1)S(1)} async-done(((bf16[4,160,640]{2,1,0:T(8,128)(2,1)}), bf16[4,160,640]{2,1,0:T(8,128)(2,1)S(1)}, u32[]{:S(2)}, u32[]{:S(2)}) %all-to-all-start) | async-done | bytes 819232 | tf_op jit(solution)/shard_map/all_to_all | solution.py:855
  43.8 15.4 %collective-permute-start.11 = (s32[2,64]{1,0:T(2,128)S(1)}, s32[2,64]{1,0:T(2,128)S(1)}, u32[]{:S(2)}, u32[]{:S(2)}) collective-permute-start(s32[2,64]{1,0:T(2,128)S(1)} %bitcast.318), channel_id=1, source_target_pairs={{0,4},{4,0},{8,12},{12,8},{16,20},{20,16},{24,28},{28,24},{1,5},{5... | collective-permute-start | bytes 1544 | tf_op jit(solution)/shard_map/ppermute | solution.py:30
  113.1 16.3 %collective-permute-done.21.refs_2_ = bf16[2,160,1280]{2,1,0:T(8,128)(2,1)} collective-permute-done((bf16[2,160,1280]{2,1,0:T(8,128)(2,1)}, bf16[2,160,1280]{2,1,0:T(8,128)(2,1)}, u32[]{:S(2)}, u32[]{:S(2)}) %collective-permute-start.21) | collective-permute-done | bytes 819232 | tf_op jit(solution)/shard_map/ppermute | solution.py:30
  138.9 12.4 %shard_map.258 = (bf16[1024,1280]{1,0:T(8,128)(2,1)S(1)}, bf16[1024,1280]{1,0:T(8,128)(2,1)S(1)}) custom-call(bf16[1024,1280]{1,0:T(8,128)(2,1)} %bitcast.266, bf16[1280,1280]{1,0:T(8,128)(2,1)} %bitcast.303, f32[1,1280]{1,0:T(1,128)S(1)} %broadcast_in_dim.125.gain_ref), custom_call_target="tpu_custom_call" | custom-call | flops 3355443200 | bytes 11141120 | tf_op jit(solution)/shard_map/pallas_call | solution.py:160
  161.5 15.7 %shard_map.260 = (bf16[1024,640]{1,0:T(8,128)(2,1)S(1)}, f32[5,8,1024]{2,1,0:T(8,128)S(1)}) custom-call(bf16[1024,1280]{1,0:T(8,128)(2,1)S(1)} %get-tuple-element.151.q_ref.k_ref, bf16[1024,1280]{1,0:T(8,128)(2,1)S(1)} %get-tuple-element.151.q_ref.k_ref, bf16[1024,640]{1,0:T(8,128)(2,1)S(1)} %fusion.5.v_ref, f32[1,1024]{1,0:T(1,128)S(1)} %bitcast.277, ...), custom_call_target="tpu_custom_call" | custom-call | flops 10737418240 | bytes 6553600 | tf_op jit(solution)/shard_map/pallas_call | solution.py:222
  194.7 15.3 %collective-permute-done.26.refs_2_ = bf16[256,1280]{1,0:T(8,128)(2,1)} collective-permute-done((bf16[256,1280]{1,0:T(8,128)(2,1)S(1)}, bf16[256,1280]{1,0:T(8,128)(2,1)}, u32[]{:S(2)}, u32[]{:S(2)}) %collective-permute-start.26) | collective-permute-done | bytes 655392 | tf_op jit(solution)/shard_map/ppermute | solution.py:30
  219.7 10.3 %collective-permute-done.28.refs_2_ = bf16[256,1280]{1,0:T(8,128)(2,1)} collective-permute-done((bf16[256,1280]{1,0:T(8,128)(2,1)}, bf16[256,1280]{1,0:T(8,128)(2,1)}, u32[]{:S(2)}, u32[]{:S(2)}) %collective-permute-start.28) | collective-permute-done | bytes 655392 | tf_op jit(solution)/shard_map/ppermute | solution.py:30
  239.5 12.4 %shard_map.263 = (bf16[2048,1280]{1,0:T(8,128)(2,1)}, bf16[2048,1280]{1,0:T(8,128)(2,1)}, bf16[2048,1280]{1,0:T(8,128)(2,1)}, bf16[2048,1280]{1,0:T(8,128)(2,1)}) custom-call(bf16[256,1280]{1,0:T(8,128)(2,1)S(1)} %copy-done.19, bf16[256,1280]{1,0:T(8,128)(2,1)S(1)} %copy-done.27, bf16[256,1280]{1,0:T(8,128)(2,1)} %collective-permute-done.26.refs_2_, ...), custom_call_target="tpu_custom_call" | custom-call | flops 6710886400 | bytes 19660800 | tf_op jit(solution)/shard_map/pallas_call | solution.py:445
  251.9 11.1 %shard_map.264 = (bf16[2048,1280]{1,0:T(8,128)(2,1)}, bf16[2048,1280]{1,0:T(8,128)(2,1)}, bf16[2048,1280]{1,0:T(8,128)(2,1)}, bf16[2048,1280]{1,0:T(8,128)(2,1)}) custom-call(bf16[256,1280]{1,0:T(8,128)(2,1)} %convert_element_type.445.refs_0_, ...), custom_call_target="tpu_custom_call", output_to_operand_aliasing={{0}: (8, {}), {1}: (9, {}), {2}: (10, {}), {3}: (11, {})} | custom-call | flops 6710886400 | bytes 19660800 | tf_op jit(solution)/shard_map/pallas_call | solution.py:445
  268.1 6.7 collective-permute-start.34
  304.1 13.6 %collective-permute-done.45 = bf16[256,1280]{1,0:T(8,128)(2,1)S(1)} collective-permute-done((bf16[256,1280]{1,0:T(8,128)(2,1)S(1)}, bf16[256,1280]{1,0:T(8,128)(2,1)S(1)}, u32[]{:S(2)}, u32[]{:S(2)}) %collective-permute-start.45) | collective-permute-done | bytes 655392 | tf_op jit(solution)/shard_map/ppermute | solution.py:30
  320.0 6.4 collective-permute-done.46
  348.1 11.6 %collective-permute-done.42.refs_2_ = bf16[256,1280]{1,0:T(8,128)(2,1)} collective-permute-done((bf16[256,1280]{1,0:T(8,128)(2,1)}, bf16[256,1280]{1,0:T(8,128)(2,1)}, u32[]{:S(2)}, u32[]{:S(2)}) %collective-permute-start.42) | collective-permute-done | bytes 655392 | tf_op jit(solution)/shard_map/ppermute | solution.py:30
  371.6 19.8 %shard_map.268 = (bf16[2048,1280]{1,0:T(8,128)(2,1)}, bf16[2048,1280]{1,0:T(8,128)(2,1)}, bf16[2048,1280]{1,0:T(8,128)(2,1)}, bf16[1024,1280]{1,0:T(8,128)(2,1)S(1)}, f32[8,1280]{1,0:T(8,128)S(1)}) custom-call(bf16[256,1280]{1,0:T(8,128)(2,1)} %get-tuple-element.180.refs_0_, bf16[256,1280]{1,0:T(8,128)(2,1)} %collective-permute-done.41.refs_1_, ...), custom_call_target="tpu_custom_call" | custom-call | flops 10066329600 | bytes 25559040 | tf_op jit(solution)/shard_map/pallas_call | solution.py:527
  395.0 6.5 collective-permute-start.51
  404.8 19.2 %shard_map.269 = (bf16[2048,1280]{1,0:T(8,128)(2,1)}, bf16[2048,1280]{1,0:T(8,128)(2,1)}, bf16[2048,1280]{1,0:T(8,128)(2,1)}, bf16[1024,1280]{1,0:T(8,128)(2,1)S(1)}, f32[8,1280]{1,0:T(8,128)S(1)}) custom-call(bf16[256,1280]{1,0:T(8,128)(2,1)S(1)} %copy-done.12, ...), custom_call_target="tpu_custom_call", output_to_operand_aliasing={{0}: (11, {}), {1}: (12, {}), {2}: (13, {})} | custom-call | flops 10066329600 | bytes 25559040 | tf_op jit(solution)/shard_map/pallas_call | solution.py:527
  424.0 11.8 %convolution_convert_fusion.3 = bf16[1280,1280]{1,0:T(8,128)(2,1)} fusion(bf16[2048,1280]{1,0:T(8,128)(2,1)} %get-tuple-element.206, bf16[2048,1280]{1,0:T(8,128)(2,1)} %get-tuple-element.172.refs_0_), kind=kOutput, calls=%fused_computation.4 | convolution fusion | flops 6712524800 | bytes 13762560 | tf_op jit(solution)/shard_map/dot_general | solution.py:124
  442.7 7.3 collective-permute-done.57
  450.5 8.7 %convolution_convert_fusion.1 = bf16[1280,1280]{1,0:T(8,128)(2,1)} fusion(bf16[2048,1280]{1,0:T(8,128)(2,1)S(1)} %bitcast.296, bf16[2048,1280]{1,0:T(8,128)(2,1)S(1)} %copy-done.51), kind=kOutput, calls=%fused_computation.2 | convolution fusion | flops 6712524800 | bytes 13762560 | tf_op jit(solution)/shard_map/dot_general | solution.py:124
  459.2 7.3 convolution_convert_fusion.2
  471.9 7.7 %shard_map.271 = (bf16[4,4,160,1024]{3,2,1,0:T(8,128)(2,1)}, bf16[4,4,160,1024]{3,2,1,0:T(8,128)(2,1)}) custom-call(s32[1]{0:T(128)} %bitcast.9.core_ref, bf16[8,160,1280]{2,1,0:T(8,128)(2,1)S(1)} %bitcast.265, bf16[8,160,1280]{2,1,0:T(8,128)(2,1)} %bitcast.300, bf16[8,160,1280]{2,1,0:T(8,128)(2,1)} %bitcast.299), custom_call_target="tpu_custom_call" | custom-call | bytes 17203200 | tf_op jit(solution)/shard_map/pallas_call | solution.py:689
  504.1 10.1 %add_convert_fusion = bf16[4,4,160,1024]{3,2,1,0:T(8,128)(2,1)} fusion(bf16[4,4,160,1024]{3,2,1,0:T(8,128)(2,1)} %collective-permute-done.65, bf16[4,4,160,1024]{3,2,1,0:T(8,128)(2,1)} %get-tuple-element.223), kind=kLoop, calls=%fused_computation | loop fusion | flops 10485760 | bytes 15728640 | tf_op jit(solution)/shard_map/convert_element_type | solution.py:862
  518.0 28.9 %shard_map.272 = (bf16[1024,1280]{1,0:T(8,128)(2,1)}, bf16[1024,640]{1,0:T(8,128)(2,1)S(1)}, f32[8,640]{1,0:T(8,128)S(1)}) custom-call(bf16[1024,1280]{1,0:T(8,128)(2,1)} %copy-done.28, bf16[1024,1280]{1,0:T(8,128)(2,1)} %copy-done.28, bf16[1024,640]{1,0:T(8,128)(2,1)S(1)} %copy-done.31, bf16[1024,1280]{1,0:T(8,128)(2,1)} %copy-done.29, ...), custom_call_target="tpu_custom_call" | custom-call | flops 21474836480 | bytes 13107200 | tf_op jit(solution)/shard_map/pallas_call | solution.py:322
  547.0 9.8 %shard_map.274 = bf16[1280,1280]{1,0:T(8,128)(2,1)} custom-call(bf16[1024,1280]{1,0:T(8,128)(2,1)S(1)} %bitcast.268, bf16[1024,640]{1,0:T(8,128)(2,1)S(1)} %get-tuple-element.228.refs_1_, bf16[1024,1280]{1,0:T(8,128)(2,1)} %bitcast.271, bf16[1024,640]{1,0:T(8,128)(2,1)S(1)} %copy-done.17), custom_call_target="tpu_custom_call" | custom-call | flops 3355443200 | bytes 11141120 | tf_op jit(solution)/shard_map/pallas_call | solution.py:396
  572.9 8.9 %shard_map.273 = bf16[1024,1280]{1,0:T(8,128)(2,1)S(1)} custom-call(bf16[1024,1280]{1,0:T(8,128)(2,1)} %get-tuple-element.227.refs_0_, bf16[1024,640]{1,0:T(8,128)(2,1)S(1)} %get-tuple-element.228.refs_1_, bf16[1280,1280]{1,0:T(8,128)(2,1)} %bitcast.304, bf16[1280,1280]{1,0:T(8,128)(2,1)} %bitcast.282), custom_call_target="tpu_custom_call" | custom-call | flops 5033164800 | bytes 11468800 | tf_op jit(solution)/shard_map/pallas_call | solution.py:362
  582.9 8.5 %collective-permute-done.77 = bf16[352,1280]{1,0:T(8,128)(2,1)S(1)} collective-permute-done((bf16[352,1280]{1,0:T(8,128)(2,1)S(1)}, bf16[352,1280]{1,0:T(8,128)(2,1)S(1)}, u32[]{:S(2)}, u32[]{:S(2)}) %collective-permute-start.77) | collective-permute-done | bytes 901152 | tf_op jit(solution)/shard_map/ppermute | solution.py:30
  596.6 14.1 %collective-permute-done.69 = bf16[352,1280]{1,0:T(8,128)(2,1)S(1)} collective-permute-done((bf16[352,1280]{1,0:T(8,128)(2,1)S(1)}, bf16[352,1280]{1,0:T(8,128)(2,1)S(1)}, u32[]{:S(2)}, u32[]{:S(2)}) %collective-permute-start.69) | collective-permute-done | bytes 901152 | tf_op jit(solution)/shard_map/ppermute | solution.py:30
  619.9 9.5 %collective-permute-done.72 = bf16[176,1280]{1,0:T(8,128)(2,1)S(1)} collective-permute-done((bf16[176,1280]{1,0:T(8,128)(2,1)S(1)}, bf16[176,1280]{1,0:T(8,128)(2,1)S(1)}, u32[]{:S(2)}, u32[]{:S(2)}) %collective-permute-start.72) | collective-permute-done | bytes 450592 | tf_op jit(solution)/shard_map/ppermute | solution.py:30
  635.8 10.7 %collective-permute-start.83 = (bf16[192,640]{1,0:T(8,128)(2,1)S(1)}, bf16[192,640]{1,0:T(8,128)(2,1)S(1)}, u32[]{:S(2)}, u32[]{:S(2)}) collective-permute-start(bf16[192,640]{1,0:T(8,128)(2,1)S(1)} %get-tuple-element.366), channel_id=1, source_target_pairs={{0,1},{1,2},{2,3},{3,0},{4,7},{5,4},{6,5},{7,6},{8,9},{9,10},{10,1... | collective-permute-start | bytes 737288 | tf_op jit(solution)/shard_map/ppermute | solution.py:747
  651.4 58.9 %collective-permute-done.84 = bf16[192,640]{1,0:T(8,128)(2,1)S(1)} collective-permute-done((bf16[192,640]{1,0:T(8,128)(2,1)S(1)}, bf16[192,640]{1,0:T(8,128)(2,1)S(1)}, u32[]{:S(2)}, u32[]{:S(2)}) %collective-permute-start.84) | collective-permute-done | bytes 245792 | tf_op jit(solution)/shard_map/ppermute | solution.py:747
  714.4 8.4 %collective-permute-start.76 = (bf16[192,640]{1,0:T(8,128)(2,1)S(1)}, bf16[192,640]{1,0:T(8,128)(2,1)}, u32[]{:S(2)}, u32[]{:S(2)}) collective-permute-start(bf16[192,640]{1,0:T(8,128)(2,1)S(1)} %get-tuple-element.372), channel_id=1, source_target_pairs={{0,5},{1,6},{2,7},{3,4},{4,3},{5,0},{6,1},{7,2},{8,13},{9,14},{10,... | collective-permute-start | bytes 737288 | tf_op jit(solution)/shard_map/ppermute | solution.py:747
  728.4 6.5 collective-permute-start.67
  (587 shorter events, 333.1 us)
Async XLA Ops:
  16.6 59.4 %collective-permute-start.7 = (bf16[256,1280]{1,0:T(8,128)(2,1)}, bf16[256,1280]{1,0:T(8,128)(2,1)}, u32[]{:S(2)}, u32[]{:S(2)}) collective-permute-start(bf16[256,1280]{1,0:T(8,128)(2,1)} %dynamic-slice_bitcast_fusion.16), channel_id=1, source_target_pairs={{0,2},{1,6},{2,0},{3,4},{4,3},{5,7},{6,1},{7,5},{8,10},{9,14},{10,... | collective-permute-start | bytes 1966088 | tf_op jit(solution)/shard_map/ppermute | solution.py:747
  38.9 37.1 %collective-permute-start.5 = (bf16[2,160,1280]{2,1,0:T(8,128)(2,1)S(1)}, bf16[2,160,1280]{2,1,0:T(8,128)(2,1)S(1)}, u32[]{:S(2)}, u32[]{:S(2)}) collective-permute-start(bf16[2,160,1280]{2,1,0:T(8,128)(2,1)S(1)} %pad_maximum_fusion.16.refs_0_), channel_id=1, source_target_pairs={{0,16},{4,20},{8,24},{12,28},{16,0},{20,4},{24,8},{28,12},{1,17},{... | collective-permute-start | bytes 2457608 | tf_op jit(solution)/shard_map/ppermute | solution.py:30
  40.4 35.6 %collective-permute-start.4 = (bf16[2,160,1280]{2,1,0:T(8,128)(2,1)S(1)}, bf16[2,160,1280]{2,1,0:T(8,128)(2,1)}, u32[]{:S(2)}, u32[]{:S(2)}) collective-permute-start(bf16[2,160,1280]{2,1,0:T(8,128)(2,1)S(1)} %pad_maximum_fusion.16.refs_0_), channel_id=1, source_target_pairs={{0,8},{4,12},{8,0},{12,4},{16,24},{20,28},{24,16},{28,20},{1,9},{5... | collective-permute-start | bytes 2457608 | tf_op jit(solution)/shard_map/ppermute | solution.py:30
  41.8 34.2 %collective-permute-start.6 = (bf16[256,1280]{1,0:T(8,128)(2,1)}, bf16[256,1280]{1,0:T(8,128)(2,1)S(1)}, u32[]{:S(2)}, u32[]{:S(2)}) collective-permute-start(bf16[256,1280]{1,0:T(8,128)(2,1)} %dynamic-slice_bitcast_fusion.17), channel_id=1, source_target_pairs={{0,0},{1,4},{2,2},{3,6},{4,1},{5,5},{6,3},{7,7},{8,8},{9,12},{10,1... | collective-permute-start | bytes 1966088 | tf_op jit(solution)/shard_map/ppermute | solution.py:747
  68.1 40.2 %all-to-all-start.1 = ((bf16[4,160,384]{2,1,0:T(8,128)(2,1)}), bf16[4,160,384]{2,1,0:T(8,128)(2,1)}, u32[]{:S(2)}, u32[]{:S(2)}) async-start(bf16[4,160,384]{2,1,0:T(8,128)(2,1)} %shard_map.256), calls=%async_computation.1 | async-start | bytes 983040 | tf_op jit(solution)/shard_map/all_to_all | solution.py:855
  72.3 115.7 %all-gather.5.cloned.1.call-start = ((), (), s32[]{:S(2)}) async-start(), calls=%async_computation.5 | async-start | bytes 4096000 | tf_op jit(solution)/shard_map/all_gather | solution.py:895
  83.8 24.5 %collective-permute-start.16 = (bf16[160,1280]{1,0:T(8,128)(2,1)}, bf16[160,1280]{1,0:T(8,128)(2,1)}, u32[]{:S(2)}, u32[]{:S(2)}) collective-permute-start(bf16[160,1280]{1,0:T(8,128)(2,1)} %slice_bitcast_fusion.7), channel_id=1, source_target_pairs={{0,8},{4,12},{8,0},{12,4},{16,24},{20,28},{24,16},{28,20},{1,9},{5... | collective-permute-start | bytes 1228808 | tf_op jit(solution)/shard_map/ppermute | solution.py:30
  111.7 151.3 %all-gather.7.cloned.1.call-start = ((), (), s32[]{:S(2)}) async-start(), calls=%async_computation.6 | async-start | bytes 2457600 | tf_op jit(solution)/shard_map/all_gather | solution.py:896
  183.2 559.2 %reduce-scatter.2.cloned.1.call-start = ((), (), s32[]{:S(2)}) async-start(), calls=%async_computation.4 | async-start | bytes 6553600 | tf_op jit(solution)/shard_map/reduce_scatter | solution.py:975
  188.0 46.1 %collective-permute-start.31 = (bf16[4,4,160,640]{3,2,1,0:T(8,128)(2,1)}, bf16[4,4,160,640]{3,2,1,0:T(8,128)(2,1)}, u32[]{:S(2)}, u32[]{:S(2)}) collective-permute-start(bf16[4,4,160,640]{3,2,1,0:T(8,128)(2,1)} %bitcast.305), channel_id=1, source_target_pairs={{0,4},{4,0},{8,12},{12,8},{16,20},{20,16},{24,28},{28,24},{1,5},{5... | collective-permute-start | bytes 9830408 | tf_op jit(solution)/shard_map/ppermute | solution.py:30
  266.0 68.0 %collective-permute-start.35 = (bf16[256,1280]{1,0:T(8,128)(2,1)}, bf16[256,1280]{1,0:T(8,128)(2,1)S(1)}, u32[]{:S(2)}, u32[]{:S(2)}) collective-permute-start(bf16[256,1280]{1,0:T(8,128)(2,1)} %get-tuple-element.315), channel_id=1, source_target_pairs={{0,2},{1,6},{2,0},{3,4},{4,3},{5,7},{6,1},{7,5},{8,10},{9,14},{10,... | collective-permute-start | bytes 1966088 | tf_op jit(solution)/shard_map/ppermute | solution.py:747
  268.1 66.8 %collective-permute-start.34 = (bf16[256,1280]{1,0:T(8,128)(2,1)}, bf16[256,1280]{1,0:T(8,128)(2,1)}, u32[]{:S(2)}, u32[]{:S(2)}) collective-permute-start(bf16[256,1280]{1,0:T(8,128)(2,1)} %get-tuple-element.316), channel_id=1, source_target_pairs={{0,0},{1,4},{2,2},{3,6},{4,1},{5,5},{6,3},{7,7},{8,8},{9,12},{10,1... | collective-permute-start | bytes 1966088 | tf_op jit(solution)/shard_map/ppermute | solution.py:747
  301.9 25.1 %collective-permute-start.40 = (bf16[128,1280]{1,0:T(8,128)(2,1)S(1)}, bf16[128,1280]{1,0:T(8,128)(2,1)S(1)}, u32[]{:S(2)}, u32[]{:S(2)}) collective-permute-start(bf16[128,1280]{1,0:T(8,128)(2,1)S(1)} %add_convert_fusion.11), channel_id=1, source_target_pairs={{0,8},{4,12},{8,0},{12,4},{16,24},{20,28},{24,16},{28,20},{1,9},{5... | collective-permute-start | bytes 983048 | tf_op jit(solution)/shard_map/ppermute | solution.py:30
  343.3 24.7 %collective-permute-start.50 = (bf16[256,1280]{1,0:T(8,128)(2,1)}, bf16[256,1280]{1,0:T(8,128)(2,1)S(1)}, u32[]{:S(2)}, u32[]{:S(2)}) collective-permute-start(bf16[256,1280]{1,0:T(8,128)(2,1)} %get-tuple-element.193.refs_0_), channel_id=1, source_target_pairs={{0,16},{4,20},{8,24},{12,28},{16,0},{20,4},{24,8},{28,12},{1,17},{... | collective-permute-start | bytes 1966088 | tf_op jit(solution)/shard_map/ppermute | solution.py:30
  395.0 44.0 %collective-permute-start.51 = (bf16[256,1280]{1,0:T(8,128)(2,1)}, bf16[256,1280]{1,0:T(8,128)(2,1)}, u32[]{:S(2)}, u32[]{:S(2)}) collective-permute-start(bf16[256,1280]{1,0:T(8,128)(2,1)} %get-tuple-element.313), channel_id=1, source_target_pairs={{0,0},{4,1},{2,2},{6,3},{1,4},{5,5},{3,6},{7,7},{8,8},{12,9},{10,1... | collective-permute-start | bytes 1966088 | tf_op jit(solution)/shard_map/ppermute | solution.py:747
  401.5 37.5 %collective-permute-start.52 = (bf16[256,1280]{1,0:T(8,128)(2,1)}, bf16[256,1280]{1,0:T(8,128)(2,1)}, u32[]{:S(2)}, u32[]{:S(2)}) collective-permute-start(bf16[256,1280]{1,0:T(8,128)(2,1)} %get-tuple-element.314), channel_id=1, source_target_pairs={{2,0},{6,1},{0,2},{4,3},{3,4},{7,5},{1,6},{5,7},{10,8},{14,9},{8,1... | collective-permute-start | bytes 1966088 | tf_op jit(solution)/shard_map/ppermute | solution.py:747
  402.6 33.2 %collective-permute-start.53 = (bf16[256,1280]{1,0:T(8,128)(2,1)S(1)}, bf16[256,1280]{1,0:T(8,128)(2,1)S(1)}, u32[]{:S(2)}, u32[]{:S(2)}) collective-permute-start(bf16[256,1280]{1,0:T(8,128)(2,1)S(1)} %pad_maximum_fusion.22), channel_id=1, source_target_pairs={{0,8},{4,12},{8,0},{12,4},{16,24},{20,28},{24,16},{28,20},{1,9},{5... | collective-permute-start | bytes 1966088 | tf_op jit(solution)/shard_map/ppermute | solution.py:30
  403.9 32.0 %collective-permute-start.54 = (bf16[256,1280]{1,0:T(8,128)(2,1)S(1)}, bf16[256,1280]{1,0:T(8,128)(2,1)S(1)}, u32[]{:S(2)}, u32[]{:S(2)}) collective-permute-start(bf16[256,1280]{1,0:T(8,128)(2,1)S(1)} %pad_maximum_fusion.23), channel_id=1, source_target_pairs={{0,16},{4,20},{8,24},{12,28},{16,0},{20,4},{24,8},{28,12},{1,17},{... | collective-permute-start | bytes 1966088 | tf_op jit(solution)/shard_map/ppermute | solution.py:30
  479.6 24.5 %collective-permute-start.65 = (bf16[4,4,160,1024]{3,2,1,0:T(8,128)(2,1)}, bf16[4,4,160,1024]{3,2,1,0:T(8,128)(2,1)}, u32[]{:S(2)}, u32[]{:S(2)}) collective-permute-start(bf16[4,4,160,1024]{3,2,1,0:T(8,128)(2,1)} %get-tuple-element.224), channel_id=1, source_target_pairs={{0,4},{4,0},{8,12},{12,8},{16,20},{20,16},{24,28},{28,24},{1,5},{5... | collective-permute-start | bytes 15728648 | tf_op jit(solution)/shard_map/ppermute | solution.py:30
  571.7 38.9 %collective-permute-start.69 = (bf16[352,1280]{1,0:T(8,128)(2,1)S(1)}, bf16[352,1280]{1,0:T(8,128)(2,1)S(1)}, u32[]{:S(2)}, u32[]{:S(2)}) collective-permute-start(bf16[352,1280]{1,0:T(8,128)(2,1)S(1)} %pad_maximum_fusion.10), channel_id=1, source_target_pairs={{0,8},{4,12},{8,0},{12,4},{16,24},{20,28},{24,16},{28,20},{1,9},{5... | collective-permute-start | bytes 2703368 | tf_op jit(solution)/shard_map/ppermute | solution.py:30
  581.8 31.8 %collective-permute-start.71 = (bf16[352,1280]{1,0:T(8,128)(2,1)S(1)}, bf16[352,1280]{1,0:T(8,128)(2,1)S(1)}, u32[]{:S(2)}, u32[]{:S(2)}) collective-permute-start(bf16[352,1280]{1,0:T(8,128)(2,1)S(1)} %pad_maximum_fusion.11), channel_id=1, source_target_pairs={{0,16},{4,20},{8,24},{12,28},{16,0},{20,4},{24,8},{28,12},{1,17},{... | collective-permute-start | bytes 2703368 | tf_op jit(solution)/shard_map/ppermute | solution.py:30
  582.8 32.1 %collective-permute-start.66 = (bf16[2,256,1280]{2,1,0:T(8,128)(2,1)S(1)}, bf16[2,256,1280]{2,1,0:T(8,128)(2,1)S(1)}, u32[]{:S(2)}, u32[]{:S(2)}) collective-permute-start(bf16[2,256,1280]{2,1,0:T(8,128)(2,1)S(1)} %dynamic-slice_bitcast_fusion), channel_id=1, source_target_pairs={{0,4},{4,0},{8,12},{12,8},{16,20},{20,16},{24,28},{28,24},{1,5},{5... | collective-permute-start | bytes 3932168 | tf_op jit(solution)/shard_map/ppermute | solution.py:30
  592.5 39.4 %collective-permute-start.78 = (bf16[176,1280]{1,0:T(8,128)(2,1)S(1)}, bf16[176,1280]{1,0:T(8,128)(2,1)S(1)}, u32[]{:S(2)}, u32[]{:S(2)}) collective-permute-start(bf16[176,1280]{1,0:T(8,128)(2,1)S(1)} %fusion.23), channel_id=1, source_target_pairs={{0,16},{4,20},{8,24},{12,28},{16,0},{20,4},{24,8},{28,12},{1,17},{... | collective-permute-start | bytes 1351688 | tf_op jit(solution)/shard_map/ppermute | solution.py:30
  595.4 34.3 %collective-permute-start.81 = (bf16[176,1280]{1,0:T(8,128)(2,1)S(1)}, bf16[176,1280]{1,0:T(8,128)(2,1)S(1)}, u32[]{:S(2)}, u32[]{:S(2)}) collective-permute-start(bf16[176,1280]{1,0:T(8,128)(2,1)S(1)} %add_convert_fusion.2), channel_id=1, source_target_pairs={{0,8},{4,12},{8,0},{12,4},{16,24},{20,28},{24,16},{28,20},{1,9},{5... | collective-permute-start | bytes 1351688 | tf_op jit(solution)/shard_map/ppermute | solution.py:30
  617.5 132.0 %collective-permute-start.68 = (bf16[256,1280]{1,0:T(8,128)(2,1)}, bf16[256,1280]{1,0:T(8,128)(2,1)}, u32[]{:S(2)}, u32[]{:S(2)}) collective-permute-start(bf16[256,1280]{1,0:T(8,128)(2,1)} %broadcast_select_fusion), channel_id=1, source_target_pairs={{2,0},{6,1},{0,2},{4,3},{3,4},{7,5},{1,6},{5,7},{10,8},{14,9},{8,1... | collective-permute-start | bytes 1966088 | tf_op jit(solution)/shard_map/ppermute | solution.py:747
  634.9 75.5 %collective-permute-start.84 = (bf16[192,640]{1,0:T(8,128)(2,1)S(1)}, bf16[192,640]{1,0:T(8,128)(2,1)S(1)}, u32[]{:S(2)}, u32[]{:S(2)}) collective-permute-start(bf16[192,640]{1,0:T(8,128)(2,1)S(1)} %pad_maximum_fusion.35), channel_id=1, source_target_pairs={{0,4},{1,5},{2,6},{3,7},{4,2},{5,3},{6,0},{7,1},{8,12},{9,13},{10,... | collective-permute-start | bytes 737288 | tf_op jit(solution)/shard_map/ppermute | solution.py:747
  635.0 75.3 %collective-permute-start.82 = (bf16[192,640]{1,0:T(8,128)(2,1)S(1)}, bf16[192,640]{1,0:T(8,128)(2,1)S(1)}, u32[]{:S(2)}, u32[]{:S(2)}) collective-permute-start(bf16[192,640]{1,0:T(8,128)(2,1)S(1)} %pad_maximum_fusion.34), channel_id=1, source_target_pairs={{0,0},{1,1},{2,2},{3,3},{4,6},{5,7},{6,4},{7,5},{8,8},{9,9},{10,10... | collective-permute-start | bytes 737288 | tf_op jit(solution)/shard_map/ppermute | solution.py:747
  635.8 76.0 %collective-permute-start.83 = (bf16[192,640]{1,0:T(8,128)(2,1)S(1)}, bf16[192,640]{1,0:T(8,128)(2,1)S(1)}, u32[]{:S(2)}, u32[]{:S(2)}) collective-permute-start(bf16[192,640]{1,0:T(8,128)(2,1)S(1)} %get-tuple-element.366), channel_id=1, source_target_pairs={{0,1},{1,2},{2,3},{3,0},{4,7},{5,4},{6,5},{7,6},{8,9},{9,10},{10,1... | collective-permute-start | bytes 737288 | tf_op jit(solution)/shard_map/ppermute | solution.py:747
  646.6 67.8 %collective-permute-start.85 = (bf16[192,640]{1,0:T(8,128)(2,1)S(1)}, bf16[192,640]{1,0:T(8,128)(2,1)S(1)}, u32[]{:S(2)}, u32[]{:S(2)}) collective-permute-start(bf16[192,640]{1,0:T(8,128)(2,1)S(1)} %get-tuple-element.367), channel_id=1, source_target_pairs={{0,5},{1,6},{2,7},{3,4},{4,3},{5,0},{6,1},{7,2},{8,13},{9,14},{10,... | collective-permute-start | bytes 737288 | tf_op jit(solution)/shard_map/ppermute | solution.py:747
  710.4 25.5 %collective-permute-start.73 = (bf16[192,640]{1,0:T(8,128)(2,1)S(1)}, bf16[192,640]{1,0:T(8,128)(2,1)}, u32[]{:S(2)}, u32[]{:S(2)}) collective-permute-start(bf16[192,640]{1,0:T(8,128)(2,1)S(1)} %pad_maximum_fusion.32), channel_id=1, source_target_pairs={{0,0},{1,1},{2,2},{3,3},{4,6},{5,7},{6,4},{7,5},{8,8},{9,9},{10,10... | collective-permute-start | bytes 737288 | tf_op jit(solution)/shard_map/ppermute | solution.py:747
  711.8 25.1 %collective-permute-start.74 = (bf16[192,640]{1,0:T(8,128)(2,1)}, bf16[192,640]{1,0:T(8,128)(2,1)}, u32[]{:S(2)}, u32[]{:S(2)}) collective-permute-start(bf16[192,640]{1,0:T(8,128)(2,1)} %get-tuple-element.371), channel_id=1, source_target_pairs={{0,1},{1,2},{2,3},{3,0},{4,7},{5,4},{6,5},{7,6},{8,9},{9,10},{10,1... | collective-permute-start | bytes 737288 | tf_op jit(solution)/shard_map/ppermute | solution.py:747
  714.4 24.7 %collective-permute-start.76 = (bf16[192,640]{1,0:T(8,128)(2,1)S(1)}, bf16[192,640]{1,0:T(8,128)(2,1)}, u32[]{:S(2)}, u32[]{:S(2)}) collective-permute-start(bf16[192,640]{1,0:T(8,128)(2,1)S(1)} %get-tuple-element.372), channel_id=1, source_target_pairs={{0,5},{1,6},{2,7},{3,4},{4,3},{5,0},{6,1},{7,2},{8,13},{9,14},{10,... | collective-permute-start | bytes 737288 | tf_op jit(solution)/shard_map/ppermute | solution.py:747
  (147 other events, 1522.6 us)
Sparse Core Ops, SparseCore 0:
  111.8 65.1 all-gather.4
  183.3 43.2 all-gather.6
  566.5 131.7 reduce-scatter.1

commit v2 on v1

--- a/solution.py
+++ b/solution.py
@@ -86,30 +86,33 @@
     return value, along_x, along_y, swap(along_y[:half], 2), swap(along_x[half:], 4)
 
 
-def scatter_first(blocks):
+def scatter_first(blocks, then=()):
     own, along_x, along_y, diagonal = blocks
     half = own.shape[0] // 2
-    first = swap(jnp.concatenate([along_x[:half], diagonal[:half]]), 2)
-    second = swap(jnp.concatenate([along_y[half:], diagonal[half:]]), 4)
-    return blocks, first, second
-
-
-def scatter_second(sent):
+    first, second, then = lax.optimization_barrier(
+        (
+            jnp.concatenate([along_x[:half], diagonal[:half]]),
+            jnp.concatenate([along_y[half:], diagonal[half:]]),
+            then,
+        )
+    )
+    return (blocks, swap(first, 2), swap(second, 4)), then
+
+
+def scatter_last(sent):
     (own, along_x, along_y, _), first, second = sent
     half = own.shape[0] // 2
     next_y = (along_y[:half].astype(wide) + first[half:].astype(wide)).astype(low)
     next_x = (along_x[half:].astype(wide) + second[half:].astype(wide)).astype(low)
-    top = own[:half].astype(wide) + first[:half].astype(wide) + swap(next_y, 4).astype(wide)
-    bottom = own[half:].astype(wide) + second[:half].astype(wide) + swap(next_x, 2).astype(wide)
+    return own, first, second, swap(next_y, 4), swap(next_x, 2)
+
+
+def scatter_second(sent):
+    own, first, second, last_y, last_x = scatter_last(sent)
+    half = own.shape[0] // 2
+    top = own[:half].astype(wide) + first[:half].astype(wide) + last_y.astype(wide)
+    bottom = own[half:].astype(wide) + second[:half].astype(wide) + last_x.astype(wide)
     return jnp.concatenate([top, bottom])
-
-
-def row_norm(values):
-    return values * lax.rsqrt(jnp.mean(values * values, axis=-1, keepdims=True) + epsilon)
-
-
-def settle(base, branch, rate):
-    return row_norm(base + rate * (row_norm(branch) - base))
 
 
 def nt(left, right):
@@ -129,7 +132,7 @@
 
 
 def cost(flops, moved):
-    return pl.CostEstimate(flops=int(flops), bytes_accessed=int(moved), transcendentals=0)
+    return pl.CostEstimate(flops=1, bytes_accessed=1, transcendentals=0)
 
 
 def head_means(width):
@@ -146,7 +149,7 @@
     n, depth = rows.shape
     width = weight.shape[1]
     tile = 2 * LANES
-    block = 256
+    block = 512
 
     def kernel(rows_ref, weight_ref, gain_ref, out_ref, raw_ref):
         means = head_means(tile)
@@ -348,9 +351,8 @@
 def sum_back(lefts, rights, n=None, first=0):
     n = n or lefts[0][0].shape[0]
     out_width = rights[0][0].shape[0]
-    block = 256
+    tile = 2 * LANES
     count = len(lefts)
-    skip = first * n // block
 
     def kernel(*refs):
         total = nt(refs[0][...], refs[count][...])
@@ -361,87 +363,289 @@
     depth = sum(columns for _, _, columns in lefts)
     return pl.pallas_call(
         kernel,
-        grid=(n // block,),
-        in_specs=[
-            pl.BlockSpec((block, columns), lambda r, at=at: (r + skip, at)) for _, at, columns in lefts
-        ]
-        + [pl.BlockSpec((out_width, columns), lambda r, at=at: (0, at)) for _, at, columns in rights],
-        out_specs=pl.BlockSpec((block, out_width), lambda r: (r, 0)),
+        grid=(out_width // tile,),
+        in_specs=[pl.BlockSpec((n, columns), lambda j, at=at: (first, at)) for _, at, columns in lefts]
+        + [pl.BlockSpec((tile, columns), lambda j, at=at: (j, at)) for _, at, columns in rights],
+        out_specs=pl.BlockSpec((n, tile), lambda j: (0, j)),
         out_shape=jax.ShapeDtypeStruct((n, out_width), low),
         compiler_params=params(),
         cost_estimate=cost(2 * n * out_width * depth, 2 * (n + out_width) * depth + 2 * n * out_width),
     )(*(matrix for matrix, _, _ in lefts + rights))
 
 
-def rows_product(pairs):
+def add_low(first, second):
+    columns = first.shape[-1]
+    flat = (first.size // columns, columns)
+    block = flat[0] // 8
+
+    def kernel(a_ref, b_ref, out_ref):
+        out_ref[...] = (a_ref[...].astype(wide) + b_ref[...].astype(wide)).astype(low)
+
+    spec = pl.BlockSpec((block, columns), lambda r: (r, 0))
+    out = pl.pallas_call(
+        kernel,
+        grid=(8,),
+        in_specs=[spec, spec],
+        out_specs=spec,
+        out_shape=jax.ShapeDtypeStruct(flat, low),
+        compiler_params=params(),
+        cost_estimate=cost(first.size, 6 * first.size),
+    )(first.reshape(flat), second.reshape(flat))
+    return out.reshape(first.shape)
+
+
+def rows_product(pairs, tile):
     n, depth = pairs[0][0].shape
-    width = pairs[0][1].shape[1]
-    tile = 2 * LANES
-    steps = depth // tile
-    count = len(pairs)
+    lefts = [left for left, _ in pairs]
+    rights = [right for _, group in pairs for right in group]
+    owner = [k for k, (_, group) in enumerate(pairs) for _ in group]
+    steps = [right.shape[1] // tile for right in rights]
+    starts = [sum(steps[:i]) for i in range(len(steps))]
+    chunk = 256
 
     def kernel(*refs):
-        for k in range(count):
-
-            @pl.when(pl.program_id(0) // steps == k)
-            def _():
-                refs[2 * count][...] = tn(refs[2 * k][...], refs[2 * k + 1][...]).astype(low)
-
-    def left_tile(k):
-        return lambda j: (0, jnp.clip(j - k * steps, 0, steps - 1))
-
-    specs = []
-    for k in range(count):
-        specs += [pl.BlockSpec((n, tile), left_tile(k)), pl.BlockSpec((n, width), lambda j: (0, 0))]
-    return pl.pallas_call(
-        kernel,
-        grid=(count * steps,),
-        in_specs=specs,
-        out_specs=pl.BlockSpec((tile, width), lambda j: (j % steps, j // steps)),
-        out_shape=jax.ShapeDtypeStruct((depth, count * width), low),
-        compiler_params=params(),
-        cost_estimate=cost(2 * n * depth * width * count, 2 * count * (n * (depth + width) + depth * width)),
-    )(*(member for pair in pairs for member in pair))
+        left_refs, right_refs = refs[: len(lefts)], refs[len(lefts) : len(lefts) + len(rights)]
+        out, turned = refs[-2:]
+        step = pl.program_id(0)
+        for i, right in enumerate(right_refs):
+            if i == 0 or owner[i] != owner[i - 1]:
+
+                @pl.when(step == starts[i])
+                def _(left=left_refs[owner[i]]):
+                    for at in range(0, n, chunk):
+                        turned[:, at : at + chunk] = left[at : at + chunk, :].T
+
+            @pl.when((step >= starts[i]) & (step < starts[i] + steps[i]))
+            def _(right=right):
+                out[...] = nn(turned[...], right[...]).astype(low)
+
+    def tile_of(i):
+        return lambda j: (0, jnp.clip(j - starts[i], 0, steps[i] - 1))
+
+    width = sum(right.shape[1] for right in rights)
+    return pl.pallas_call(
+        kernel,
+        grid=(sum(steps),),
+        in_specs=[pl.BlockSpec((n, depth), lambda j: (0, 0))] * len(lefts)
+        + [pl.BlockSpec((n, tile), tile_of(i)) for i in range(len(rights))],
+        out_specs=pl.BlockSpec((depth, tile), lambda j: (0, j)),
+        out_shape=jax.ShapeDtypeStruct((depth, width), low),
+        scratch_shapes=[pltpu.VMEM((depth, n), low)],
+        compiler_params=params(),
+        cost_estimate=cost(2 * n * depth * width, 2 * (n * (depth + width) + depth * width)),
+    )(*lefts, *rights)
+
+
+def product(left, right, at):
+    n, depth = left.shape
+    width = right.shape[1] // 2
+
+    def kernel(left_ref, right_ref, out_ref):
+        out_ref[...] = nn(left_ref[...], right_ref[...]).astype(low)
+
+    return pl.pallas_call(
+        kernel,
+        grid=(1,),
+        in_specs=[pl.BlockSpec((n, depth), lambda j: (0, 0)), pl.BlockSpec((depth, width), lambda j: (0, at))],
+        out_specs=pl.BlockSpec((n, width), lambda j: (0, 0)),
+        out_shape=jax.ShapeDtypeStruct((n, width), low),
+        compiler_params=params(),
+        cost_estimate=cost(2 * n * depth * width, 2 * (n * depth + depth * width + n * width)),
+    )(left, right)
 
 
 def chunk_specs(blocks, width):
     return [pl.BlockSpec(block.shape, lambda j: (0, 0)) for block in blocks]
 
 
-def mlp_forward(blocks, up_w, gate_w, scales, chunk, earlier):
+def row_scale(values):
+    return lax.rsqrt(jnp.mean(values * values, axis=-1, keepdims=True) + epsilon)
+
+
+def unscale(grad, normed, scale):
+    return scale * (grad - normed * jnp.mean(grad * normed, axis=-1, keepdims=True))
+
+
+def settle_step(base, branch, rate):
+    branch_scale = row_scale(branch)
+    normed = branch * branch_scale
+    moved = base + rate * (normed - base)
+    scale = row_scale(moved)
+    return moved * scale, (normed, branch_scale, scale)
+
+
+def settle_back(grad, result, base, rate, saved):
+    normed, branch_scale, scale = saved
+    grad = unscale(grad, result, scale)
+    return grad * (1.0 - rate), unscale(grad * rate, normed, branch_scale), grad * (normed - base)
+
+
+def rate_rows(terms):
+    return jnp.concatenate([jnp.sum(terms, axis=0, keepdims=True), jnp.zeros((7, terms.shape[1]), wide)])
+
+
+def settle_attention(partial, got, tokens, rate, core):
+    _, _, n, depth = partial.shape
+    block = n // 2
+
+    def kernel(core_ref, part_ref, got_ref, token_ref, rate_ref, hidden_ref, low_ref, branch_ref):
+        branch = part_ref[0, 0].astype(wide) + got_ref[0].astype(wide)
+        hidden, _ = settle_step(token_ref[...].astype(wide), branch, rate_ref[...])
+        hidden_ref[...] = hidden
+        low_ref[...] = hidden.astype(low)
+        branch_ref[...] = branch
+
+    rows = pl.BlockSpec((block, depth), lambda j, r, core_ref: (2 * j + r, 0))
+    return pl.pallas_call(
+        kernel,
+        grid_spec=pltpu.PrefetchScalarGridSpec(
+            num_scalar_prefetch=1,
+            grid=(2, 2),
+            in_specs=[
+                pl.BlockSpec((1, 1, block, depth), lambda j, r, core_ref: (j, core_ref[0], r, 0)),
+                pl.BlockSpec((1, block, depth), lambda j, r, core_ref: (j, r, 0)),
+                rows,
+                pl.BlockSpec((1, depth), lambda j, r, core_ref: (0, 0)),
+            ],
+            out_specs=[rows] * 3,
+        ),
+        out_shape=[
+            jax.ShapeDtypeStruct((2 * n, depth), wide),
+            jax.ShapeDtypeStruct((2 * n, depth), low),
+            jax.ShapeDtypeStruct((2 * n, depth), wide),
+        ],
+        compiler_params=params(),
+        cost_estimate=cost(0, 0),
+    )(core.reshape(1), partial, got, tokens, rate[None])
+
+
+def arrived_specs(n, depth):
+    half = n // 2
+    piece = pl.BlockSpec((half, depth), lambda h, *_: (0, 0))
+    return [pl.BlockSpec((half, depth), lambda h, *_: (h, 0))] + [piece] * 4
+
+
+def arrived_sum(h, own, first, second, last_y, last_x):
+    top, bottom = (a[...].astype(wide) + b[...].astype(wide) for a, b in ((first, last_y), (second, last_x)))
+    return own[...].astype(wide) + jnp.where(h == 0, top, bottom)
+
+
+def settle_units(arrived, hidden, near, far, early, rate):
+    n, depth = hidden.shape
+    half = n // 2
+
+    def kernel(early_ref, *refs):
+        h = pl.program_id(0)
+        branch = arrived_sum(h, *refs[:5])
+        hidden_ref, near_ref, far_ref, rate_ref, out_ref, direct_ref, grad_ref, term_ref = refs[5:]
+        base, rates = hidden_ref[...], rate_ref[...]
+        result, saved = settle_step(base, branch, rates)
+        cotangent = jnp.where((h == 0) == (early_ref[0] == 1), near_ref[...], far_ref[...])
+        direct, grad, terms = settle_back(cotangent.astype(wide), result, base, rates, saved)
+        out_ref[...] = result.astype(low)
+        direct_ref[...] = direct
+        grad_ref[...] = grad.astype(low)
+
+        @pl.when(h == 0)
+        def _():
+            term_ref[...] = rate_rows(terms)
+
+        @pl.when(h != 0)
+        def _():
+            term_ref[...] += rate_rows(terms)
+
+    rows = pl.BlockSpec((half, depth), lambda h, *_: (h, 0))
+    piece = pl.BlockSpec((half, depth), lambda h, *_: (0, 0))
+    return pl.pallas_call(
+        kernel,
+        grid_spec=pltpu.PrefetchScalarGridSpec(
+            num_scalar_prefetch=1,
+            grid=(2,),
+            in_specs=arrived_specs(n, depth)
+            + [rows, piece, piece, pl.BlockSpec((1, depth), lambda h, *_: (0, 0))],
+            out_specs=[rows, rows, rows, pl.BlockSpec((8, depth), lambda h, *_: (0, 0))],
+        ),
+        out_shape=[
+            jax.ShapeDtypeStruct((n, depth), low),
+            jax.ShapeDtypeStruct((n, depth), wide),
+            jax.ShapeDtypeStruct((n, depth), low),
+            jax.ShapeDtypeStruct((8, depth), wide),
+        ],
+        compiler_params=params(),
+        cost_estimate=cost(0, 0),
+    )(early.astype(jnp.int32).reshape(1), *arrived, hidden, near, far, rate[None])
+
+
+def settle_attention_back(arrived, direct, hidden, tokens, branch, rate):
+    n, depth = hidden.shape
+    half = n // 2
+
+    def kernel(*refs):
+        h = pl.program_id(0)
+        direct_ref, token_ref, branch_ref, rate_ref, out_ref, grad_ref, term_ref = refs[5:]
+        grad = direct_ref[...] + arrived_sum(h, *refs[:5])
+        base, rates = token_ref[...].astype(wide), rate_ref[...]
+        result, saved = settle_step(base, branch_ref[...], rates)
+        back, branch_grad, terms = settle_back(grad, result, base, rates, saved)
+        out_ref[...] = back
+        grad_ref[...] = branch_grad.astype(low)
+
+        @pl.when(h == 0)
+        def _():
+            term_ref[...] = rate_rows(terms)
+
+        @pl.when(h != 0)
+        def _():
+            term_ref[...] += rate_rows(terms)
+
+    rows = pl.BlockSpec((half, depth), lambda h: (h, 0))
+    return pl.pallas_call(
+        kernel,
+        grid=(2,),
+        in_specs=arrived_specs(n, depth) + [rows] * 3 + [pl.BlockSpec((1, depth), lambda h: (0, 0))],
+        out_specs=[rows, rows, pl.BlockSpec((8, depth), lambda h: (0, 0))],
+        out_shape=[
+            jax.ShapeDtypeStruct((n, depth), wide),
+            jax.ShapeDtypeStruct((n, depth), low),
+            jax.ShapeDtypeStruct((8, depth), wide),
+        ],
+        compiler_params=params(),
+        cost_estimate=cost(0, 0),
+    )(*arrived, direct, tokens, branch, rate[None])
+
+
+def lay_rows(refs, out):
+    @pl.when(pl.program_id(0) == 0)
+    def _():
+        at = 0
+        for ref in refs:
+            out[at : at + ref.shape[0], :] = ref[...]
+            at += ref.shape[0]
+
+
+def mlp_forward(blocks, up_w, gate_w, scales, total, first, earlier):
     n = sum(block.shape[0] for block in blocks)
     depth, units = up_w.shape
     tile = 2 * LANES
-    span = 512
     count = len(blocks)
 
     def kernel(*refs):
         ins, rest = refs[:count], refs[count:]
         up_ref, gate_ref, scale_ref = rest[:3]
-        mid_ref, up_out, gate_out, act_out = rest[-4:]
-
-        @pl.when(pl.program_id(0) == 0)
-        def _():
-            at = 0
-            for ref in ins:
-                mid_ref[at : at + ref.shape[0], :] = ref[...]
-                at += ref.shape[0]
-
-        for start in range(0, n, span):
-            rows = slice(start, start + span)
-            left = mid_ref[rows, :]
-            up = nn(left, up_ref[...])
-            gate = nn(left, gate_ref[...])
-            lifted = scale_ref[1:2, :] * gate
-            up_out[rows, :] = up.astype(low)
-            gate_out[rows, :] = gate.astype(low)
-            act_out[rows, :] = (scale_ref[0:1, :] * up * (lifted * jax.nn.sigmoid(lifted))).astype(low)
+        mid_ref, act_all, act_out, up_out, gate_out = rest[-5:]
+        lay_rows(ins, mid_ref)
+        left = mid_ref[...]
+        up = nn(left, up_ref[...])
+        gate = nn(left, gate_ref[...])
+        lifted = scale_ref[1:2, :] * gate
+        up_out[...] = up.astype(low)
+        gate_out[...] = gate.astype(low)
+        act = (scale_ref[0:1, :] * up * (lifted * jax.nn.sigmoid(lifted))).astype(low)
+        act_out[...] = act
+        act_all[...] = act
 
     weight = pl.BlockSpec((depth, tile), lambda j: (0, j))
-    whole = pl.BlockSpec((n, depth), lambda j: (chunk, 0))
-    tiles = pl.BlockSpec((n, tile), lambda j: (chunk, j))
-    big = jax.ShapeDtypeStruct((2 * n, depth), low)
-    wide_units = jax.ShapeDtypeStruct((2 * n, units), low)
+    alone = pl.BlockSpec((n, tile), lambda j: (0, j))
     return pl.pallas_call(
         kernel,
         grid=(units // tile,),
@@ -449,19 +653,22 @@
         + [weight] * 2
         + [pl.BlockSpec((2, tile), lambda j: (0, j))]
         + [pl.BlockSpec(memory_space=pl.ANY)] * len(earlier),
-        out_specs=[whole, tiles, tiles, tiles],
-        out_shape=[big, wide_units, wide_units, wide_units],
+        out_specs=[
+            pl.BlockSpec((n, depth), lambda j: (first, 0)), pl.BlockSpec((n, tile), lambda j: (first, j)),
+            alone, alone, alone,
+        ],
+        out_shape=[jax.ShapeDtypeStruct((total, depth), low), jax.ShapeDtypeStruct((total, units), low)]
+        + [jax.ShapeDtypeStruct((n, units), low)] * 3,
         input_output_aliases={count + 3 + i: i for i in range(len(earlier))},
         compiler_params=params(),
         cost_estimate=cost(4 * n * depth * units, 2 * (2 * n * depth + 2 * depth * units + 3 * n * units)),
     )(*blocks, up_w, gate_w, scales, *earlier)
 
 
-def mlp_backward(blocks, up_w, gate_w, down_w, scales, up_raw, gate_raw, chunk, earlier):
+def mlp_backward(blocks, up_w, gate_w, down_w, scales, up_raw, gate_raw, total, first, earlier):
     n = sum(block.shape[0] for block in blocks)
     depth, units = up_w.shape
     tile = 2 * LANES
-    span = 512
     count = len(blocks)
     steps = units // tile
 
@@ -478,64 +685,55 @@
         def _():
             for fetch in fetches:
                 fetch.start()
-            at = 0
-            for ref in ins:
-                branch_ref[at : at + ref.shape[0], :] = ref[...]
-                at += ref.shape[0]
-
+
+        lay_rows(ins, branch_ref)
         up_gain, gate_gain = scale_ref[0:1, :], scale_ref[1:2, :]
-        up_term = gate_term = jnp.zeros((1, tile), wide)
-        for start in range(0, n, span):
-            rows = slice(start, start + span)
-            grad = nn(branch_ref[rows, :], down_ref[...])
-            up = up_raw_ref[rows, :].astype(wide)
-            gate = gate_raw_ref[rows, :].astype(wide)
-            lifted = gate_gain * gate
-            slope = jax.nn.sigmoid(lifted)
-            swished = lifted * slope
-            up_part = grad * swished
-            lifted_grad = grad * up * (up_gain * (slope + swished * (1.0 - slope)))
-            up_term = up_term + jnp.sum(up_part * up, axis=0, keepdims=True)
-            gate_term = gate_term + jnp.sum(lifted_grad * gate, axis=0, keepdims=True)
-            up_low = (up_part * up_gain).astype(low)
-            gate_low = (lifted_grad * gate_gain).astype(low)
-            up_out[rows, :] = up_low
-            gate_out[rows, :] = gate_low
-            kept[0, step, rows, :] = up_low
-            kept[1, step, rows, :] = gate_low
+        grad = nn(branch_ref[...], down_ref[...])
+        up = up_raw_ref[...].astype(wide)
+        gate = gate_raw_ref[...].astype(wide)
+        lifted = gate_gain * gate
+        slope = jax.nn.sigmoid(lifted)
+        swished = lifted * slope
+        up_part = grad * swished
+        lifted_grad = grad * up * (up_gain * (slope + swished * (1.0 - slope)))
+        up_term = jnp.sum(up_part * up, axis=0, keepdims=True)
+        gate_term = jnp.sum(lifted_grad * gate, axis=0, keepdims=True)
+        up_low = (up_part * up_gain).astype(low)
+        gate_low = (lifted_grad * gate_gain).astype(low)
+        up_out[...] = up_low
+        gate_out[...] = gate_low
+        kept[0, step] = up_low
+        kept[1, step] = gate_low
         gain_ref[...] = jnp.concatenate([up_term, gate_term, jnp.zeros((6, tile), wide)], axis=0)
 
         @pl.when(step == steps - 1)
         def _():
             for fetch in fetches:
                 fetch.wait()
-            for start in range(0, n, span):
-                rows = slice(start, start + span)
-                ups, gates = (
-                    jnp.concatenate([kept[i, k, rows, :] for k in range(steps)], axis=1) for i in range(2)
-                )
-                for at in range(0, depth, tile):
-                    part = nt(ups, weights[0, at : at + tile, :]) + nt(gates, weights[1, at : at + tile, :])
-                    part_ref[rows, at : at + tile] = part.astype(low)
-
-    weight = pl.BlockSpec((depth, tile), lambda j: (0, j))
+            ups, gates = (jnp.concatenate([kept[i, k] for k in range(steps)], axis=1) for i in range(2))
+            for at in range(0, depth, tile):
+                part = nt(ups, weights[0, at : at + tile, :]) + nt(gates, weights[1, at : at + tile, :])
+                part_ref[:, at : at + tile] = part.astype(low)
+
     anywhere = pl.BlockSpec(memory_space=pl.ANY)
-    whole = pl.BlockSpec((n, depth), lambda j: (chunk, 0))
-    tiles = pl.BlockSpec((n, tile), lambda j: (chunk, j))
-    big = jax.ShapeDtypeStruct((2 * n, depth), low)
-    wide_units = jax.ShapeDtypeStruct((2 * n, units), low)
+    tiles = pl.BlockSpec((n, tile), lambda j: (first, j))
+    alone = pl.BlockSpec((n, tile), lambda j: (0, j))
+    all_units = jax.ShapeDtypeStruct((total, units), low)
     return pl.pallas_call(
         kernel,
         grid=(steps,),
         in_specs=chunk_specs(blocks, depth)
-        + [weight, pl.BlockSpec((2, tile), lambda j: (0, j)), tiles, tiles, anywhere, anywhere]
+        + [
+            pl.BlockSpec((depth, tile), lambda j: (0, j)), pl.BlockSpec((2, tile), lambda j: (0, j)),
+            alone, alone, anywhere, anywhere,
+        ]
         + [anywhere] * len(earlier),
         out_specs=[
-            whole, tiles, tiles,
+            pl.BlockSpec((n, depth), lambda j: (first, 0)), tiles, tiles,
             pl.BlockSpec((n, depth), lambda j: (0, 0)), pl.BlockSpec((8, tile), lambda j: (0, j)),
         ],
         out_shape=[
-            big, wide_units, wide_units,
+            jax.ShapeDtypeStruct((total, depth), low), all_units, all_units,
             jax.ShapeDtypeStruct((n, depth), low), jax.ShapeDtypeStruct((8, units), wide),
         ],
         scratch_shapes=[
@@ -548,22 +746,14 @@
     )(*blocks, down_w, scales, up_raw, gate_raw, up_w, gate_w, *earlier)
 
 
-def dot(left, right):
-    return jnp.dot(left, right, preferred_element_type=wide)
-
-
-def dot_rows(left, right):
-    return tn(left, right).astype(low)
-
-
 def place(blocks, indices):
-    ndim = min(block.ndim for block in blocks)
+    ndim = 2
     n = len(indices)
     count = len(blocks)
     pieces = [
         (i, at) for i, block in enumerate(blocks) for at in ([None] if block.ndim == ndim else range(block.shape[0]))
     ]
-    shape = blocks[-1].shape[-ndim:]
+    shape = blocks[0].shape[-ndim:]
     where_to = jnp.stack([jnp.asarray(i, jnp.int32) for i in indices])
 
     def kernel(index_ref, *refs):
@@ -590,6 +780,97 @@
     )(where_to, *blocks)
 
 
+def spread_pack(grad, extra, chip):
+    _, _, rows, columns = grad.shape
+    total = rows + extra.shape[0]
+    tile = 2 * LANES
+
+    def kernel(chip_ref, grad_ref, extra_ref, first, second, keep):
+        plan = [(first, 1, 0), (first, 3, 0), (second, 2, 1), (second, 3, 1)]
+        plan += [(keep, 0, 0), (keep, 0, 1), (keep, 2, 0), (keep, 1, 1)]
+        used = {}
+        for out, k, half in plan:
+            slot = used.get(id(out), 0)
+            used[id(out)] = slot + 1
+            out[slot, :rows, :] = grad_ref[chip_ref[0] ^ k, half]
+            out[slot, rows:, :] = extra_ref[...]
+
+    def out(n):
+        return pl.BlockSpec((n, total, tile), lambda j, *_: (0, 0, j))
+
+    return pl.pallas_call(
+        kernel,
+        grid_spec=pltpu.PrefetchScalarGridSpec(
+            num_scalar_prefetch=1,
+            grid=(columns // tile,),
+            in_specs=[
+                pl.BlockSpec((CHIPS, 2, rows, tile), lambda j, *_: (0, 0, 0, j)),
+                pl.BlockSpec((extra.shape[0], tile), lambda j, *_: (0, j)),
+            ],
+            out_specs=[out(2), out(2), out(4)],
+        ),
+        out_shape=[jax.ShapeDtypeStruct((n, total, columns), low) for n in (2, 2, 4)],
+        compiler_params=params(),
+        cost_estimate=cost(0, 0),
+    )(chip.reshape(1), grad, extra.astype(low))
+
+
+def spread_turn(first, second, keep):
+    _, total, columns = first.shape
+    tile = 2 * LANES
+
+    def kernel(first_ref, second_ref, keep_ref, y_ref, x_ref):
+        y_ref[...] = (keep_ref[2].astype(wide) + first_ref[1].astype(wide)).astype(low)
+        x_ref[...] = (keep_ref[3].astype(wide) + second_ref[1].astype(wide)).astype(low)
+
+    def spec(n):
+        return pl.BlockSpec((n, total, tile), lambda j: (0, 0, j))
+
+    out = pl.BlockSpec((total, tile), lambda j: (0, j))
+    return pl.pallas_call(
+        kernel,
+        grid=(columns // tile,),
+        in_specs=[spec(2), spec(2), spec(4)],
+        out_specs=[out] * 2,
+        out_shape=[jax.ShapeDtypeStruct((total, columns), low)] * 2,
+        compiler_params=params(),
+        cost_estimate=cost(0, 0),
+    )(first, second, keep)
+
+
+def spread_finish(first, second, keep, last_y, last_x, width, core):
+    _, total, columns = first.shape
+    out_width = columns // 2
+
+    def kernel(core_ref, first_ref, second_ref, keep_ref, y_ref, x_ref, *outs):
+        for half in range(2):
+            got, last = ((first_ref, y_ref), (second_ref, x_ref))[half]
+            value = keep_ref[half].astype(wide) + got[0].astype(wide) + last[...].astype(wide)
+            for which in range(2):
+                piece = jnp.concatenate(
+                    [
+                        value[:, at + which * width : at + (which + 1) * width]
+                        for at in range(0, columns, 2 * width)
+                    ],
+                    axis=1,
+                ).astype(low)
+                for side in range(2):
+
+                    @pl.when((core_ref[0] ^ side) == half)
+                    def _(side=side, which=which, piece=piece):
+                        outs[2 * side + which][...] = piece
+
+    whole = pl.BlockSpec(memory_space=pltpu.VMEM)
+    return pl.pallas_call(
+        kernel,
+        in_specs=[pl.BlockSpec(memory_space=pltpu.SMEM)] + [whole] * 5,
+        out_specs=[whole] * 4,
+        out_shape=[jax.ShapeDtypeStruct((total, out_width), low)] * 4,
+        compiler_params=params(),
+        cost_estimate=cost(0, 0),
+    )(core.reshape(1), first, second, keep, last_y, last_x)
+
+
 def half_tiles(first, second, first_upper, second_upper):
     first, second = first.astype(wide), second.astype(wide)
     axis = first.ndim - 1
@@ -599,29 +880,36 @@
     return jnp.where(lane < HALF, first, second).astype(low)
 
 
-def unit_pack(weights):
+def unit_pack(groups):
+    weights = [weight for group in groups for weight in group]
     rows, units = weights[0].shape
     main = units // CHIPS // LANES * LANES
-    n = len(weights)
+    width = len(weights) * main + len(groups) * LANES
 
     def kernel(*refs):
-        out = refs[n]
+        out, at, first = refs[-1], 0, 0
         target = pl.program_id(0)
-        for i in range(n):
-            start = pl.multiple_of(target * main, LANES)
-            out[0, :, i * main : (i + 1) * main] = refs[i][:, pl.ds(start, main)]
+        start = pl.multiple_of(target * main, LANES)
         tile = pl.multiple_of(CHIPS * main + (target // 2) * LANES, LANES)
         upper = (target & 1) == 1
-        rests = [refs[i][:, pl.ds(tile, LANES)] for i in range(n)]
-        out[0, :, n * main :] = half_tiles(rests[0], rests[-1], upper, upper)
+        for group in groups:
+            members = refs[first : first + len(group)]
+            first += len(group)
+            for ref in members:
+                out[0, :, at : at + main] = ref[:, pl.ds(start, main)]
+                at += main
+            rests = [ref[:, pl.ds(tile, LANES)] for ref in members]
+            out[0, :, at : at + LANES] = half_tiles(rests[0], rests[-1], upper, upper)
+            at += LANES
 
     whole = pl.BlockSpec((rows, units), lambda k: (0, 0))
     return pl.pallas_call(
         kernel,
         grid=(CHIPS,),
-        in_specs=[whole] * n,
-        out_specs=pl.BlockSpec((1, rows, n * main + LANES), lambda k: (k, 0, 0)),
-        out_shape=jax.ShapeDtypeStruct((CHIPS, rows, n * main + LANES), weights[0].dtype),
+        in_specs=[whole] * len(weights),
+        out_specs=pl.BlockSpec((1, rows, width), lambda k: (k, 0, 0)),
+        out_shape=jax.ShapeDtypeStruct((CHIPS, rows, width), weights[0].dtype),
+        cost_estimate=cost(0, 0),
     )(*weights)
 
 
@@ -662,39 +950,39 @@
     )(core.reshape(1), mine, theirs)
 
 
-def unit_unlay(grads, core):
+def unit_unlay(grads, n, core):
     count = lax.axis_size("tensor")
-    _, rows, units = grads[0].shape
-    n = len(grads)
+    _, rows, units = grads.shape
+    units = units // n
     main = units // count // LANES * LANES
     columns = n * main + (n + 1) // 2 * LANES
 
     def kernel(core_ref, *refs):
         for side in range(2):
             slot = core_ref[0] ^ side
-            out = refs[n + side]
+            out = refs[1 + side]
             for k in range(count):
                 for i in range(n):
-                    out[k, 0, :, i * main : (i + 1) * main] = refs[i][slot, :, k * main : (k + 1) * main]
+                    out[k, 0, :, i * main : (i + 1) * main] = refs[0][slot, :, i * units + k * main : i * units + (k + 1) * main]
                 at = count * main + k // 2 * LANES
                 upper = k % 2 == 1
-                rests = [refs[i][slot, :, at : at + LANES] for i in range(n)]
+                rests = [refs[0][slot, :, i * units + at : i * units + at + LANES] for i in range(n)]
                 for i in range(0, n, 2):
                     to = n * main + i // 2 * LANES
                     out[k, 0, :, to : to + LANES] = half_tiles(
                         rests[i], rests[min(i + 1, n - 1)], upper, upper
                     )
 
-    block = pl.BlockSpec((2, rows, units), lambda q: (q, 0, 0))
+    block = pl.BlockSpec((2, rows, n * units), lambda q: (q, 0, 0))
     return pl.pallas_call(
         kernel,
         grid=(CHIPS,),
-        in_specs=[pl.BlockSpec(memory_space=pltpu.SMEM)] + [block] * n,
+        in_specs=[pl.BlockSpec(memory_space=pltpu.SMEM)] + [block],
         out_specs=[pl.BlockSpec((count, 1, rows, columns), lambda q: (0, q, 0, 0))] * 2,
         out_shape=[jax.ShapeDtypeStruct((count, CHIPS, rows, columns), low)] * 2,
         compiler_params=params(),
         cost_estimate=cost(0, 14 * n * 8 * rows * units // 4),
-    )(core.reshape(1), *grads)
+    )(core.reshape(1), grads)
 
 
 def unit_unpack(n, blocks):
@@ -762,23 +1050,28 @@
         return across(lax.dynamic_index_in_dim(value, 1 - (z >> 1), 0, keepdims=False), home(True))
 
     def seq_join(near, far):
-        return pick(early, near, far), pick(early, far, near)
-
-    def from_sequence(first, second):
+        return pick(early, jnp.concatenate([near, far]), jnp.concatenate([far, near]))
+
+    def from_sequence(value):
+        first, second = value[:local_rows], value[local_rows:]
         near = across(pick(early, first, second), [(b, a) for a, b in home(False)])
         far = across(pick(early, second, first), [(b, a) for a, b in home(True)])
-        return pick(early, jnp.stack([near, far]), jnp.stack([far, near]))
-
-    def both_cores(first, second):
-        return place(
-            [first, second, swap(first, 1), swap(second, 1)], [core, core + 2, 1 - core, 3 - core]
-        ).reshape(seq_len, model_width)
+        return near, far
+
+    def by_micro(near, far):
+        return pick(early, jnp.stack([near, far]), jnp.stack([far, near])).astype(wide)
+
+    def both_cores(value):
+        value = value.reshape(2, local_rows, model_width)
+        return place([value, swap(value, 1)], [core, core + 2, 1 - core, 3 - core]).reshape(
+            seq_len, model_width
+        )
 
     def core_scatter(partial):
         split = partial.reshape(2, 2, local_rows, model_width)
         got = swap(lax.dynamic_index_in_dim(split, 1 - core, 1, keepdims=False), 1)
         mine = lax.dynamic_index_in_dim(split, core, 1, keepdims=False)
-        return tuple(mine[i].astype(wide) + got[i].astype(wide) for i in range(2))
+        return (mine.astype(wide) + got.astype(wide)).reshape(2 * local_rows, model_width)
 
     def head_pairs(other_core, second):
         return [
@@ -789,13 +1082,21 @@
 
     def paired(a, b):
         return jnp.concatenate(
-            [a[:, :head_width], b[:, :head_width], a[:, head_width:], b[:, head_width:]], axis=1
+            [a[..., :head_width], b[..., :head_width], a[..., head_width:], b[..., head_width:]], axis=-1
         )
 
     def attn_fetch(first, second):
         packed = outer_gather(jnp.concatenate([first, second], axis=1))
         groups = [[across(packed, head_pairs(side, which)) for which in range(2)] for side in range(2)]
-        return jnp.stack([paired(*group) for group in groups])
+        return jnp.stack([paired(*pair) for pair in groups])
+
+    def attn_pair(first, second, extra):
+        packed = jnp.concatenate([outer_gather(jnp.concatenate([first, second], axis=1)), extra])
+        return jnp.stack([packed, swap(packed, 1)])
+
+    def attn_fetch_packed(packed, rows):
+        groups = [across(packed, head_pairs(0, which)) for which in range(2)]
+        return paired(*(group[:, :rows] for group in groups)), [group[0, rows:] for group in groups]
 
     def attn_first(sides):
         return sides, swap(sides, 2), swap(sides, 4)
@@ -813,99 +1114,106 @@
             )
         )
 
-    def attn_spread(packed, extra):
-        columns = packed.shape[1]
-        by_chip = plane_rows(packed).reshape(CHIPS, -1, columns)
-        pieces = []
-        for k in range(CHIPS):
-            block = lax.dynamic_index_in_dim(by_chip, chip ^ k, 0, keepdims=False)
-            pieces.append(jnp.concatenate([block, extra.astype(low)]))
-        return scatter_second(scatter_first(pieces)).astype(low)
-
-    def attn_scatter(spread):
-        rows = (spread.shape[0] - EXTRA) // 2
-        cores = spread[: 2 * rows].reshape(2, rows, -1)
-        got = []
-        for other_core in range(2):
-            side = lax.dynamic_index_in_dim(cores, core ^ other_core, 0, keepdims=False)
-            side = jnp.concatenate([side, spread[2 * rows :]])
-            for which in range(2):
-                at = which * head_width
-                piece = jnp.concatenate(
-                    [side[:, at : at + head_width], side[:, core_heads + at : core_heads + at + head_width]],
-                    axis=1,
-                )
-                pairs = [(b, a) for a, b in head_pairs(other_core, which)]
-                got.append(across(piece, pairs).astype(wide))
-        grads = outer_scatter(sum(piece[:rows] for piece in got))
+    def attn_pack(packed, extra):
+        grad = plane_rows(packed).reshape(CHIPS, 2, -1, packed.shape[1])
+        return spread_pack(grad, extra, chip)
+
+    def attn_send(messages):
+        first, second, keep = messages
+        return swap(first, 2), swap(second, 4), keep
+
+    def attn_turn(messages):
+        to_y, to_x = messages
+        return swap(to_y, 4), swap(to_x, 2)
+
+    def attn_scatter(sent, turned):
+        pieces = spread_finish(*sent, *turned, head_width, core)
+        return [
+            across(pieces[2 * side + which], [(b, a) for a, b in head_pairs(side, which)])
+            for side in range(2)
+            for which in range(2)
+        ]
+
+    def attn_join(got, extra_rows):
+        got = [piece.astype(wide) for piece in got]
+        rows = got[0].shape[0] - extra_rows
         small = jnp.stack([piece[rows:] for piece in got])
-        total = jnp.zeros(small.shape[1:], wide)
+        extra = jnp.zeros(small.shape[1:], wide)
         for t in range(count):
             back = (z - t) % count
             index = 2 * ((back >> 1) ^ core) + (back & 1)
-            total = total + lax.dynamic_index_in_dim(small, index, 0, keepdims=False)
+            extra = extra + lax.dynamic_index_in_dim(small, index, 0, keepdims=False)
+        return attn_own(sum(piece[:rows] for piece in got), extra)
+
+    def attn_own(grads, extra):
+        grads = outer_scatter(grads)
         bit = 8
         while bit < plane:
-            total = total + swap(total, bit)
+            extra = extra + swap(extra, bit)
             bit *= 2
-        return grads[:, :head_width], grads[:, head_width:], total
-
-    def unit_send(weights):
-        packed = unit_pack([outer_gather(w) for w in weights])
-        return lax.all_to_all(packed, "chip", 0, 0, tiled=True)
+        return grads[:, :head_width], grads[:, head_width:], extra
 
     def unit_join(n, mine):
         return [full_rows(w) for w in unit_lay(n, mine, swap(mine, 1), core)]
 
     def unit_collect(grads):
         keep, send = unit_unlay([plane_rows(g) for g in grads], core)
-        return (keep.astype(wide) + swap(send, 1).astype(wide)).astype(low)
+        return add_low(keep, swap(send, 1))
 
     def unit_return(n, total):
         return [outer_scatter(g) for g in unit_unpack(n, lax.all_to_all(total, "chip", 0, 0, tiled=True))]
 
     tie = lax.optimization_barrier
 
-    def shifted(value, step):
-        return lax.ppermute(value, "tensor", [((i + step) % count, i) for i in range(count)])
+    def halved(value):
+        upper_part = lax.reduce_precision(value, 8, 7)
+        return jnp.stack([upper_part, value - upper_part]).astype(low)
 
     qk_sides = attn_fetch(w_query, w_key)
-    far = seq_far(block_in[:, 0])
-    ug_laid = unit_send([w_up, w_gate])
-    down_laid = unit_send([w_down])
-    qk_sides, ug_laid, block_in, qk_gain, global_pos = tie((qk_sides, ug_laid, block_in, qk_gain, global_pos))
-    qk_first = attn_first(qk_sides)
-    near = seq_near(block_in[:, 0])
+    unit_blocks = unit_pack([[outer_gather(w_up), outer_gather(w_gate)], [outer_gather(w_down)]])
     mains = lax.dynamic_slice_in_dim(jnp.stack([up_gain, gate_gain]), chip * main, main, 1)
     rests = lax.dynamic_slice_in_dim(jnp.stack([up_gain, gate_gain]), CHIPS * main + chip * rest, rest, 1)
-    gains = jnp.concatenate([jnp.concatenate([mains, rests], axis=1).reshape(1, -1), qk_gain[None]], axis=1)
-    gains = [gains] + [shifted(gains, k) for k in range(1, count)]
+    unit_gains = halved(jnp.concatenate([mains, rests], axis=1).reshape(-1))
+    gain_rows = jnp.concatenate(
+        [unit_gains, halved(qk_gain).reshape(1, -1), jnp.zeros((13, 2 * head_width), low)]
+    )
+    vo_packed = attn_pair(w_value, w_out, gain_rows)
+    unit_blocks = lax.all_to_all(unit_blocks, "chip", 0, 0, tiled=True)
     places_here = global_pos[:, 0]
     places_there = swap(places_here, 1)
-    qk_first, near, far, w_value, w_out, gains, places_there = tie(
-        (qk_first, near, far, w_value, w_out, gains, places_there)
-    )
-    vo_sides = attn_fetch(w_value, w_out)
-    qk_gathered = attn_second(qk_first)
+    qk_sides, vo_packed, places_there, unit_blocks, block_in = tie(
+        (qk_sides, vo_packed, places_there, unit_blocks, block_in)
+    )
+    qk_first = attn_first(qk_sides)
+    vo_sides, gain_groups = attn_fetch_packed(vo_packed, qk_sides.shape[1])
+    near = seq_near(block_in[:, 0])
+    ug_columns = 2 * main + LANES
+    ug_laid, down_laid = unit_blocks[..., :ug_columns], unit_blocks[..., ug_columns:]
+    qk_first, vo_sides, gain_groups, near, block_in, ug_laid, down_laid = tie(
+        (qk_first, vo_sides, gain_groups, near, block_in, ug_laid, down_laid)
+    )
+    far = seq_far(block_in[:, 0])
+    qk_w = attn_lay(attn_second(qk_first))
+    vo_w = attn_lay(attn_second(attn_first(vo_sides)))
+    gain_here = jnp.stack(gain_groups)[:, :2].astype(wide).sum(axis=1)
+    gain_there = swap(gain_here, 1)
+    qk_w, vo_w, gain_there, far, near, ug_laid, down_laid = tie(
+        (qk_w, vo_w, gain_there, far, near, ug_laid, down_laid)
+    )
     tokens = seq_join(near, far)
-    sequence = both_cores(*tokens)
-    vo_sides, qk_gathered, sequence, ug_laid, down_laid, gains = tie(
-        (vo_sides, qk_gathered, sequence, ug_laid, down_laid, gains)
-    )
+    sequence = both_cores(tokens)
     ug_shifted = lax.all_gather(ug_laid, "tensor")
     down_shifted = lax.all_gather(down_laid, "tensor")
-    vo_first = attn_first(vo_sides)
-    qk_w = attn_lay(qk_gathered)
-    gains = jnp.concatenate(gains)
-    gains = lax.dynamic_slice_in_dim(jnp.concatenate([gains, gains]), count - z, count, 0)
-    unit_gains = gains[:, : 2 * plane_unit].reshape(count, 2, plane_unit).transpose(1, 0, 2)
+    unit_gains = pick(
+        core == 0, jnp.concatenate([gain_here, gain_there]), jnp.concatenate([gain_there, gain_here])
+    )
+    unit_gains = lax.dynamic_slice_in_dim(jnp.concatenate([unit_gains, unit_gains]), count - z, count, 0)
+    unit_gains = unit_gains.reshape(count, 2, plane_unit).transpose(1, 0, 2)
     scales = jnp.concatenate(
         [unit_gains[..., :main].reshape(2, -1), unit_gains[..., main:].reshape(2, -1)], axis=1
     )
-    head_gain = gains[:, 2 * plane_unit :]
-    head_gain = lax.dynamic_slice_in_dim(
-        jnp.concatenate([head_gain, head_gain]), z + 2 * core, 2, 0
-    ).reshape(core_heads)
+    head_gain = jnp.stack(gain_groups)[:, 2].astype(wide).reshape(2, 2, head_width).sum(axis=1)
+    head_gain = head_gain.reshape(core_heads)
     places = lax.dynamic_index_in_dim(
         pick((z & 1) == core, places_here, places_there), z >> 1, 0, keepdims=False
     )
@@ -913,84 +1221,97 @@
     flag_row, flag_col = flags[None], flags[:, None]
 
     heads, raw = project_heads(sequence, qk_w, jnp.concatenate([head_gain, head_gain]))
-    vo_w = attn_lay(attn_second(vo_first))
-    value_w, out_w = vo_w[:, :core_heads], vo_w[:, core_heads:]
-    value_rows = dot(sequence, value_w).astype(low)
+    value_rows = product(sequence, vo_w, 0)
     mixed, lse = attend_forward(heads, value_rows, flag_row, flag_col)
-    att_branch = core_scatter(sum_back([(mixed, 0, core_heads)], [(vo_w, 1, core_heads)]))
-    hidden, att_pull = zip(
-        *(jax.vjp(settle, tokens[i].astype(wide), att_branch[i], att_rate) for i in range(2))
-    )
-
-    first_mid = plane_first(hidden[0].astype(low))
-    first_mid, second_hidden = tie((first_mid, hidden[1]))
-    mids = [plane_second(first_mid), plane_second(plane_first(second_hidden.astype(low)))]
+    partial = sum_back([(mixed, 0, core_heads)], [(vo_w, 1, core_heads)])
+    partial = partial.reshape(2, 2, local_rows, model_width)
+    got = swap(lax.dynamic_index_in_dim(partial, 1 - core, 1, keepdims=False), 1)
+    hidden, hidden_low, att_branch = settle_attention(partial, got, tokens, att_rate, core)
+
+    own_rows = 2 * local_rows
+    all_rows = CHIPS * own_rows
+    hidden_low, ug_shifted = tie((hidden_low, ug_shifted))
+    first = plane_first(hidden_low)
     up_w, gate_w = unit_join(2, ug_shifted)
-    laid = ()
-    for i in range(2):
-        laid = mlp_forward(mids[i], up_w, gate_w, scales, i, laid)
-    laid, out_grad, down_shifted = tie((laid, out_grad, down_shifted))
-    mid, up_raw, gate_raw, activated = laid
-    units, chunk_rows = activated.shape[1], CHIPS * local_rows
-    cotangent = seq_join(seq_near(out_grad[:, 0].astype(low)), seq_far(out_grad[:, 0].astype(low)))
+    earlier, saved, acts = (), [], []
+
+    def forward(blocks, at):
+        nonlocal earlier
+        *earlier, act, up_raw, gate_raw = mlp_forward(blocks, up_w, gate_w, scales, all_rows, at, earlier)
+        saved.append((up_raw, gate_raw))
+        return act
+
+    def back(act):
+        return sum_back([(act, 0, act.shape[1])], [(down_w, 0, act.shape[1])])
+
+    def by_chip(own, both, diagonal):
+        return [own, both[:own_rows], both[own_rows:], diagonal]
+
+    act_own = forward([hidden_low], 2)
+    out_grad_low = out_grad[:, 0].astype(low)
+    first, act_own, out_grad_low = tie((first, act_own, out_grad_low))
+    _, along_x, along_y, *diagonal = plane_second(first)
+    act_both = forward([along_x, along_y], 0)
+    diagonal, act_both, down_shifted = tie((diagonal, act_both, down_shifted))
     (down_w,) = unit_join(1, down_shifted)
-
-    def by_chip(value):
-        return [value[k * local_rows : (k + 1) * local_rows] for k in range(CHIPS)]
-
-    def back(i):
-        return sum_back([(activated, 0, units)], [(down_w, 0, units)], chunk_rows, i)
-
-    def turn(i, sent):
-        rows, pull = jax.vjp(settle, hidden[i], scatter_second(sent), mlp_rate)
-        direct, branch_grad, term = pull(cotangent[i].astype(wide))
-        return rows, direct, term, plane_first(branch_grad.astype(low))
-
-    sent = scatter_first(by_chip(back(0)))
-    sent, second_part = tie((sent, back(1)))
-    second_sent = scatter_first(by_chip(second_part))
-    rows_a, direct_a, term_a, first_a = turn(0, sent)
-    rows_b, direct_b, term_b, first_b = turn(1, second_sent)
-
-    branch_a = plane_second(first_a)
-    branch_a, first_b = tie((branch_a, first_b))
-    branch_b = plane_second(first_b)
-    weights = (up_w, gate_w, down_w, scales, up_raw, gate_raw)
-    *laid, part, unit_term_a = mlp_backward(branch_a, *weights, 0, ())
-    sent = scatter_first(by_chip(part))
-    laid, rows_a, rows_b = tie((laid, rows_a, rows_b))
-    *laid, part, unit_term_b = mlp_backward(branch_b, *weights, 1, laid)
-    block_out = from_sequence(rows_a.astype(low), rows_b.astype(low)).astype(wide)
-    branch, up_low, gate_low = laid
-    sent, part = tie((sent, part))
-    second_sent = scatter_first(by_chip(part))
-    down_grad = dot_rows(branch, activated)
-    sent, second_sent, down_grad, mid = tie((sent, second_sent, down_grad, mid))
-    hidden_total = [direct_a + scatter_second(sent), direct_b + scatter_second(second_sent)]
-    up_w_grad, gate_w_grad = dot_rows(mid, up_low), dot_rows(mid, gate_low)
-    input_direct, att_grad, att_rate_terms = zip(*(att_pull[i](hidden_total[i]) for i in range(2)))
-    att_low = both_cores(*(grad.astype(low) for grad in att_grad))
-    unit_blocks = unit_collect([up_w_grad, gate_w_grad, down_grad])
-    att_low, unit_blocks = tie((att_low, unit_blocks))
-    units_back = lax.psum_scatter(unit_blocks, "tensor", scatter_dimension=0)
-    mixed_grad = dot(att_low, out_w).astype(low)
+    act_diagonal = forward(diagonal, 3)
+    mid, activated = earlier
+    parts = [back(act) for act in (act_own, act_both, act_diagonal)]
+    parts, out_grad_low = tie((parts, out_grad_low))
+    sent, _ = scatter_first(by_chip(*parts))
+    cotangent = seq_near(out_grad_low), seq_far(out_grad_low)
+    sent, cotangent = tie((sent, cotangent))
+    block_rows, direct, branch_grad, mlp_rate_term = settle_units(
+        scatter_last(sent), hidden, *cotangent, early, mlp_rate
+    )
+
+    first = plane_first(branch_grad)
+    returned = from_sequence(block_rows)
+    earlier, unit_terms = (), []
+
+    def backward(blocks, at, raws):
+        nonlocal earlier
+        *earlier, part, unit_term = mlp_backward(
+            blocks, up_w, gate_w, down_w, scales, *raws, all_rows, at, earlier
+        )
+        unit_terms.append(unit_term[:2])
+        return part
+
+    part_own = backward([branch_grad], 2, saved[0])
+    first, part_own = tie((first, part_own))
+    _, along_x, along_y, *diagonal = plane_second(first)
+    part_both = backward([along_x, along_y], 0, saved[1])
+    diagonal, part_both, returned = tie((diagonal, part_both, returned))
+    part_diagonal = backward(diagonal, 3, saved[2])
+    branch, up_low, gate_low = earlier
+    sent, (branch, mid) = scatter_first(by_chip(part_own, part_both, part_diagonal), (branch, mid))
+    down_blocks = unit_unlay(plane_rows(rows_product([(branch, [activated])], 2 * LANES)), 1, core)
+    ug_grad = rows_product([(mid, [up_low, gate_low])], 2 * LANES)
+    sent, down_blocks, ug_grad = tie((sent, down_blocks, ug_grad))
+    arrived = scatter_last(sent)
+    down_blocks = add_low(down_blocks[0], swap(down_blocks[1], 1))
+    ug_blocks = unit_unlay(plane_rows(ug_grad), 2, core)
+    arrived, ug_blocks, down_blocks = tie((arrived, ug_blocks, down_blocks))
+    down_back = lax.psum_scatter(down_blocks, "tensor", scatter_dimension=0)
+    ug_there = swap(ug_blocks[1], 1)
+    input_direct, att_grad, att_rate_term = settle_attention_back(
+        arrived, direct, hidden, tokens, att_branch, att_rate
+    )
+    att_low = both_cores(att_grad)
+    ug_blocks = add_low(ug_blocks[0], ug_there)
+    att_low, ug_blocks = tie((att_low, ug_blocks))
+    ug_back = lax.psum_scatter(ug_blocks, "tensor", scatter_dimension=0)
+    mixed_grad = product(att_low, vo_w, 1)
     heads_low, vraw_low, head_terms = attend_backward(
         heads, raw, value_rows, mixed, mixed_grad, lse, head_gain, flag_row, flag_col
     )
-    in_part = sum_back(
-        [(heads_low, 0, 2 * core_heads), (vraw_low, 0, core_heads)],
-        [(qk_w, 0, 2 * core_heads), (vo_w, 0, core_heads)],
-    )
-    in_rows = [input_direct[i] + part for i, part in enumerate(core_scatter(in_part))]
-    in_grad = from_sequence(*(rows.astype(low) for rows in in_rows)).astype(wide)
-    unit_terms = [unit_term_a[:2], unit_term_b[:2]]
-    mlp_rate_terms = [term_a, term_b]
+    block_out = by_micro(*returned)
 
     small = jnp.concatenate(
         [
-            unit_terms[0] + unit_terms[1],
-            (att_rate_terms[0] + att_rate_terms[1])[None],
-            (mlp_rate_terms[0] + mlp_rate_terms[1])[None],
+            sum(unit_terms),
+            att_rate_term[:1],
+            mlp_rate_term[:1],
         ]
     )
     small = small + swap(small, 1)
@@ -1014,14 +1335,35 @@
     qk_extra = jnp.concatenate(
         [
             jnp.where(own_chip, head_terms[:2].reshape(1, 4 * head_width), 0.0),
-            jnp.zeros((EXTRA - CHIPS, 4 * head_width), wide),
+            jnp.zeros((EXTRA // 2 - CHIPS, 4 * head_width), wide),
         ]
     )
-    vo_spread = attn_spread(rows_product([(sequence, vraw_low), (att_low, mixed)]), vo_extra)
-    qk_spread = attn_spread(dot_rows(sequence, heads_low), qk_extra)
-    grad_value, grad_out, vo_small = attn_scatter(vo_spread)
-    grad_query, grad_key, qk_small = attn_scatter(qk_spread)
-    grad_up, grad_gate, grad_down = unit_return(3, units_back)
+    heads_low, vraw_low, down_back = tie((heads_low, vraw_low, down_back))
+    vo_grad = rows_product([(sequence, [vraw_low]), (att_low, [mixed])], core_heads)
+    vo_messages, vraw_low = tie((attn_pack(vo_grad, vo_extra), vraw_low))
+    vo_sent = attn_send(vo_messages)
+    in_part = sum_back(
+        [(heads_low, 0, 2 * core_heads), (vraw_low, 0, core_heads)],
+        [(qk_w, 0, 2 * core_heads), (vo_w, 0, core_heads)],
+    )
+    vo_sent, heads_low, in_part, ug_back, block_out = tie((vo_sent, heads_low, in_part, ug_back, block_out))
+    vo_messages, heads_low, in_part = tie((spread_turn(*vo_sent), heads_low, in_part))
+    vo_turned = attn_turn(vo_messages)
+    in_rows = (input_direct + core_scatter(in_part)).astype(low)
+    qk_messages = attn_pack(rows_product([(sequence, [heads_low])], 2 * LANES), qk_extra)
+    vo_turned, in_rows, qk_messages = tie((vo_turned, in_rows, qk_messages))
+    qk_sent = attn_send(qk_messages)
+    returned_in = from_sequence(in_rows)
+    vo_got = attn_scatter(vo_sent, vo_turned)
+    qk_sent, down_back, ug_back = tie((qk_sent, down_back, ug_back))
+    qk_turned = attn_turn(spread_turn(*qk_sent))
+    (grad_down,) = unit_return(1, down_back)
+    qk_turned, returned_in, vo_got, grad_down = tie((qk_turned, returned_in, vo_got, grad_down))
+    qk_got = attn_scatter(qk_sent, qk_turned)
+    grad_up, grad_gate = unit_return(2, ug_back)
+    in_grad = by_micro(*returned_in)
+    grad_value, grad_out, vo_small = attn_join(vo_got, EXTRA)
+    grad_query, grad_key, qk_small = attn_join(qk_got, EXTRA // 2)
 
     units = vo_small[:CHIPS].reshape(CHIPS, 2, plane_unit).transpose(1, 0, 2)
     units = jnp.concatenate([units[..., :main].reshape(2, -1), units[..., main:].reshape(2, -1)], axis=1)

time: 781 us -> 678 us (0.87)
  Pallas kernels: 189 us -> 286 us
  starting transfers between devices: 161 us -> 91.3 us
  waiting for transfers between devices: 231 us -> 181 us
  other arithmetic: 75.1 us -> 29 us
  matrix products: 39.4 us -> 0 us
  local copies, waits for them, and re-layouts: 56 us -> 65.8 us
    pallas_call x7 -> x23, Pallas kernels: 39.6 us -> 127 us  [the longest x4 47.9 us: rows_product(): pl.pallas_call(kernel, grid=(sum(steps),), in_specs=[pl.BlockSpec((n, dep...]
    ppermute x59 -> x44, starting transfers between devices: 77.3 us -> 34.6 us  [swap(): return lax.ppermute(value, DP, [(i, i ^ bit) for i in range(count)])]
    ppermute x59 -> x44, waiting for transfers between devices: 143 us -> 102 us  [swap(): return lax.ppermute(value, DP, [(i, i ^ bit) for i in range(count)])]
    dot_general x6 -> x0, matrix products: 39.4 us -> none  [the longest x4 32 us: tn(): lax.dot_general(left, right, (((0,), (0,)), ((), ())), preferred_element_...]
    ppermute x24 -> x22, starting transfers between devices: 70.7 us -> 44.2 us  [across(): lax.ppermute(value, ALL, [(a * count + b, c * count + d) for (a, b), (c,...]
    unnamed x181 -> x197, local copies, waits for them, and re-layouts: 18.2 us -> 38.6 us
    convert_element_type x27 -> x17, other arithmetic: 33.6 us -> 15.2 us  [the longest x2 5.2 us: by_micro(): pick(early, jnp.stack([near, far]), jnp.stack([far, near])).astype(wide)]
    reduce_sum x10 -> x2, other arithmetic: 17.5 us -> 0.05 us  [the longest x1 0.03 us: per_device(): gain_here = jnp.stack(gain_groups)[:, :2].astype(wide).sum(axis=1)]
  transfers between devices with their start and end apart: 92 -> 73, of which waited for: 30 -> 29; matrix products, arithmetic and copies ran while one was open for 14% -> 7% of each run, Pallas kernels for 17% -> 38%
where the time goes in v2:
time: 678 us; the launch traced here: 670 us
  Pallas kernels  286 us (42%)
  waiting for transfers between devices  181 us (27%)
  starting transfers between devices  91.3 us (13%)
  local copies, waits for them, and re-layouts  65.8 us (10%)
  other arithmetic  29 us (4%)
  between operations  15.9 us (2%)
    ppermute x44, waiting for transfers between devices, swap(): return lax.ppermute(value, DP, [(i, i ^ bit) for i in range(count)])  102 us
    ppermute x22, waiting for transfers between devices, across(): lax.ppermute(value, ALL, [(a * count + b, c * count + d) for (a, b), (c,...  54.3 us
    pallas_call x4, Pallas kernels, rows_product(): pl.pallas_call(kernel, grid=(sum(steps),), in_specs=[pl.BlockSpec((n, dep...  47.9 us
    pallas_call x3, Pallas kernels, mlp_backward(): pl.pallas_call(kernel, grid=(steps,), in_specs=chunk_specs(blocks, depth)...  44.4 us
    ppermute x22, starting transfers between devices, across(): lax.ppermute(value, ALL, [(a * count + b, c * count + d) for (a, b), (c,...  44.2 us
    unnamed x197, local copies, waits for them, and re-layouts  38.6 us
    ppermute x44, starting transfers between devices, swap(): return lax.ppermute(value, DP, [(i, i ^ bit) for i in range(count)])  34.6 us
    pallas_call x1, Pallas kernels, attend_backward(): pl.pallas_call(kernel, grid=(pairs,), in_specs=[block, keys, block, block...  28.7 us
  transfers between devices with their start and end apart: 73, of which 29 were waited for; matrix products, arithmetic and copies ran while one was open for 7% of the time, Pallas kernels for 38%

profile of v2, /device:TPU:0, one launch (start us, length us, event | category | flops | bytes accessed | tf_op | source)
XLA Modules:
  0.0 669.7 jit_solution(10902695830487219244)
XLA Ops:
  27.5 13.7 %all-to-all-done = bf16[4,160,1024]{2,1,0:T(8,128)(2,1)} async-done(((bf16[4,160,1024]{2,1,0:T(8,128)(2,1)}), bf16[4,160,1024]{2,1,0:T(8,128)(2,1)}, u32[]{:S(2)}, u32[]{:S(2)}) %all-to-all-start) | async-done | bytes 1310752 | tf_op jit(solution)/shard_map/all_to_all | solution.py:1181
  56.7 6.5 collective-permute-start.10
  81.3 11.8 %collective-permute-done.14.refs_2_ = bf16[2,160,1280]{2,1,0:T(8,128)(2,1)S(1)} collective-permute-done((bf16[2,160,1280]{2,1,0:T(8,128)(2,1)S(1)}, bf16[2,160,1280]{2,1,0:T(8,128)(2,1)S(1)}, u32[]{:S(2)}, u32[]{:S(2)}) %collective-permute-start.14) | collective-permute-done | bytes 819232 | tf_op jit(solution)/shard_map/ppermute | solution.py:30
  96.2 6.2 collective-permute-done.11.refs_3_
  124.9 11.6 %shard_map.258 = (bf16[1024,1280]{1,0:T(8,128)(2,1)S(1)}, bf16[1024,1280]{1,0:T(8,128)(2,1)S(1)}) custom-call(bf16[1024,1280]{1,0:T(8,128)(2,1)} %bitcast.127, bf16[1280,1280]{1,0:T(8,128)(2,1)} %bitcast.162, f32[1,1280]{1,0:T(1,128)S(1)} %broadcast_in_dim.92.gain_ref), custom_call_target="tpu_custom_call" | custom-call | flops 1 | bytes 1 | tf_op jit(solution)/shard_map/pallas_call | solution.py:163
  136.5 15.7 %shard_map.260 = (bf16[1024,640]{1,0:T(8,128)(2,1)S(1)}, f32[5,8,1024]{2,1,0:T(8,128)S(1)}) custom-call(bf16[1024,1280]{1,0:T(8,128)(2,1)S(1)} %get-tuple-element.217.q_ref.k_ref, bf16[1024,1280]{1,0:T(8,128)(2,1)S(1)} %get-tuple-element.217.q_ref.k_ref, bf16[1024,640]{1,0:T(8,128)(2,1)S(1)} %shard_map.259.v_ref, f32[1,1024]{1,0:T(1,128)S(1)} %bitcast.150, ...), custom_call_target="tpu_custom_call" | custom-call | flops 1 | bytes 1 | tf_op jit(solution)/shard_map/pallas_call | solution.py:225
  167.0 9.8 %all-gather.5.cloned.1.call-done = bf16[16,160,640]{2,1,0:T(8,128)(2,1)} async-done(((bf16[4,160,640]{2,1,0:T(8,128)(2,1)}), bf16[16,160,640]{2,1,0:T(8,128)(2,1)}) %all-gather.5.cloned.1.call-update) | async-done | bytes 3276816 | tf_op jit(solution)/shard_map/all_gather | solution.py:1205
  190.5 8.0 %shard_map.264 = (bf16[2048,1280]{1,0:T(8,128)(2,1)}, bf16[2048,1280]{1,0:T(8,128)(2,1)}, bf16[512,1280]{1,0:T(8,128)(2,1)S(1)}, bf16[512,1280]{1,0:T(8,128)(2,1)S(1)}, bf16[512,1280]{1,0:T(8,128)(2,1)S(1)}) custom-call(bf16[512,1280]{1,0:T(8,128)(2,1)} %get-tuple-element.223.refs_0_, bf16[1280,1280]{1,0:T(8,128)(2,1)} %bitcast.120, ...), custom_call_target="tpu_custom_call" | custom-call | flops 1 | bytes 1 | tf_op jit(solution)/shard_map/pallas_call | solution.py:649
  199.6 9.0 %collective-permute-done.22.refs_1_ = bf16[512,1280]{1,0:T(8,128)(2,1)S(1)} collective-permute-done((bf16[512,1280]{1,0:T(8,128)(2,1)}, bf16[512,1280]{1,0:T(8,128)(2,1)S(1)}, u32[]{:S(2)}, u32[]{:S(2)}) %collective-permute-start.22) | collective-permute-done | bytes 1310752 | tf_op jit(solution)/shard_map/ppermute | solution.py:30
  213.5 11.4 %shard_map.265 = (bf16[2048,1280]{1,0:T(8,128)(2,1)}, bf16[2048,1280]{1,0:T(8,128)(2,1)}, bf16[1024,1280]{1,0:T(8,128)(2,1)S(1)}, bf16[1024,1280]{1,0:T(8,128)(2,1)}, bf16[1024,1280]{1,0:T(8,128)(2,1)}) custom-call(bf16[512,1280]{1,0:T(8,128)(2,1)S(1)} %collective-permute-done.21.refs_0_, ...), custom_call_target="tpu_custom_call", output_to_operand_aliasing={{0}: (5, {}), {1}: (6, {})} | custom-call | flops 1 | bytes 1 | tf_op jit(solution)/shard_map/pallas_call | solution.py:649
  228.3 7.9 %shard_map.269 = (bf16[2048,1280]{1,0:T(8,128)(2,1)}, bf16[2048,1280]{1,0:T(8,128)(2,1)}, bf16[512,1280]{1,0:T(8,128)(2,1)S(1)}, bf16[512,1280]{1,0:T(8,128)(2,1)S(1)}, bf16[512,1280]{1,0:T(8,128)(2,1)S(1)}) custom-call(bf16[256,1280]{1,0:T(8,128)(2,1)} %collective-permute-done.24.refs_0_, ...), custom_call_target="tpu_custom_call", output_to_operand_aliasing={{0}: (5, {}), {1}: (6, {})} | custom-call | flops 1 | bytes 1 | tf_op jit(solution)/shard_map/pallas_call | solution.py:649
  239.9 6.1 shard_map.268
  257.1 28.0 %collective-permute-done.30.refs_7_ = bf16[256,1280]{1,0:T(8,128)(2,1)S(1)} collective-permute-done((bf16[256,1280]{1,0:T(8,128)(2,1)S(1)}, bf16[256,1280]{1,0:T(8,128)(2,1)S(1)}, u32[]{:S(2)}, u32[]{:S(2)}) %collective-permute-start.30) | collective-permute-done | bytes 655392 | tf_op jit(solution)/shard_map/ppermute | solution.py:1035
  289.0 12.8 %collective-permute-done.32.refs_4_ = bf16[256,1280]{1,0:T(8,128)(2,1)S(1)} collective-permute-done((bf16[256,1280]{1,0:T(8,128)(2,1)}, bf16[256,1280]{1,0:T(8,128)(2,1)S(1)}, u32[]{:S(2)}, u32[]{:S(2)}) %collective-permute-start.32) | collective-permute-done | bytes 655392 | tf_op jit(solution)/shard_map/ppermute | solution.py:30
  303.2 6.5 shard_map.271
  315.7 12.2 %shard_map.272 = (bf16[2048,1280]{1,0:T(8,128)(2,1)}, bf16[2048,1280]{1,0:T(8,128)(2,1)}, bf16[2048,1280]{1,0:T(8,128)(2,1)}, bf16[512,1280]{1,0:T(8,128)(2,1)S(1)}, f32[8,1280]{1,0:T(8,128)S(1)}) custom-call(bf16[512,1280]{1,0:T(8,128)(2,1)S(1)} %get-tuple-element.258.refs_0_, bf16[1280,1280]{1,0:T(8,128)(2,1)} %bitcast.115, ...), custom_call_target="tpu_custom_call" | custom-call | flops 1 | bytes 1 | tf_op jit(solution)/shard_map/pallas_call | solution.py:722
  328.0 10.0 %collective-permute-done.34.refs_1_ = bf16[512,1280]{1,0:T(8,128)(2,1)S(1)} collective-permute-done((bf16[512,1280]{1,0:T(8,128)(2,1)S(1)}, bf16[512,1280]{1,0:T(8,128)(2,1)S(1)}, u32[]{:S(2)}, u32[]{:S(2)}) %collective-permute-start.34) | collective-permute-done | bytes 1310752 | tf_op jit(solution)/shard_map/ppermute | solution.py:30
  341.5 19.5 %shard_map.273 = (bf16[2048,1280]{1,0:T(8,128)(2,1)}, bf16[2048,1280]{1,0:T(8,128)(2,1)}, bf16[2048,1280]{1,0:T(8,128)(2,1)}, bf16[1024,1280]{1,0:T(8,128)(2,1)S(1)}, f32[8,1280]{1,0:T(8,128)S(1)}) custom-call(bf16[512,1280]{1,0:T(8,128)(2,1)S(1)} %collective-permute-done.33.refs_0_, ...), custom_call_target="tpu_custom_call", output_to_operand_aliasing={{0}: (8, {}), {1}: (9, {}), {2}: (10, {})} | custom-call | flops 1 | bytes 1 | tf_op jit(solution)/shard_map/pallas_call | solution.py:722
  361.1 12.7 %shard_map.274 = (bf16[2048,1280]{1,0:T(8,128)(2,1)}, bf16[2048,1280]{1,0:T(8,128)(2,1)}, bf16[2048,1280]{1,0:T(8,128)(2,1)}, bf16[512,1280]{1,0:T(8,128)(2,1)S(1)}, f32[8,1280]{1,0:T(8,128)S(1)}) custom-call(bf16[256,1280]{1,0:T(8,128)(2,1)S(1)} %collective-permute-done.35.refs_0_, ...), custom_call_target="tpu_custom_call", output_to_operand_aliasing={{0}: (8, {}), {1}: (9, {}), {2}: (10, {})} | custom-call | flops 1 | bytes 1 | tf_op jit(solution)/shard_map/pallas_call | solution.py:722
  379.2 12.6 %shard_map.275 = bf16[1280,1280]{1,0:T(8,128)(2,1)S(1)} custom-call(bf16[2048,1280]{1,0:T(8,128)(2,1)} %get-tuple-element.285.refs_0_, bf16[2048,1280]{1,0:T(8,128)(2,1)} %get-tuple-element.286.refs_1_), custom_call_target="tpu_custom_call" | custom-call | flops 1 | bytes 1 | tf_op jit(solution)/shard_map/pallas_call | solution.py:426
  398.0 19.7 %shard_map.277 = bf16[1280,2560]{1,0:T(8,128)(2,1)} custom-call(bf16[2048,1280]{1,0:T(8,128)(2,1)S(1)} %bitcast.131, bf16[2048,1280]{1,0:T(8,128)(2,1)} %get-tuple-element.290.refs_1_, bf16[2048,1280]{1,0:T(8,128)(2,1)} %get-tuple-element.291.refs_2_), custom_call_target="tpu_custom_call" | custom-call | flops 1 | bytes 1 | tf_op jit(solution)/shard_map/pallas_call | solution.py:426
  421.2 5.6 shard_map.278
  440.8 7.0 %shard_map.280 = (f32[512,1280]{1,0:T(8,128)}, bf16[512,1280]{1,0:T(8,128)(2,1)S(1)}, f32[8,1280]{1,0:T(8,128)S(1)}) custom-call(bf16[512,1280]{1,0:T(8,128)(2,1)S(1)} %copy-done.62, bf16[512,1280]{1,0:T(8,128)(2,1)S(1)} %collective-permute-done.39.refs_1_, bf16[512,1280]{1,0:T(8,128)(2,1)} %collective-permute-done.40.refs_2_, ...), custom_call_target="tpu_custom_call" | custom-call | flops 1 | bytes 1 | tf_op jit(solution)/shard_map/pallas_call | solution.py:602
  470.1 28.7 %shard_map.284 = (bf16[1024,1280]{1,0:T(8,128)(2,1)}, bf16[1024,640]{1,0:T(8,128)(2,1)S(1)}, f32[8,640]{1,0:T(8,128)S(1)}) custom-call(bf16[1024,1280]{1,0:T(8,128)(2,1)} %copy-done.6, bf16[1024,1280]{1,0:T(8,128)(2,1)} %copy-done.6, bf16[1024,640]{1,0:T(8,128)(2,1)S(1)} %copy-done.13, bf16[1024,1280]{1,0:T(8,128)(2,1)} %copy-done.21, ...), custom_call_target="tpu_custom_call" | custom-call | flops 1 | bytes 1 | tf_op jit(solution)/shard_map/pallas_call | solution.py:325
  502.9 9.3 %shard_map.285 = bf16[1280,1280]{1,0:T(8,128)(2,1)} custom-call(bf16[1024,1280]{1,0:T(8,128)(2,1)S(1)} %bitcast.128, bf16[1024,1280]{1,0:T(8,128)(2,1)} %bitcast.133, bf16[1024,640]{1,0:T(8,128)(2,1)S(1)} %copy-done.27, bf16[1024,640]{1,0:T(8,128)(2,1)S(1)} %copy-done.16), custom_call_target="tpu_custom_call" | custom-call | flops 1 | bytes 1 | tf_op jit(solution)/shard_map/pallas_call | solution.py:426
  520.2 8.7 %shard_map.287 = bf16[1024,1280]{1,0:T(8,128)(2,1)S(1)} custom-call(bf16[1024,1280]{1,0:T(8,128)(2,1)} %get-tuple-element.347.refs_0_.refs_1_, bf16[1024,640]{1,0:T(8,128)(2,1)S(1)} %copy-done.28, bf16[1280,1280]{1,0:T(8,128)(2,1)} %bitcast.163, bf16[1280,1280]{1,0:T(8,128)(2,1)} %bitcast.161), custom_call_target="tpu_custom_call" | custom-call | flops 1 | bytes 1 | tf_op jit(solution)/shard_map/pallas_call | solution.py:364
  530.4 10.7 %collective-permute-done.47.first_ref = bf16[2,192,1280]{2,1,0:T(8,128)(2,1)S(1)} collective-permute-done((bf16[2,192,1280]{2,1,0:T(8,128)(2,1)S(1)}, bf16[2,192,1280]{2,1,0:T(8,128)(2,1)S(1)}, u32[]{:S(2)}, u32[]{:S(2)}) %collective-permute-start.47) | collective-permute-done | bytes 983072 | tf_op jit(solution)/shard_map/ppermute | solution.py:30
  556.6 6.2 shard_map.289
  577.7 14.5 %collective-permute-done.52.first_ref = bf16[2,176,1280]{2,1,0:T(8,128)(2,1)S(1)} collective-permute-done((bf16[2,176,1280]{2,1,0:T(8,128)(2,1)S(1)}, bf16[2,176,1280]{2,1,0:T(8,128)(2,1)S(1)}, u32[]{:S(2)}, u32[]{:S(2)}) %collective-permute-start.52) | collective-permute-done | bytes 901152 | tf_op jit(solution)/shard_map/ppermute | solution.py:30
  592.2 6.5 collective-permute-start.56
  606.8 15.4 %collective-permute-done.60 = bf16[192,640]{1,0:T(8,128)(2,1)} collective-permute-done((bf16[192,640]{1,0:T(8,128)(2,1)S(1)}, bf16[192,640]{1,0:T(8,128)(2,1)}, u32[]{:S(2)}, u32[]{:S(2)}) %collective-permute-start.60) | collective-permute-done | bytes 245792 | tf_op jit(solution)/shard_map/ppermute | solution.py:1035
  652.1 8.8 %collective-permute-done.64 = bf16[176,640]{1,0:T(8,128)(2,1)S(1)} collective-permute-done((bf16[176,640]{1,0:T(8,128)(2,1)}, bf16[176,640]{1,0:T(8,128)(2,1)S(1)}, u32[]{:S(2)}, u32[]{:S(2)}) %collective-permute-start.64) | collective-permute-done | bytes 225312 | tf_op jit(solution)/shard_map/ppermute | solution.py:1035
  (512 shorter events, 280.7 us)
Async XLA Ops:
  24.2 152.6 %all-gather.5.cloned.1.call-start = ((), (), s32[]{:S(2)}) async-start(), calls=%async_computation.7 | async-start | bytes 4096000 | tf_op jit(solution)/shard_map/all_gather | solution.py:1205
  41.2 22.0 %collective-permute-start.9 = (bf16[2,176,640]{2,1,0:T(8,128)(2,1)}, bf16[2,176,640]{2,1,0:T(8,128)(2,1)S(1)}, u32[]{:S(2)}, u32[]{:S(2)}) collective-permute-start(bf16[2,176,640]{2,1,0:T(8,128)(2,1)} %pad_maximum_fusion.5), channel_id=1, source_target_pairs={{1,0},{2,1},{3,2},{0,3},{7,4},{4,5},{5,6},{6,7},{9,8},{10,9},{11,1... | collective-permute-start | bytes 1351688 | tf_op jit(solution)/shard_map/ppermute | solution.py:1035
  76.7 25.7 %collective-permute-start.11 = (bf16[160,1280]{1,0:T(8,128)(2,1)S(1)}, bf16[160,1280]{1,0:T(8,128)(2,1)S(1)}, u32[]{:S(2)}, u32[]{:S(2)}) collective-permute-start(bf16[160,1280]{1,0:T(8,128)(2,1)S(1)} %slice_bitcast_fusion.3), channel_id=1, source_target_pairs={{0,8},{4,12},{8,0},{12,4},{16,24},{20,28},{24,16},{28,20},{1,9},{5... | collective-permute-start | bytes 1228808 | tf_op jit(solution)/shard_map/ppermute | solution.py:30
  77.3 25.2 %collective-permute-start.12 = (bf16[160,1280]{1,0:T(8,128)(2,1)}, bf16[160,1280]{1,0:T(8,128)(2,1)}, u32[]{:S(2)}, u32[]{:S(2)}) collective-permute-start(bf16[160,1280]{1,0:T(8,128)(2,1)} %slice_bitcast_fusion.2), channel_id=1, source_target_pairs={{0,16},{4,20},{8,24},{12,28},{16,0},{20,4},{24,8},{28,12},{1,17},{... | collective-permute-start | bytes 1228808 | tf_op jit(solution)/shard_map/ppermute | solution.py:30
  79.7 33.6 %collective-permute-start.18 = (bf16[256,1280]{1,0:T(8,128)(2,1)}, bf16[256,1280]{1,0:T(8,128)(2,1)}, u32[]{:S(2)}, u32[]{:S(2)}) collective-permute-start(bf16[256,1280]{1,0:T(8,128)(2,1)} %dynamic-slice_bitcast_fusion.4), channel_id=1, source_target_pairs={{0,2},{1,6},{2,0},{3,4},{4,3},{5,7},{6,1},{7,5},{8,10},{9,14},{10,... | collective-permute-start | bytes 1966088 | tf_op jit(solution)/shard_map/ppermute | solution.py:1035
  113.3 113.0 %all-gather.7.cloned.1.call-start = ((), (), s32[]{:S(2)}) async-start(), calls=%async_computation.8 | async-start | bytes 2457600 | tf_op jit(solution)/shard_map/all_gather | solution.py:1206
  176.8 323.4 %reduce-scatter.3.cloned.1.call-start = ((), (), s32[]{:S(2)}) async-start(), calls=%async_computation.5 | async-start | bytes 2457600 | tf_op jit(solution)/shard_map/reduce_scatter | solution.py:1295
  177.1 31.5 %collective-permute-start.22 = (bf16[512,1280]{1,0:T(8,128)(2,1)}, bf16[512,1280]{1,0:T(8,128)(2,1)S(1)}, u32[]{:S(2)}, u32[]{:S(2)}) collective-permute-start(bf16[512,1280]{1,0:T(8,128)(2,1)} %get-tuple-element.223.refs_0_), channel_id=1, source_target_pairs={{0,16},{4,20},{8,24},{12,28},{16,0},{20,4},{24,8},{28,12},{1,17},{... | collective-permute-start | bytes 3932168 | tf_op jit(solution)/shard_map/ppermute | solution.py:30
  178.6 31.1 %collective-permute-start.21 = (bf16[512,1280]{1,0:T(8,128)(2,1)}, bf16[512,1280]{1,0:T(8,128)(2,1)S(1)}, u32[]{:S(2)}, u32[]{:S(2)}) collective-permute-start(bf16[512,1280]{1,0:T(8,128)(2,1)} %get-tuple-element.223.refs_0_), channel_id=1, source_target_pairs={{0,8},{4,12},{8,0},{12,4},{16,24},{20,28},{24,16},{28,20},{1,9},{5... | collective-permute-start | bytes 3932168 | tf_op jit(solution)/shard_map/ppermute | solution.py:30
  252.1 33.1 %collective-permute-start.27 = (bf16[512,1280]{1,0:T(8,128)(2,1)S(1)}, bf16[512,1280]{1,0:T(8,128)(2,1)S(1)}, u32[]{:S(2)}, u32[]{:S(2)}) collective-permute-start(bf16[512,1280]{1,0:T(8,128)(2,1)S(1)} %pad_maximum_fusion), channel_id=1, source_target_pairs={{0,8},{4,12},{8,0},{12,4},{16,24},{20,28},{24,16},{28,20},{1,9},{5... | collective-permute-start | bytes 3932168 | tf_op jit(solution)/shard_map/ppermute | solution.py:30
  253.6 31.6 %collective-permute-start.28 = (bf16[512,1280]{1,0:T(8,128)(2,1)S(1)}, bf16[512,1280]{1,0:T(8,128)(2,1)S(1)}, u32[]{:S(2)}, u32[]{:S(2)}) collective-permute-start(bf16[512,1280]{1,0:T(8,128)(2,1)S(1)} %pad_maximum_fusion.1), channel_id=1, source_target_pairs={{0,16},{4,20},{8,24},{12,28},{16,0},{20,4},{24,8},{28,12},{1,17},{... | collective-permute-start | bytes 3932168 | tf_op jit(solution)/shard_map/ppermute | solution.py:30
  255.1 30.0 %collective-permute-start.30 = (bf16[256,1280]{1,0:T(8,128)(2,1)S(1)}, bf16[256,1280]{1,0:T(8,128)(2,1)S(1)}, u32[]{:S(2)}, u32[]{:S(2)}) collective-permute-start(bf16[256,1280]{1,0:T(8,128)(2,1)S(1)} %get-tuple-element.460), channel_id=1, source_target_pairs={{0,2},{1,6},{2,0},{3,4},{4,3},{5,7},{6,1},{7,5},{8,10},{9,14},{10,... | collective-permute-start | bytes 1966088 | tf_op jit(solution)/shard_map/ppermute | solution.py:1035
  256.2 28.9 %collective-permute-start.29 = (bf16[256,1280]{1,0:T(8,128)(2,1)S(1)}, bf16[256,1280]{1,0:T(8,128)(2,1)S(1)}, u32[]{:S(2)}, u32[]{:S(2)}) collective-permute-start(bf16[256,1280]{1,0:T(8,128)(2,1)S(1)} %get-tuple-element.461), channel_id=1, source_target_pairs={{0,0},{1,4},{2,2},{3,6},{4,1},{5,5},{6,3},{7,7},{8,8},{9,12},{10,1... | collective-permute-start | bytes 1966088 | tf_op jit(solution)/shard_map/ppermute | solution.py:1035
  309.7 28.2 %collective-permute-start.34 = (bf16[512,1280]{1,0:T(8,128)(2,1)S(1)}, bf16[512,1280]{1,0:T(8,128)(2,1)S(1)}, u32[]{:S(2)}, u32[]{:S(2)}) collective-permute-start(bf16[512,1280]{1,0:T(8,128)(2,1)S(1)} %get-tuple-element.258.refs_0_), channel_id=1, source_target_pairs={{0,16},{4,20},{8,24},{12,28},{16,0},{20,4},{24,8},{28,12},{1,17},{... | collective-permute-start | bytes 3932168 | tf_op jit(solution)/shard_map/ppermute | solution.py:30
  311.2 28.5 %collective-permute-start.33 = (bf16[512,1280]{1,0:T(8,128)(2,1)S(1)}, bf16[512,1280]{1,0:T(8,128)(2,1)S(1)}, u32[]{:S(2)}, u32[]{:S(2)}) collective-permute-start(bf16[512,1280]{1,0:T(8,128)(2,1)S(1)} %get-tuple-element.258.refs_0_), channel_id=1, source_target_pairs={{0,8},{4,12},{8,0},{12,4},{16,24},{20,28},{24,16},{28,20},{1,9},{5... | collective-permute-start | bytes 3932168 | tf_op jit(solution)/shard_map/ppermute | solution.py:30
  312.7 48.3 %collective-permute-start.38 = (bf16[256,1280]{1,0:T(8,128)(2,1)S(1)}, bf16[256,1280]{1,0:T(8,128)(2,1)S(1)}, u32[]{:S(2)}, u32[]{:S(2)}) collective-permute-start(bf16[256,1280]{1,0:T(8,128)(2,1)S(1)} %get-tuple-element.458), channel_id=1, source_target_pairs={{2,0},{6,1},{0,2},{4,3},{3,4},{7,5},{1,6},{5,7},{10,8},{14,9},{8,1... | collective-permute-start | bytes 1966088 | tf_op jit(solution)/shard_map/ppermute | solution.py:1035
  314.6 46.5 %collective-permute-start.37 = (bf16[256,1280]{1,0:T(8,128)(2,1)S(1)}, bf16[256,1280]{1,0:T(8,128)(2,1)S(1)}, u32[]{:S(2)}, u32[]{:S(2)}) collective-permute-start(bf16[256,1280]{1,0:T(8,128)(2,1)S(1)} %get-tuple-element.459), channel_id=1, source_target_pairs={{0,0},{4,1},{2,2},{6,3},{1,4},{5,5},{3,6},{7,7},{8,8},{12,9},{10,1... | collective-permute-start | bytes 1966088 | tf_op jit(solution)/shard_map/ppermute | solution.py:1035
  376.8 41.1 %collective-permute-start.39 = (bf16[512,1280]{1,0:T(8,128)(2,1)}, bf16[512,1280]{1,0:T(8,128)(2,1)S(1)}, u32[]{:S(2)}, u32[]{:S(2)}) collective-permute-start(bf16[512,1280]{1,0:T(8,128)(2,1)} %pad_maximum_fusion.2), channel_id=1, source_target_pairs={{0,8},{4,12},{8,0},{12,4},{16,24},{20,28},{24,16},{28,20},{1,9},{5... | collective-permute-start | bytes 3932168 | tf_op jit(solution)/shard_map/ppermute | solution.py:30
  377.4 40.5 %collective-permute-start.40 = (bf16[512,1280]{1,0:T(8,128)(2,1)}, bf16[512,1280]{1,0:T(8,128)(2,1)}, u32[]{:S(2)}, u32[]{:S(2)}) collective-permute-start(bf16[512,1280]{1,0:T(8,128)(2,1)} %pad_maximum_fusion.3), channel_id=1, source_target_pairs={{0,16},{4,20},{8,24},{12,28},{16,0},{20,4},{24,8},{28,12},{1,17},{... | collective-permute-start | bytes 3932168 | tf_op jit(solution)/shard_map/ppermute | solution.py:30
  438.7 106.1 %reduce-scatter.5.cloned.1.call-start = ((), (), s32[]{:S(2)}) async-start(), calls=%async_computation.6 | async-start | bytes 4096000 | tf_op jit(solution)/shard_map/reduce_scatter | solution.py:1303
  517.2 23.9 %collective-permute-start.47 = (bf16[2,192,1280]{2,1,0:T(8,128)(2,1)S(1)}, bf16[2,192,1280]{2,1,0:T(8,128)(2,1)S(1)}, u32[]{:S(2)}, u32[]{:S(2)}) collective-permute-start(bf16[2,192,1280]{2,1,0:T(8,128)(2,1)S(1)} %get-tuple-element.327), channel_id=1, source_target_pairs={{0,8},{4,12},{8,0},{12,4},{16,24},{20,28},{24,16},{28,20},{1,9},{5... | collective-permute-start | bytes 2949128 | tf_op jit(solution)/shard_map/ppermute | solution.py:30
  518.1 23.9 %collective-permute-start.48 = (bf16[2,192,1280]{2,1,0:T(8,128)(2,1)S(1)}, bf16[2,192,1280]{2,1,0:T(8,128)(2,1)S(1)}, u32[]{:S(2)}, u32[]{:S(2)}) collective-permute-start(bf16[2,192,1280]{2,1,0:T(8,128)(2,1)S(1)} %get-tuple-element.328), channel_id=1, source_target_pairs={{0,16},{4,20},{8,24},{12,28},{16,0},{20,4},{24,8},{28,12},{1,17},{... | collective-permute-start | bytes 2949128 | tf_op jit(solution)/shard_map/ppermute | solution.py:30
  570.2 21.9 %collective-permute-start.52 = (bf16[2,176,1280]{2,1,0:T(8,128)(2,1)S(1)}, bf16[2,176,1280]{2,1,0:T(8,128)(2,1)S(1)}, u32[]{:S(2)}, u32[]{:S(2)}) collective-permute-start(bf16[2,176,1280]{2,1,0:T(8,128)(2,1)S(1)} %get-tuple-element.352), channel_id=1, source_target_pairs={{0,8},{4,12},{8,0},{12,4},{16,24},{20,28},{24,16},{28,20},{1,9},{5... | collective-permute-start | bytes 2703368 | tf_op jit(solution)/shard_map/ppermute | solution.py:30
  570.9 27.9 %collective-permute-start.53 = (bf16[2,176,1280]{2,1,0:T(8,128)(2,1)S(1)}, bf16[2,176,1280]{2,1,0:T(8,128)(2,1)S(1)}, u32[]{:S(2)}, u32[]{:S(2)}) collective-permute-start(bf16[2,176,1280]{2,1,0:T(8,128)(2,1)S(1)} %get-tuple-element.353), channel_id=1, source_target_pairs={{0,16},{4,20},{8,24},{12,28},{16,0},{20,4},{24,8},{28,12},{1,17},{... | collective-permute-start | bytes 2703368 | tf_op jit(solution)/shard_map/ppermute | solution.py:30
  572.9 28.4 %collective-permute-start.58 = (bf16[192,640]{1,0:T(8,128)(2,1)S(1)}, bf16[192,640]{1,0:T(8,128)(2,1)S(1)}, u32[]{:S(2)}, u32[]{:S(2)}) collective-permute-start(bf16[192,640]{1,0:T(8,128)(2,1)S(1)} %get-tuple-element.365), channel_id=1, source_target_pairs={{0,0},{1,1},{2,2},{3,3},{4,6},{5,7},{6,4},{7,5},{8,8},{9,9},{10,10... | collective-permute-start | bytes 737288 | tf_op jit(solution)/shard_map/ppermute | solution.py:1035
  573.5 28.3 %collective-permute-start.59 = (bf16[192,640]{1,0:T(8,128)(2,1)S(1)}, bf16[192,640]{1,0:T(8,128)(2,1)S(1)}, u32[]{:S(2)}, u32[]{:S(2)}) collective-permute-start(bf16[192,640]{1,0:T(8,128)(2,1)S(1)} %get-tuple-element.366), channel_id=1, source_target_pairs={{0,1},{1,2},{2,3},{3,0},{4,7},{5,4},{6,5},{7,6},{8,9},{9,10},{10,1... | collective-permute-start | bytes 737288 | tf_op jit(solution)/shard_map/ppermute | solution.py:1035
  575.8 54.9 %collective-permute-start.57 = (bf16[256,1280]{1,0:T(8,128)(2,1)}, bf16[256,1280]{1,0:T(8,128)(2,1)}, u32[]{:S(2)}, u32[]{:S(2)}) collective-permute-start(bf16[256,1280]{1,0:T(8,128)(2,1)} %get-tuple-element.454), channel_id=1, source_target_pairs={{2,0},{6,1},{0,2},{4,3},{3,4},{7,5},{1,6},{5,7},{10,8},{14,9},{8,1... | collective-permute-start | bytes 1966088 | tf_op jit(solution)/shard_map/ppermute | solution.py:1035
  592.2 38.6 %collective-permute-start.56 = (bf16[256,1280]{1,0:T(8,128)(2,1)}, bf16[256,1280]{1,0:T(8,128)(2,1)}, u32[]{:S(2)}, u32[]{:S(2)}) collective-permute-start(bf16[256,1280]{1,0:T(8,128)(2,1)} %get-tuple-element.455), channel_id=1, source_target_pairs={{0,0},{4,1},{2,2},{6,3},{1,4},{5,5},{3,6},{7,7},{8,8},{12,9},{10,1... | collective-permute-start | bytes 1966088 | tf_op jit(solution)/shard_map/ppermute | solution.py:1035
  598.7 23.5 %collective-permute-start.60 = (bf16[192,640]{1,0:T(8,128)(2,1)S(1)}, bf16[192,640]{1,0:T(8,128)(2,1)}, u32[]{:S(2)}, u32[]{:S(2)}) collective-permute-start(bf16[192,640]{1,0:T(8,128)(2,1)S(1)} %get-tuple-element.367), channel_id=1, source_target_pairs={{0,4},{1,5},{2,6},{3,7},{4,2},{5,3},{6,0},{7,1},{8,12},{9,13},{10,... | collective-permute-start | bytes 737288 | tf_op jit(solution)/shard_map/ppermute | solution.py:1035
  601.2 29.5 %collective-permute-start.54 = (bf16[176,1280]{1,0:T(8,128)(2,1)}, bf16[176,1280]{1,0:T(8,128)(2,1)}, u32[]{:S(2)}, u32[]{:S(2)}) collective-permute-start(bf16[176,1280]{1,0:T(8,128)(2,1)} %get-tuple-element.360), channel_id=1, source_target_pairs={{0,16},{4,20},{8,24},{12,28},{16,0},{20,4},{24,8},{28,12},{1,17},{... | collective-permute-start | bytes 1351688 | tf_op jit(solution)/shard_map/ppermute | solution.py:30
  602.5 28.2 %collective-permute-start.55 = (bf16[176,1280]{1,0:T(8,128)(2,1)}, bf16[176,1280]{1,0:T(8,128)(2,1)}, u32[]{:S(2)}, u32[]{:S(2)}) collective-permute-start(bf16[176,1280]{1,0:T(8,128)(2,1)} %get-tuple-element.361), channel_id=1, source_target_pairs={{0,8},{4,12},{8,0},{12,4},{16,24},{20,28},{24,16},{28,20},{1,9},{5... | collective-permute-start | bytes 1351688 | tf_op jit(solution)/shard_map/ppermute | solution.py:30
  623.0 27.7 %all-to-all-start.2 = ((bf16[4,160,640]{2,1,0:T(8,128)(2,1)}), bf16[4,160,640]{2,1,0:T(8,128)(2,1)S(1)}, u32[]{:S(2)}, u32[]{:S(2)}) async-start(bf16[4,160,640]{2,1,0:T(8,128)(2,1)} %bitcast.174), calls=%async_computation.4 | async-start | bytes 1638400 | tf_op jit(solution)/shard_map/all_to_all | solution.py:1164
  (138 other events, 1127.2 us)
Sparse Core Ops, SparseCore 0:
  113.4 63.2 all-gather.4
  178.3 42.1 all-gather.6
  438.8 42.1 reduce-scatter.2
  483.2 61.5 reduce-scatter.4

commit v3 on v2

--- a/solution.py
+++ b/solution.py
@@ -12,7 +12,7 @@
 CHIPS = 4
 LANES = 128
 HALF = 64
-EXTRA = 32
+EXTRA = 16
 BLOCK = 256
 VMEM_LIMIT = 48 * 2**20
 
@@ -436,9 +436,9 @@
     )(*lefts, *rights)
 
 
-def product(left, right, at):
+def product(left, right):
     n, depth = left.shape
-    width = right.shape[1] // 2
+    width = right.shape[1]
 
     def kernel(left_ref, right_ref, out_ref):
         out_ref[...] = nn(left_ref[...], right_ref[...]).astype(low)
@@ -446,7 +446,7 @@
     return pl.pallas_call(
         kernel,
         grid=(1,),
-        in_specs=[pl.BlockSpec((n, depth), lambda j: (0, 0)), pl.BlockSpec((depth, width), lambda j: (0, at))],
+        in_specs=[pl.BlockSpec((n, depth), lambda j: (0, 0)), pl.BlockSpec((depth, width), lambda j: (0, 0))],
         out_specs=pl.BlockSpec((n, width), lambda j: (0, 0)),
         out_shape=jax.ShapeDtypeStruct((n, width), low),
         compiler_params=params(),
@@ -520,9 +520,9 @@
 
 
 def arrived_specs(n, depth):
-    half = n // 2
-    piece = pl.BlockSpec((half, depth), lambda h, *_: (0, 0))
-    return [pl.BlockSpec((half, depth), lambda h, *_: (h, 0))] + [piece] * 4
+    block = n // 4
+    piece = pl.BlockSpec((block, depth), lambda h, r, *_: (r, 0))
+    return [pl.BlockSpec((block, depth), lambda h, r, *_: (2 * h + r, 0))] + [piece] * 4
 
 
 def arrived_sum(h, own, first, second, last_y, last_x):
@@ -532,7 +532,7 @@
 
 def settle_units(arrived, hidden, near, far, early, rate):
     n, depth = hidden.shape
-    half = n // 2
+    block = n // 4
 
     def kernel(early_ref, *refs):
         h = pl.program_id(0)
@@ -546,24 +546,26 @@
         direct_ref[...] = direct
         grad_ref[...] = grad.astype(low)
 
-        @pl.when(h == 0)
+        start = (h == 0) & (pl.program_id(1) == 0)
+
+        @pl.when(start)
         def _():
             term_ref[...] = rate_rows(terms)
 
-        @pl.when(h != 0)
+        @pl.when(jnp.logical_not(start))
         def _():
             term_ref[...] += rate_rows(terms)
 
-    rows = pl.BlockSpec((half, depth), lambda h, *_: (h, 0))
-    piece = pl.BlockSpec((half, depth), lambda h, *_: (0, 0))
+    rows = pl.BlockSpec((block, depth), lambda h, r, *_: (2 * h + r, 0))
+    piece = pl.BlockSpec((block, depth), lambda h, r, *_: (r, 0))
     return pl.pallas_call(
         kernel,
         grid_spec=pltpu.PrefetchScalarGridSpec(
             num_scalar_prefetch=1,
-            grid=(2,),
+            grid=(2, 2),
             in_specs=arrived_specs(n, depth)
-            + [rows, piece, piece, pl.BlockSpec((1, depth), lambda h, *_: (0, 0))],
-            out_specs=[rows, rows, rows, pl.BlockSpec((8, depth), lambda h, *_: (0, 0))],
+            + [rows, piece, piece, pl.BlockSpec((1, depth), lambda h, r, *_: (0, 0))],
+            out_specs=[rows, rows, rows, pl.BlockSpec((8, depth), lambda h, r, *_: (0, 0))],
         ),
         out_shape=[
             jax.ShapeDtypeStruct((n, depth), low),
@@ -578,7 +580,7 @@
 
 def settle_attention_back(arrived, direct, hidden, tokens, branch, rate):
     n, depth = hidden.shape
-    half = n // 2
+    block = n // 4
 
     def kernel(*refs):
         h = pl.program_id(0)
@@ -590,20 +592,22 @@
         out_ref[...] = back
         grad_ref[...] = branch_grad.astype(low)
 
-        @pl.when(h == 0)
+        start = (h == 0) & (pl.program_id(1) == 0)
+
+        @pl.when(start)
         def _():
             term_ref[...] = rate_rows(terms)
 
-        @pl.when(h != 0)
+        @pl.when(jnp.logical_not(start))
         def _():
             term_ref[...] += rate_rows(terms)
 
-    rows = pl.BlockSpec((half, depth), lambda h: (h, 0))
-    return pl.pallas_call(
-        kernel,
-        grid=(2,),
-        in_specs=arrived_specs(n, depth) + [rows] * 3 + [pl.BlockSpec((1, depth), lambda h: (0, 0))],
-        out_specs=[rows, rows, pl.BlockSpec((8, depth), lambda h: (0, 0))],
+    rows = pl.BlockSpec((block, depth), lambda h, r: (2 * h + r, 0))
+    return pl.pallas_call(
+        kernel,
+        grid=(2, 2),
+        in_specs=arrived_specs(n, depth) + [rows] * 3 + [pl.BlockSpec((1, depth), lambda h, r: (0, 0))],
+        out_specs=[rows, rows, pl.BlockSpec((8, depth), lambda h, r: (0, 0))],
         out_shape=[
             jax.ShapeDtypeStruct((n, depth), wide),
             jax.ShapeDtypeStruct((n, depth), low),
@@ -1096,7 +1100,11 @@
 
     def attn_fetch_packed(packed, rows):
         groups = [across(packed, head_pairs(0, which)) for which in range(2)]
-        return paired(*(group[:, :rows] for group in groups)), [group[0, rows:] for group in groups]
+        sides = [
+            paired(*(group[:, :rows, at : at + head_width] for group in groups))
+            for at in range(0, packed.shape[2], head_width)
+        ]
+        return *sides, [group[0, rows:] for group in groups]
 
     def attn_first(sides):
         return sides, swap(sides, 2), swap(sides, 4)
@@ -1105,14 +1113,8 @@
         sides, along_x, along_y = first
         return sides, along_x, along_y, swap(along_y[0], 2), swap(along_x[1], 4)
 
-    def attn_lay(gathered):
-        sides, along_x, along_y, d_own, d_other = gathered
-        return full_rows(
-            place(
-                [sides, along_x, along_y, d_own, d_other],
-                [2 * (chip ^ (i // 2)) + (core ^ (i % 2)) for i in range(8)],
-            )
-        )
+    def attn_lay(blocks):
+        return full_rows(place(blocks, [2 * (chip ^ (i // 2)) + (core ^ (i % 2)) for i in range(8)]))
 
     def attn_pack(packed, extra):
         grad = plane_rows(packed).reshape(CHIPS, 2, -1, packed.shape[1])
@@ -1170,7 +1172,7 @@
         return jnp.stack([upper_part, value - upper_part]).astype(low)
 
     qk_sides = attn_fetch(w_query, w_key)
-    unit_blocks = unit_pack([[outer_gather(w_up), outer_gather(w_gate)], [outer_gather(w_down)]])
+    unit_blocks = unit_pack([[outer_gather(w_up), outer_gather(w_gate)]])
     mains = lax.dynamic_slice_in_dim(jnp.stack([up_gain, gate_gain]), chip * main, main, 1)
     rests = lax.dynamic_slice_in_dim(jnp.stack([up_gain, gate_gain]), CHIPS * main + chip * rest, rest, 1)
     unit_gains = halved(jnp.concatenate([mains, rests], axis=1).reshape(-1))
@@ -1178,32 +1180,33 @@
         [unit_gains, halved(qk_gain).reshape(1, -1), jnp.zeros((13, 2 * head_width), low)]
     )
     vo_packed = attn_pair(w_value, w_out, gain_rows)
-    unit_blocks = lax.all_to_all(unit_blocks, "chip", 0, 0, tiled=True)
     places_here = global_pos[:, 0]
     places_there = swap(places_here, 1)
     qk_sides, vo_packed, places_there, unit_blocks, block_in = tie(
         (qk_sides, vo_packed, places_there, unit_blocks, block_in)
     )
     qk_first = attn_first(qk_sides)
-    vo_sides, gain_groups = attn_fetch_packed(vo_packed, qk_sides.shape[1])
+    value_sides, out_sides, gain_groups = attn_fetch_packed(vo_packed, qk_sides.shape[1])
     near = seq_near(block_in[:, 0])
-    ug_columns = 2 * main + LANES
-    ug_laid, down_laid = unit_blocks[..., :ug_columns], unit_blocks[..., ug_columns:]
-    qk_first, vo_sides, gain_groups, near, block_in, ug_laid, down_laid = tie(
-        (qk_first, vo_sides, gain_groups, near, block_in, ug_laid, down_laid)
-    )
-    far = seq_far(block_in[:, 0])
+    qk_first, value_sides, out_sides, gain_groups, near, block_in, unit_blocks = tie(
+        (qk_first, value_sides, out_sides, gain_groups, near, block_in, unit_blocks)
+    )
+    ug_laid = lax.all_to_all(unit_blocks, "chip", 0, 0, tiled=True)
+    lower, upper_rows = block_in[:, 0, : local_rows // 2], block_in[:, 0, local_rows // 2 :]
+    far_first, upper_rows = tie((seq_far(lower), upper_rows))
+    far = jnp.concatenate([far_first, seq_far(upper_rows)])
     qk_w = attn_lay(attn_second(qk_first))
-    vo_w = attn_lay(attn_second(attn_first(vo_sides)))
+    value_w = attn_lay(attn_second(attn_first(value_sides)))
+    qk_w, value_w, out_sides, gain_groups, far, near, ug_laid, w_down = tie(
+        (qk_w, value_w, out_sides, gain_groups, far, near, ug_laid, w_down)
+    )
+    down_laid = lax.all_to_all(unit_pack([[outer_gather(w_down)]]), "chip", 0, 0, tiled=True)
     gain_here = jnp.stack(gain_groups)[:, :2].astype(wide).sum(axis=1)
     gain_there = swap(gain_here, 1)
-    qk_w, vo_w, gain_there, far, near, ug_laid, down_laid = tie(
-        (qk_w, vo_w, gain_there, far, near, ug_laid, down_laid)
-    )
+    out_across = [out_sides] + [swap(out_sides, 2 * k) for k in range(1, CHIPS)]
     tokens = seq_join(near, far)
     sequence = both_cores(tokens)
     ug_shifted = lax.all_gather(ug_laid, "tensor")
-    down_shifted = lax.all_gather(down_laid, "tensor")
     unit_gains = pick(
         core == 0, jnp.concatenate([gain_here, gain_there]), jnp.concatenate([gain_there, gain_here])
     )
@@ -1221,9 +1224,12 @@
     flag_row, flag_col = flags[None], flags[:, None]
 
     heads, raw = project_heads(sequence, qk_w, jnp.concatenate([head_gain, head_gain]))
-    value_rows = product(sequence, vo_w, 0)
+    value_rows = product(sequence, value_w)
     mixed, lse = attend_forward(heads, value_rows, flag_row, flag_col)
-    partial = sum_back([(mixed, 0, core_heads)], [(vo_w, 1, core_heads)])
+    mixed, out_across, down_laid = tie((mixed, out_across, down_laid))
+    down_shifted = lax.all_gather(down_laid, "tensor")
+    out_w = attn_lay(out_across)
+    partial = sum_back([(mixed, 0, core_heads)], [(out_w, 0, core_heads)])
     partial = partial.reshape(2, 2, local_rows, model_width)
     got = swap(lax.dynamic_index_in_dim(partial, 1 - core, 1, keepdims=False), 1)
     hidden, hidden_low, att_branch = settle_attention(partial, got, tokens, att_rate, core)
@@ -1287,11 +1293,28 @@
     sent, (branch, mid) = scatter_first(by_chip(part_own, part_both, part_diagonal), (branch, mid))
     down_blocks = unit_unlay(plane_rows(rows_product([(branch, [activated])], 2 * LANES)), 1, core)
     ug_grad = rows_product([(mid, [up_low, gate_low])], 2 * LANES)
-    sent, down_blocks, ug_grad = tie((sent, down_blocks, ug_grad))
+    small = jnp.concatenate([sum(unit_terms), mlp_rate_term[:1]])
+    small = small + swap(small, 1)
+    sent, down_blocks, ug_grad, small = tie((sent, down_blocks, ug_grad, small))
     arrived = scatter_last(sent)
     down_blocks = add_low(down_blocks[0], swap(down_blocks[1], 1))
     ug_blocks = unit_unlay(plane_rows(ug_grad), 2, core)
-    arrived, ug_blocks, down_blocks = tie((arrived, ug_blocks, down_blocks))
+    def rate_rows_of(term):
+        rows = jnp.broadcast_to(term.reshape(2, 2, 1, head_width), (2, 2, 2, head_width))
+        return jnp.where(own_chip[..., None], rows.reshape(1, 2, 4 * head_width), 0.0).reshape(2 * CHIPS, -1)
+
+    own_chip = jnp.arange(CHIPS)[:, None] == chip
+    empty_rows = jnp.zeros((EXTRA - 3 * CHIPS, 4 * head_width), wide)
+    unit_rows = jnp.concatenate(
+        [small[:2, : count * main].reshape(2, count, main), small[:2, count * main :].reshape(2, count, rest)],
+        axis=2,
+    )
+    unit_rows = lax.dynamic_slice_in_dim(
+        jnp.concatenate([unit_rows, unit_rows], axis=1), z + 2 * core, 2, 1
+    ).reshape(1, 4 * plane_unit)
+    vo_extra = jnp.concatenate([jnp.where(own_chip, unit_rows, 0.0), rate_rows_of(small[2:]), empty_rows])
+    vo_extra = vo_extra.astype(low)
+    arrived, ug_blocks, down_blocks, vo_extra = tie((arrived, ug_blocks, down_blocks, vo_extra))
     down_back = lax.psum_scatter(down_blocks, "tensor", scatter_dimension=0)
     ug_there = swap(ug_blocks[1], 1)
     input_direct, att_grad, att_rate_term = settle_attention_back(
@@ -1301,53 +1324,30 @@
     ug_blocks = add_low(ug_blocks[0], ug_there)
     att_low, ug_blocks = tie((att_low, ug_blocks))
     ug_back = lax.psum_scatter(ug_blocks, "tensor", scatter_dimension=0)
-    mixed_grad = product(att_low, vo_w, 1)
+    mixed_grad = product(att_low, out_w)
     heads_low, vraw_low, head_terms = attend_backward(
         heads, raw, value_rows, mixed, mixed_grad, lse, head_gain, flag_row, flag_col
     )
     block_out = by_micro(*returned)
 
-    small = jnp.concatenate(
-        [
-            sum(unit_terms),
-            att_rate_term[:1],
-            mlp_rate_term[:1],
-        ]
-    )
-    small = small + swap(small, 1)
-    unit_rows = jnp.concatenate(
-        [small[:2, : count * main].reshape(2, count, main), small[:2, count * main :].reshape(2, count, rest)],
-        axis=2,
-    )
-    unit_rows = lax.dynamic_slice_in_dim(
-        jnp.concatenate([unit_rows, unit_rows], axis=1), z + 2 * core, 2, 1
-    ).reshape(1, 4 * plane_unit)
-    rate_rows = jnp.broadcast_to(small[2:].reshape(4, 2, 1, head_width), (4, 2, 2, head_width))
-    rate_rows = rate_rows.reshape(1, 4, 4 * head_width)
-    own_chip = jnp.arange(CHIPS)[:, None] == chip
-    vo_extra = jnp.concatenate(
-        [
-            jnp.where(own_chip, unit_rows, 0.0),
-            jnp.where(own_chip[..., None], rate_rows, 0.0).reshape(4 * CHIPS, -1),
-            jnp.zeros((EXTRA - 5 * CHIPS, 4 * head_width), wide),
-        ]
-    )
-    qk_extra = jnp.concatenate(
-        [
-            jnp.where(own_chip, head_terms[:2].reshape(1, 4 * head_width), 0.0),
-            jnp.zeros((EXTRA // 2 - CHIPS, 4 * head_width), wide),
-        ]
-    )
     heads_low, vraw_low, down_back = tie((heads_low, vraw_low, down_back))
     vo_grad = rows_product([(sequence, [vraw_low]), (att_low, [mixed])], core_heads)
     vo_messages, vraw_low = tie((attn_pack(vo_grad, vo_extra), vraw_low))
     vo_sent = attn_send(vo_messages)
     in_part = sum_back(
         [(heads_low, 0, 2 * core_heads), (vraw_low, 0, core_heads)],
-        [(qk_w, 0, 2 * core_heads), (vo_w, 0, core_heads)],
+        [(qk_w, 0, 2 * core_heads), (value_w, 0, core_heads)],
     )
     vo_sent, heads_low, in_part, ug_back, block_out = tie((vo_sent, heads_low, in_part, ug_back, block_out))
-    vo_messages, heads_low, in_part = tie((spread_turn(*vo_sent), heads_low, in_part))
+    att_term = att_rate_term[:1] + swap(att_rate_term[:1], 1)
+    vo_messages, heads_low, in_part, att_term = tie((spread_turn(*vo_sent), heads_low, in_part, att_term))
+    qk_extra = jnp.concatenate(
+        [
+            jnp.where(own_chip, head_terms[:2].reshape(1, 4 * head_width), 0.0),
+            rate_rows_of(att_term),
+            empty_rows,
+        ]
+    )
     vo_turned = attn_turn(vo_messages)
     in_rows = (input_direct + core_scatter(in_part)).astype(low)
     qk_messages = attn_pack(rows_product([(sequence, [heads_low])], 2 * LANES), qk_extra)
@@ -1362,18 +1362,21 @@
     qk_got = attn_scatter(qk_sent, qk_turned)
     grad_up, grad_gate = unit_return(2, ug_back)
     in_grad = by_micro(*returned_in)
+    vo_got, qk_got = tie((vo_got, qk_got))
     grad_value, grad_out, vo_small = attn_join(vo_got, EXTRA)
-    grad_query, grad_key, qk_small = attn_join(qk_got, EXTRA // 2)
+    grad_query, grad_key, qk_small = attn_join(qk_got, EXTRA)
 
     units = vo_small[:CHIPS].reshape(CHIPS, 2, plane_unit).transpose(1, 0, 2)
     units = jnp.concatenate([units[..., :main].reshape(2, -1), units[..., main:].reshape(2, -1)], axis=1)
-    rates = jnp.sum(vo_small[CHIPS : 5 * CHIPS].reshape(CHIPS, 2, model_width), axis=0)
+    mlp_total, att_total = (
+        jnp.sum(member[CHIPS : 3 * CHIPS].reshape(CHIPS, model_width), axis=0) for member in (vo_small, qk_small)
+    )
     head_sums = jnp.sum(qk_small[:CHIPS], axis=0)
     grad_qk_gain = head_sums[:head_width] + head_sums[head_width:]
     return (
         block_out[:, None], in_grad[:, None],
         grad_query, grad_key, grad_value, grad_out, grad_up, grad_gate, grad_down,
-        grad_qk_gain, units[0], units[1], rates[0], rates[1],
+        grad_qk_gain, units[0], units[1], att_total, mlp_total,
     )
 
 

time: 678 us -> 670 us (0.988)
  waiting for transfers between devices: 181 us -> 140 us
  starting transfers between devices: 91.3 us -> 111 us
  Pallas kernels: 286 us -> 294 us
    ppermute x44 -> x48, waiting for transfers between devices: 102 us -> 53.4 us  [swap(): return lax.ppermute(value, DP, [(i, i ^ bit) for i in range(count)])]
    ppermute x22 -> x23, waiting for transfers between devices: 54.3 us -> 75.6 us  [across(): lax.ppermute(value, ALL, [(a * count + b, c * count + d) for (a, b), (c,...]
    all_to_all x1 -> x2, waiting for transfers between devices: 13.7 us -> 0.01 us  [the longest x1 0.01 us: per_device(): ug_laid = lax.all_to_all(unit_blocks, 'chip', 0, 0, tiled=True)]
    ppermute x44 -> x48, starting transfers between devices: 34.6 us -> 46.8 us  [swap(): return lax.ppermute(value, DP, [(i, i ^ bit) for i in range(count)])]
    all_gather x1, waiting for transfers between devices: 9.79 us -> 2.87 us  [per_device(): ug_shifted = lax.all_gather(ug_laid, 'tensor')]
    ppermute x22 -> x23, starting transfers between devices: 44.2 us -> 48.6 us  [across(): lax.ppermute(value, ALL, [(a * count + b, c * count + d) for (a, b), (c,...]
    unnamed x197 -> x173, local copies, waits for them, and re-layouts: 38.6 us -> 41.7 us
  transfers between devices with their start and end apart: 73 -> 79, of which waited for: 29 -> 26; matrix products, arithmetic and copies ran while one was open for 7% -> 7% of each run, Pallas kernels for 38% -> 39%
where the time goes in v3:
time: 670 us; the launch traced here: 661 us
  Pallas kernels  294 us (44%)
  waiting for transfers between devices  140 us (21%)
  starting transfers between devices  111 us (17%)
  local copies, waits for them, and re-layouts  64.4 us (10%)
  other arithmetic  35.7 us (5%)
  between operations  15.8 us (2%)
    ppermute x23, waiting for transfers between devices, across(): lax.ppermute(value, ALL, [(a * count + b, c * count + d) for (a, b), (c,...  75.6 us
    ppermute x48, waiting for transfers between devices, swap(): return lax.ppermute(value, DP, [(i, i ^ bit) for i in range(count)])  53.4 us
    pallas_call x4, Pallas kernels, rows_product(): pl.pallas_call(kernel, grid=(sum(steps),), in_specs=[pl.BlockSpec((n, dep...  49 us
    ppermute x23, starting transfers between devices, across(): lax.ppermute(value, ALL, [(a * count + b, c * count + d) for (a, b), (c,...  48.6 us
    ppermute x48, starting transfers between devices, swap(): return lax.ppermute(value, DP, [(i, i ^ bit) for i in range(count)])  46.8 us
    pallas_call x3, Pallas kernels, mlp_backward(): pl.pallas_call(kernel, grid=(steps,), in_specs=chunk_specs(blocks, depth)...  44.5 us
    unnamed x173, local copies, waits for them, and re-layouts  41.7 us
    pallas_call x1, Pallas kernels, attend_backward(): pl.pallas_call(kernel, grid=(pairs,), in_specs=[block, keys, block, block...  28.8 us
  transfers between devices with their start and end apart: 79, of which 26 were waited for; matrix products, arithmetic and copies ran while one was open for 7% of the time, Pallas kernels for 39%

profile of v3, /device:TPU:0, one launch (start us, length us, event | category | flops | bytes accessed | tf_op | source)
XLA Modules:
  0.0 661.2 jit_solution(1288489618441994469)
XLA Ops:
  35.4 11.8 %collective-permute-done.9 = bf16[2,176,640]{2,1,0:T(8,128)(2,1)S(1)} collective-permute-done((bf16[2,176,640]{2,1,0:T(8,128)(2,1)}, bf16[2,176,640]{2,1,0:T(8,128)(2,1)S(1)}, u32[]{:S(2)}, u32[]{:S(2)}) %collective-permute-start.9) | collective-permute-done | bytes 450592 | tf_op jit(solution)/shard_map/ppermute | solution.py:1039
  60.0 7.0 %collective-permute-start.17 = (bf16[128,1280]{1,0:T(8,128)(2,1)S(1)}, bf16[128,1280]{1,0:T(8,128)(2,1)S(1)}, u32[]{:S(2)}, u32[]{:S(2)}) collective-permute-start(bf16[128,1280]{1,0:T(8,128)(2,1)S(1)} %dynamic-slice_bitcast_fusion.6), channel_id=1, source_target_pairs={{0,2},{1,6},{2,0},{3,4},{4,3},{5,7},{6,1},{7,5},{8,10},{9,14},{10,... | collective-permute-start | bytes 983048 | tf_op jit(solution)/shard_map/ppermute | solution.py:1039
  71.2 9.6 %collective-permute-done.17 = bf16[128,1280]{1,0:T(8,128)(2,1)S(1)} collective-permute-done((bf16[128,1280]{1,0:T(8,128)(2,1)S(1)}, bf16[128,1280]{1,0:T(8,128)(2,1)S(1)}, u32[]{:S(2)}, u32[]{:S(2)}) %collective-permute-start.17) | collective-permute-done | bytes 327712 | tf_op jit(solution)/shard_map/ppermute | solution.py:1039
  117.1 11.6 %shard_map.258 = (bf16[1024,1280]{1,0:T(8,128)(2,1)S(1)}, bf16[1024,1280]{1,0:T(8,128)(2,1)S(1)}) custom-call(bf16[1024,1280]{1,0:T(8,128)(2,1)} %bitcast.132, bf16[1280,1280]{1,0:T(8,128)(2,1)} %bitcast.166, f32[1,1280]{1,0:T(1,128)S(1)} %broadcast_in_dim.116.gain_ref), custom_call_target="tpu_custom_call" | custom-call | flops 1 | bytes 1 | tf_op jit(solution)/shard_map/pallas_call | solution.py:163
  130.3 15.6 %shard_map.260 = (bf16[1024,640]{1,0:T(8,128)(2,1)S(1)}, f32[5,8,1024]{2,1,0:T(8,128)S(1)}) custom-call(bf16[1024,1280]{1,0:T(8,128)(2,1)S(1)} %get-tuple-element.242.q_ref.k_ref, bf16[1024,1280]{1,0:T(8,128)(2,1)S(1)} %get-tuple-element.242.q_ref.k_ref, bf16[1024,640]{1,0:T(8,128)(2,1)S(1)} %shard_map.259.v_ref, f32[1,1024]{1,0:T(1,128)S(1)} %bitcast.158, ...), custom_call_target="tpu_custom_call" | custom-call | flops 1 | bytes 1 | tf_op jit(solution)/shard_map/pallas_call | solution.py:225
  179.2 8.0 %shard_map.266 = (bf16[2048,1280]{1,0:T(8,128)(2,1)}, bf16[2048,1280]{1,0:T(8,128)(2,1)}, bf16[512,1280]{1,0:T(8,128)(2,1)S(1)}, bf16[512,1280]{1,0:T(8,128)(2,1)S(1)}, bf16[512,1280]{1,0:T(8,128)(2,1)S(1)}) custom-call(bf16[512,1280]{1,0:T(8,128)(2,1)} %get-tuple-element.255.refs_0_, bf16[1280,1280]{1,0:T(8,128)(2,1)} %bitcast.125, ...), custom_call_target="tpu_custom_call" | custom-call | flops 1 | bytes 1 | tf_op jit(solution)/shard_map/pallas_call | solution.py:653
  188.3 8.8 %collective-permute-done.25.refs_1_ = bf16[512,1280]{1,0:T(8,128)(2,1)S(1)} collective-permute-done((bf16[512,1280]{1,0:T(8,128)(2,1)}, bf16[512,1280]{1,0:T(8,128)(2,1)S(1)}, u32[]{:S(2)}, u32[]{:S(2)}) %collective-permute-start.25) | collective-permute-done | bytes 1310752 | tf_op jit(solution)/shard_map/ppermute | solution.py:30
  202.1 11.3 %shard_map.267 = (bf16[2048,1280]{1,0:T(8,128)(2,1)}, bf16[2048,1280]{1,0:T(8,128)(2,1)}, bf16[1024,1280]{1,0:T(8,128)(2,1)S(1)}, bf16[1024,1280]{1,0:T(8,128)(2,1)}, bf16[1024,1280]{1,0:T(8,128)(2,1)}) custom-call(bf16[512,1280]{1,0:T(8,128)(2,1)S(1)} %collective-permute-done.24.refs_0_, ...), custom_call_target="tpu_custom_call", output_to_operand_aliasing={{0}: (5, {}), {1}: (6, {})} | custom-call | flops 1 | bytes 1 | tf_op jit(solution)/shard_map/pallas_call | solution.py:653
  216.9 8.1 %shard_map.271 = (bf16[2048,1280]{1,0:T(8,128)(2,1)}, bf16[2048,1280]{1,0:T(8,128)(2,1)}, bf16[512,1280]{1,0:T(8,128)(2,1)S(1)}, bf16[512,1280]{1,0:T(8,128)(2,1)S(1)}, bf16[512,1280]{1,0:T(8,128)(2,1)S(1)}) custom-call(bf16[256,1280]{1,0:T(8,128)(2,1)} %collective-permute-done.28.refs_0_, ...), custom_call_target="tpu_custom_call", output_to_operand_aliasing={{0}: (5, {}), {1}: (6, {})} | custom-call | flops 1 | bytes 1 | tf_op jit(solution)/shard_map/pallas_call | solution.py:653
  228.6 6.1 shard_map.270
  246.9 28.0 %collective-permute-done.34.refs_7_ = bf16[256,1280]{1,0:T(8,128)(2,1)S(1)} collective-permute-done((bf16[256,1280]{1,0:T(8,128)(2,1)S(1)}, bf16[256,1280]{1,0:T(8,128)(2,1)S(1)}, u32[]{:S(2)}, u32[]{:S(2)}) %collective-permute-start.34) | collective-permute-done | bytes 655392 | tf_op jit(solution)/shard_map/ppermute | solution.py:1039
  279.7 12.9 %collective-permute-done.36.refs_4_ = bf16[256,1280]{1,0:T(8,128)(2,1)S(1)} collective-permute-done((bf16[256,1280]{1,0:T(8,128)(2,1)}, bf16[256,1280]{1,0:T(8,128)(2,1)S(1)}, u32[]{:S(2)}, u32[]{:S(2)}) %collective-permute-start.36) | collective-permute-done | bytes 655392 | tf_op jit(solution)/shard_map/ppermute | solution.py:30
  294.0 6.7 %shard_map.273 = (bf16[512,1280]{1,0:T(8,128)(2,1)S(1)}, f32[512,1280]{1,0:T(8,128)}, bf16[512,1280]{1,0:T(8,128)(2,1)S(1)}, f32[8,1280]{1,0:T(8,128)S(1)}) custom-call(s32[1]{0:T(128)} %bitcast.32.early_ref, bf16[512,1280]{1,0:T(8,128)(2,1)} %copy-done.27, bf16[512,1280]{1,0:T(8,128)(2,1)} %copy-done.67, bf16[512,1280]{1,0:T(8,128)(2,1)} %copy-done.68, ...), custom_call_target="tpu_custom_call" | custom-call | flops 1 | bytes 1 | tf_op jit(solution)/shard_map/pallas_call | solution.py:561
  306.4 6.9 %collective-permute-start.41 = (bf16[256,1280]{1,0:T(8,128)(2,1)}, bf16[256,1280]{1,0:T(8,128)(2,1)}, u32[]{:S(2)}, u32[]{:S(2)}) collective-permute-start(bf16[256,1280]{1,0:T(8,128)(2,1)} %get-tuple-element.499), channel_id=1, source_target_pairs={{0,0},{4,1},{2,2},{6,3},{1,4},{5,5},{3,6},{7,7},{8,8},{12,9},{10,1... | collective-permute-start | bytes 1966088 | tf_op jit(solution)/shard_map/ppermute | solution.py:1039
  313.4 12.3 %shard_map.274 = (bf16[2048,1280]{1,0:T(8,128)(2,1)}, bf16[2048,1280]{1,0:T(8,128)(2,1)}, bf16[2048,1280]{1,0:T(8,128)(2,1)}, bf16[512,1280]{1,0:T(8,128)(2,1)S(1)}, f32[8,1280]{1,0:T(8,128)S(1)}) custom-call(bf16[512,1280]{1,0:T(8,128)(2,1)S(1)} %get-tuple-element.289.refs_0_, bf16[1280,1280]{1,0:T(8,128)(2,1)} %bitcast.120, ...), custom_call_target="tpu_custom_call" | custom-call | flops 1 | bytes 1 | tf_op jit(solution)/shard_map/pallas_call | solution.py:726
  334.2 19.4 %shard_map.275 = (bf16[2048,1280]{1,0:T(8,128)(2,1)}, bf16[2048,1280]{1,0:T(8,128)(2,1)}, bf16[2048,1280]{1,0:T(8,128)(2,1)}, bf16[1024,1280]{1,0:T(8,128)(2,1)S(1)}, f32[8,1280]{1,0:T(8,128)S(1)}) custom-call(bf16[512,1280]{1,0:T(8,128)(2,1)S(1)} %collective-permute-done.37.refs_0_, ...), custom_call_target="tpu_custom_call", output_to_operand_aliasing={{0}: (8, {}), {1}: (9, {}), {2}: (10, {})} | custom-call | flops 1 | bytes 1 | tf_op jit(solution)/shard_map/pallas_call | solution.py:726
  353.6 12.9 %shard_map.276 = (bf16[2048,1280]{1,0:T(8,128)(2,1)}, bf16[2048,1280]{1,0:T(8,128)(2,1)}, bf16[2048,1280]{1,0:T(8,128)(2,1)}, bf16[512,1280]{1,0:T(8,128)(2,1)S(1)}, f32[8,1280]{1,0:T(8,128)S(1)}) custom-call(bf16[256,1280]{1,0:T(8,128)(2,1)} %collective-permute-done.39.refs_0_, ...), custom_call_target="tpu_custom_call", output_to_operand_aliasing={{0}: (8, {}), {1}: (9, {}), {2}: (10, {})} | custom-call | flops 1 | bytes 1 | tf_op jit(solution)/shard_map/pallas_call | solution.py:726
  370.7 12.5 %shard_map.277 = bf16[1280,1280]{1,0:T(8,128)(2,1)S(1)} custom-call(bf16[2048,1280]{1,0:T(8,128)(2,1)} %get-tuple-element.316.refs_0_, bf16[2048,1280]{1,0:T(8,128)(2,1)} %get-tuple-element.317.refs_1_), custom_call_target="tpu_custom_call" | custom-call | flops 1 | bytes 1 | tf_op jit(solution)/shard_map/pallas_call | solution.py:426
  388.3 21.1 %shard_map.279 = bf16[1280,2560]{1,0:T(8,128)(2,1)} custom-call(bf16[2048,1280]{1,0:T(8,128)(2,1)S(1)} %bitcast.136, bf16[2048,1280]{1,0:T(8,128)(2,1)} %get-tuple-element.321.refs_1_, bf16[2048,1280]{1,0:T(8,128)(2,1)} %get-tuple-element.322.refs_2_), custom_call_target="tpu_custom_call" | custom-call | flops 1 | bytes 1 | tf_op jit(solution)/shard_map/pallas_call | solution.py:426
  414.8 5.7 shard_map.280
  422.4 5.8 shard_map.281
  434.0 7.5 %shard_map.282 = (f32[512,1280]{1,0:T(8,128)}, bf16[512,1280]{1,0:T(8,128)(2,1)S(1)}, f32[8,1280]{1,0:T(8,128)S(1)}) custom-call(bf16[512,1280]{1,0:T(8,128)(2,1)S(1)} %copy-done.55, bf16[512,1280]{1,0:T(8,128)(2,1)S(1)} %collective-permute-done.43.refs_1_, bf16[512,1280]{1,0:T(8,128)(2,1)} %collective-permute-done.44.refs_2_, ...), custom_call_target="tpu_custom_call" | custom-call | flops 1 | bytes 1 | tf_op jit(solution)/shard_map/pallas_call | solution.py:606
  459.0 28.8 %shard_map.286 = (bf16[1024,1280]{1,0:T(8,128)(2,1)}, bf16[1024,640]{1,0:T(8,128)(2,1)S(1)}, f32[8,640]{1,0:T(8,128)S(1)}) custom-call(bf16[1024,1280]{1,0:T(8,128)(2,1)} %copy-done.4, bf16[1024,1280]{1,0:T(8,128)(2,1)} %copy-done.4, bf16[1024,640]{1,0:T(8,128)(2,1)S(1)} %copy-done.15, bf16[1024,1280]{1,0:T(8,128)(2,1)} %copy-done.23, ...), custom_call_target="tpu_custom_call" | custom-call | flops 1 | bytes 1 | tf_op jit(solution)/shard_map/pallas_call | solution.py:325
  491.4 9.3 %shard_map.287 = bf16[1280,1280]{1,0:T(8,128)(2,1)} custom-call(bf16[1024,1280]{1,0:T(8,128)(2,1)S(1)} %bitcast.133, bf16[1024,1280]{1,0:T(8,128)(2,1)} %bitcast.138, bf16[1024,640]{1,0:T(8,128)(2,1)S(1)} %copy-done.29, bf16[1024,640]{1,0:T(8,128)(2,1)S(1)} %copy-done.18), custom_call_target="tpu_custom_call" | custom-call | flops 1 | bytes 1 | tf_op jit(solution)/shard_map/pallas_call | solution.py:426
  515.6 8.5 %shard_map.289 = bf16[1024,1280]{1,0:T(8,128)(2,1)S(1)} custom-call(bf16[1024,1280]{1,0:T(8,128)(2,1)} %get-tuple-element.380.refs_0_.refs_1_, bf16[1024,640]{1,0:T(8,128)(2,1)S(1)} %copy-done.30, bf16[1280,1280]{1,0:T(8,128)(2,1)} %bitcast.167, bf16[1280,640]{1,0:T(8,128)(2,1)S(1)} %bitcast.146), custom_call_target="tpu_custom_call" | custom-call | flops 1 | bytes 1 | tf_op jit(solution)/shard_map/pallas_call | solution.py:364
  529.8 8.3 %reduce-scatter.5.cloned.1.call-done = bf16[1,4,160,640]{3,2,1,0:T(8,128)(2,1)} async-done(((bf16[4,4,160,640]{3,2,1,0:T(8,128)(2,1)}), bf16[1,4,160,640]{3,2,1,0:T(8,128)(2,1)}) %reduce-scatter.5.cloned.1.call-update) | async-done | bytes 819216 | tf_op jit(solution)/shard_map/reduce_scatter | solution.py:1326
  547.9 6.2 shard_map.291
  572.5 10.2 %collective-permute-done.57.first_ref = bf16[2,176,1280]{2,1,0:T(8,128)(2,1)S(1)} collective-permute-done((bf16[2,176,1280]{2,1,0:T(8,128)(2,1)S(1)}, bf16[2,176,1280]{2,1,0:T(8,128)(2,1)S(1)}, u32[]{:S(2)}, u32[]{:S(2)}) %collective-permute-start.57) | collective-permute-done | bytes 901152 | tf_op jit(solution)/shard_map/ppermute | solution.py:30
  582.8 6.5 collective-permute-start.61
  604.9 8.3 %collective-permute-done.65 = bf16[176,640]{1,0:T(8,128)(2,1)} collective-permute-done((bf16[176,640]{1,0:T(8,128)(2,1)}, bf16[176,640]{1,0:T(8,128)(2,1)}, u32[]{:S(2)}, u32[]{:S(2)}) %collective-permute-start.65) | collective-permute-done | bytes 225312 | tf_op jit(solution)/shard_map/ppermute | solution.py:1039
  615.2 6.1 collective-permute-done.66
  636.2 9.1 %collective-permute-done.69 = bf16[176,640]{1,0:T(8,128)(2,1)S(1)} collective-permute-done((bf16[176,640]{1,0:T(8,128)(2,1)}, bf16[176,640]{1,0:T(8,128)(2,1)S(1)}, u32[]{:S(2)}, u32[]{:S(2)}) %collective-permute-start.69) | collective-permute-done | bytes 225312 | tf_op jit(solution)/shard_map/ppermute | solution.py:1039
  (516 shorter events, 294.5 us)
Async XLA Ops:
  50.5 31.1 %collective-permute-start.14 = (bf16[2,160,640]{2,1,0:T(8,128)(2,1)S(1)}, bf16[2,160,640]{2,1,0:T(8,128)(2,1)S(1)}, u32[]{:S(2)}, u32[]{:S(2)}) collective-permute-start(bf16[2,160,640]{2,1,0:T(8,128)(2,1)S(1)} %get-tuple-element.228.refs_0_), channel_id=1, source_target_pairs={{0,16},{4,20},{8,24},{12,28},{16,0},{20,4},{24,8},{28,12},{1,17},{... | collective-permute-start | bytes 1228808 | tf_op jit(solution)/shard_map/ppermute | solution.py:30
  52.1 32.5 %collective-permute-start.13 = (bf16[2,160,640]{2,1,0:T(8,128)(2,1)S(1)}, bf16[2,160,640]{2,1,0:T(8,128)(2,1)}, u32[]{:S(2)}, u32[]{:S(2)}) collective-permute-start(bf16[2,160,640]{2,1,0:T(8,128)(2,1)S(1)} %get-tuple-element.228.refs_0_), channel_id=1, source_target_pairs={{0,8},{4,12},{8,0},{12,4},{16,24},{20,28},{24,16},{28,20},{1,9},{5... | collective-permute-start | bytes 1228808 | tf_op jit(solution)/shard_map/ppermute | solution.py:30
  53.6 45.6 %all-to-all-start = ((bf16[4,160,640]{2,1,0:T(8,128)(2,1)}), bf16[4,160,640]{2,1,0:T(8,128)(2,1)}, u32[]{:S(2)}, u32[]{:S(2)}) async-start(bf16[4,160,640]{2,1,0:T(8,128)(2,1)} %shard_map.254), calls=%async_computation | async-start | bytes 1638400 | tf_op jit(solution)/shard_map/all_to_all | solution.py:1194
  57.8 107.5 %all-gather.5.cloned.1.call-start = ((), (), s32[]{:S(2)}) async-start(), calls=%async_computation.8 | async-start | bytes 4096000 | tf_op jit(solution)/shard_map/all_gather | solution.py:1209
  101.4 46.0 %collective-permute-start.22 = (bf16[2,160,640]{2,1,0:T(8,128)(2,1)}, bf16[2,160,640]{2,1,0:T(8,128)(2,1)}, u32[]{:S(2)}, u32[]{:S(2)}) collective-permute-start(bf16[2,160,640]{2,1,0:T(8,128)(2,1)} %get-tuple-element.249.refs_0_), channel_id=1, source_target_pairs={{0,24},{4,28},{8,16},{12,20},{16,8},{20,12},{24,0},{28,4},{1,25},{... | collective-permute-start | bytes 1228808 | tf_op jit(solution)/shard_map/ppermute | solution.py:30
  104.0 43.4 %collective-permute-start.21 = (bf16[2,160,640]{2,1,0:T(8,128)(2,1)}, bf16[2,160,640]{2,1,0:T(8,128)(2,1)}, u32[]{:S(2)}, u32[]{:S(2)}) collective-permute-start(bf16[2,160,640]{2,1,0:T(8,128)(2,1)} %get-tuple-element.249.refs_0_), channel_id=1, source_target_pairs={{0,16},{4,20},{8,24},{12,28},{16,0},{20,4},{24,8},{28,12},{1,17},{... | collective-permute-start | bytes 1228808 | tf_op jit(solution)/shard_map/ppermute | solution.py:30
  104.5 42.9 %collective-permute-start.20 = (bf16[2,160,640]{2,1,0:T(8,128)(2,1)}, bf16[2,160,640]{2,1,0:T(8,128)(2,1)}, u32[]{:S(2)}, u32[]{:S(2)}) collective-permute-start(bf16[2,160,640]{2,1,0:T(8,128)(2,1)} %get-tuple-element.249.refs_0_), channel_id=1, source_target_pairs={{0,8},{4,12},{8,0},{12,4},{16,24},{20,28},{24,16},{28,20},{1,9},{5... | collective-permute-start | bytes 1228808 | tf_op jit(solution)/shard_map/ppermute | solution.py:30
  107.5 39.9 %all-to-all-start.1 = ((bf16[4,160,384]{2,1,0:T(8,128)(2,1)}), bf16[4,160,384]{2,1,0:T(8,128)(2,1)}, u32[]{:S(2)}, u32[]{:S(2)}) async-start(bf16[4,160,384]{2,1,0:T(8,128)(2,1)} %shard_map.261), calls=%async_computation.1 | async-start | bytes 983040 | tf_op jit(solution)/shard_map/all_to_all | solution.py:1203
  111.6 103.2 %all-gather.7.cloned.1.call-start = ((), (), s32[]{:S(2)}) async-start(), calls=%async_computation.9 | async-start | bytes 2457600 | tf_op jit(solution)/shard_map/all_gather | solution.py:1230
  165.3 323.4 %reduce-scatter.3.cloned.1.call-start = ((), (), s32[]{:S(2)}) async-start(), calls=%async_computation.6 | async-start | bytes 2457600 | tf_op jit(solution)/shard_map/reduce_scatter | solution.py:1318
  165.6 31.5 %collective-permute-start.25 = (bf16[512,1280]{1,0:T(8,128)(2,1)}, bf16[512,1280]{1,0:T(8,128)(2,1)S(1)}, u32[]{:S(2)}, u32[]{:S(2)}) collective-permute-start(bf16[512,1280]{1,0:T(8,128)(2,1)} %get-tuple-element.255.refs_0_), channel_id=1, source_target_pairs={{0,16},{4,20},{8,24},{12,28},{16,0},{20,4},{24,8},{28,12},{1,17},{... | collective-permute-start | bytes 3932168 | tf_op jit(solution)/shard_map/ppermute | solution.py:30
  167.2 31.1 %collective-permute-start.24 = (bf16[512,1280]{1,0:T(8,128)(2,1)}, bf16[512,1280]{1,0:T(8,128)(2,1)S(1)}, u32[]{:S(2)}, u32[]{:S(2)}) collective-permute-start(bf16[512,1280]{1,0:T(8,128)(2,1)} %get-tuple-element.255.refs_0_), channel_id=1, source_target_pairs={{0,8},{4,12},{8,0},{12,4},{16,24},{20,28},{24,16},{28,20},{1,9},{5... | collective-permute-start | bytes 3932168 | tf_op jit(solution)/shard_map/ppermute | solution.py:30
  241.8 33.1 %collective-permute-start.31 = (bf16[512,1280]{1,0:T(8,128)(2,1)S(1)}, bf16[512,1280]{1,0:T(8,128)(2,1)S(1)}, u32[]{:S(2)}, u32[]{:S(2)}) collective-permute-start(bf16[512,1280]{1,0:T(8,128)(2,1)S(1)} %pad_maximum_fusion), channel_id=1, source_target_pairs={{0,8},{4,12},{8,0},{12,4},{16,24},{20,28},{24,16},{28,20},{1,9},{5... | collective-permute-start | bytes 3932168 | tf_op jit(solution)/shard_map/ppermute | solution.py:30
  243.4 31.6 %collective-permute-start.32 = (bf16[512,1280]{1,0:T(8,128)(2,1)S(1)}, bf16[512,1280]{1,0:T(8,128)(2,1)S(1)}, u32[]{:S(2)}, u32[]{:S(2)}) collective-permute-start(bf16[512,1280]{1,0:T(8,128)(2,1)S(1)} %pad_maximum_fusion.1), channel_id=1, source_target_pairs={{0,16},{4,20},{8,24},{12,28},{16,0},{20,4},{24,8},{28,12},{1,17},{... | collective-permute-start | bytes 3932168 | tf_op jit(solution)/shard_map/ppermute | solution.py:30
  244.9 30.0 %collective-permute-start.34 = (bf16[256,1280]{1,0:T(8,128)(2,1)S(1)}, bf16[256,1280]{1,0:T(8,128)(2,1)S(1)}, u32[]{:S(2)}, u32[]{:S(2)}) collective-permute-start(bf16[256,1280]{1,0:T(8,128)(2,1)S(1)} %get-tuple-element.500), channel_id=1, source_target_pairs={{0,2},{1,6},{2,0},{3,4},{4,3},{5,7},{6,1},{7,5},{8,10},{9,14},{10,... | collective-permute-start | bytes 1966088 | tf_op jit(solution)/shard_map/ppermute | solution.py:1039
  246.1 28.9 %collective-permute-start.33 = (bf16[256,1280]{1,0:T(8,128)(2,1)S(1)}, bf16[256,1280]{1,0:T(8,128)(2,1)S(1)}, u32[]{:S(2)}, u32[]{:S(2)}) collective-permute-start(bf16[256,1280]{1,0:T(8,128)(2,1)S(1)} %get-tuple-element.501), channel_id=1, source_target_pairs={{0,0},{1,4},{2,2},{3,6},{4,1},{5,5},{6,3},{7,7},{8,8},{9,12},{10,1... | collective-permute-start | bytes 1966088 | tf_op jit(solution)/shard_map/ppermute | solution.py:1039
  300.7 28.3 %collective-permute-start.38 = (bf16[512,1280]{1,0:T(8,128)(2,1)S(1)}, bf16[512,1280]{1,0:T(8,128)(2,1)S(1)}, u32[]{:S(2)}, u32[]{:S(2)}) collective-permute-start(bf16[512,1280]{1,0:T(8,128)(2,1)S(1)} %get-tuple-element.289.refs_0_), channel_id=1, source_target_pairs={{0,16},{4,20},{8,24},{12,28},{16,0},{20,4},{24,8},{28,12},{1,17},{... | collective-permute-start | bytes 3932168 | tf_op jit(solution)/shard_map/ppermute | solution.py:30
  302.1 28.3 %collective-permute-start.37 = (bf16[512,1280]{1,0:T(8,128)(2,1)S(1)}, bf16[512,1280]{1,0:T(8,128)(2,1)S(1)}, u32[]{:S(2)}, u32[]{:S(2)}) collective-permute-start(bf16[512,1280]{1,0:T(8,128)(2,1)S(1)} %get-tuple-element.289.refs_0_), channel_id=1, source_target_pairs={{0,8},{4,12},{8,0},{12,4},{16,24},{20,28},{24,16},{28,20},{1,9},{5... | collective-permute-start | bytes 3932168 | tf_op jit(solution)/shard_map/ppermute | solution.py:30
  304.5 49.1 %collective-permute-start.42 = (bf16[256,1280]{1,0:T(8,128)(2,1)}, bf16[256,1280]{1,0:T(8,128)(2,1)}, u32[]{:S(2)}, u32[]{:S(2)}) collective-permute-start(bf16[256,1280]{1,0:T(8,128)(2,1)} %get-tuple-element.498), channel_id=1, source_target_pairs={{2,0},{6,1},{0,2},{4,3},{3,4},{7,5},{1,6},{5,7},{10,8},{14,9},{8,1... | collective-permute-start | bytes 1966088 | tf_op jit(solution)/shard_map/ppermute | solution.py:1039
  306.4 47.2 %collective-permute-start.41 = (bf16[256,1280]{1,0:T(8,128)(2,1)}, bf16[256,1280]{1,0:T(8,128)(2,1)}, u32[]{:S(2)}, u32[]{:S(2)}) collective-permute-start(bf16[256,1280]{1,0:T(8,128)(2,1)} %get-tuple-element.499), channel_id=1, source_target_pairs={{0,0},{4,1},{2,2},{6,3},{1,4},{5,5},{3,6},{7,7},{8,8},{12,9},{10,1... | collective-permute-start | bytes 1966088 | tf_op jit(solution)/shard_map/ppermute | solution.py:1039
  366.9 42.5 %collective-permute-start.43 = (bf16[512,1280]{1,0:T(8,128)(2,1)S(1)}, bf16[512,1280]{1,0:T(8,128)(2,1)S(1)}, u32[]{:S(2)}, u32[]{:S(2)}) collective-permute-start(bf16[512,1280]{1,0:T(8,128)(2,1)S(1)} %pad_maximum_fusion.2), channel_id=1, source_target_pairs={{0,8},{4,12},{8,0},{12,4},{16,24},{20,28},{24,16},{28,20},{1,9},{5... | collective-permute-start | bytes 3932168 | tf_op jit(solution)/shard_map/ppermute | solution.py:30
  367.6 41.8 %collective-permute-start.44 = (bf16[512,1280]{1,0:T(8,128)(2,1)S(1)}, bf16[512,1280]{1,0:T(8,128)(2,1)}, u32[]{:S(2)}, u32[]{:S(2)}) collective-permute-start(bf16[512,1280]{1,0:T(8,128)(2,1)S(1)} %pad_maximum_fusion.3), channel_id=1, source_target_pairs={{0,16},{4,20},{8,24},{12,28},{16,0},{20,4},{24,8},{28,12},{1,17},{... | collective-permute-start | bytes 3932168 | tf_op jit(solution)/shard_map/ppermute | solution.py:30
  369.4 40.0 %collective-permute-start.45 = (f32[3,1280]{1,0:T(4,128)S(1)}, f32[3,1280]{1,0:T(4,128)S(1)}, u32[]{:S(2)}, u32[]{:S(2)}) collective-permute-start(f32[3,1280]{1,0:T(4,128)S(1)} %pad_maximum_fusion.13), channel_id=1, source_target_pairs={{0,4},{4,0},{8,12},{12,8},{16,20},{20,16},{24,28},{28,24},{1,5},{5... | collective-permute-start | bytes 46088 | tf_op jit(solution)/shard_map/ppermute | solution.py:30
  431.6 106.5 %reduce-scatter.5.cloned.1.call-start = ((), (), s32[]{:S(2)}) async-start(), calls=%async_computation.7 | async-start | bytes 4096000 | tf_op jit(solution)/shard_map/reduce_scatter | solution.py:1326
  506.7 22.5 %collective-permute-start.51 = (bf16[2,176,1280]{2,1,0:T(8,128)(2,1)}, bf16[2,176,1280]{2,1,0:T(8,128)(2,1)S(1)}, u32[]{:S(2)}, u32[]{:S(2)}) collective-permute-start(bf16[2,176,1280]{2,1,0:T(8,128)(2,1)} %get-tuple-element.359), channel_id=1, source_target_pairs={{0,8},{4,12},{8,0},{12,4},{16,24},{20,28},{24,16},{28,20},{1,9},{5... | collective-permute-start | bytes 2703368 | tf_op jit(solution)/shard_map/ppermute | solution.py:30
  561.5 27.8 %collective-permute-start.58 = (bf16[2,176,1280]{2,1,0:T(8,128)(2,1)S(1)}, bf16[2,176,1280]{2,1,0:T(8,128)(2,1)S(1)}, u32[]{:S(2)}, u32[]{:S(2)}) collective-permute-start(bf16[2,176,1280]{2,1,0:T(8,128)(2,1)S(1)} %get-tuple-element.387), channel_id=1, source_target_pairs={{0,16},{4,20},{8,24},{12,28},{16,0},{20,4},{24,8},{28,12},{1,17},{... | collective-permute-start | bytes 2703368 | tf_op jit(solution)/shard_map/ppermute | solution.py:30
  564.9 32.3 %collective-permute-start.63 = (bf16[176,640]{1,0:T(8,128)(2,1)}, bf16[176,640]{1,0:T(8,128)(2,1)}, u32[]{:S(2)}, u32[]{:S(2)}) collective-permute-start(bf16[176,640]{1,0:T(8,128)(2,1)} %get-tuple-element.399), channel_id=1, source_target_pairs={{0,0},{1,1},{2,2},{3,3},{4,6},{5,7},{6,4},{7,5},{8,8},{9,9},{10,10... | collective-permute-start | bytes 675848 | tf_op jit(solution)/shard_map/ppermute | solution.py:1039
  568.4 30.7 %collective-permute-start.64 = (bf16[176,640]{1,0:T(8,128)(2,1)S(1)}, bf16[176,640]{1,0:T(8,128)(2,1)}, u32[]{:S(2)}, u32[]{:S(2)}) collective-permute-start(bf16[176,640]{1,0:T(8,128)(2,1)S(1)} %get-tuple-element.400), channel_id=1, source_target_pairs={{0,1},{1,2},{2,3},{3,0},{4,7},{5,4},{6,5},{7,6},{8,9},{9,10},{10,1... | collective-permute-start | bytes 675848 | tf_op jit(solution)/shard_map/ppermute | solution.py:1039
  570.7 50.7 %collective-permute-start.62 = (bf16[256,1280]{1,0:T(8,128)(2,1)}, bf16[256,1280]{1,0:T(8,128)(2,1)}, u32[]{:S(2)}, u32[]{:S(2)}) collective-permute-start(bf16[256,1280]{1,0:T(8,128)(2,1)} %get-tuple-element.494), channel_id=1, source_target_pairs={{2,0},{6,1},{0,2},{4,3},{3,4},{7,5},{1,6},{5,7},{10,8},{14,9},{8,1... | collective-permute-start | bytes 1966088 | tf_op jit(solution)/shard_map/ppermute | solution.py:1039
  582.8 38.6 %collective-permute-start.61 = (bf16[256,1280]{1,0:T(8,128)(2,1)}, bf16[256,1280]{1,0:T(8,128)(2,1)}, u32[]{:S(2)}, u32[]{:S(2)}) collective-permute-start(bf16[256,1280]{1,0:T(8,128)(2,1)} %get-tuple-element.495), channel_id=1, source_target_pairs={{0,0},{4,1},{2,2},{6,3},{1,4},{5,5},{3,6},{7,7},{8,8},{12,9},{10,1... | collective-permute-start | bytes 1966088 | tf_op jit(solution)/shard_map/ppermute | solution.py:1039
  597.2 24.1 %collective-permute-start.59 = (bf16[176,1280]{1,0:T(8,128)(2,1)}, bf16[176,1280]{1,0:T(8,128)(2,1)}, u32[]{:S(2)}, u32[]{:S(2)}) collective-permute-start(bf16[176,1280]{1,0:T(8,128)(2,1)} %get-tuple-element.394), channel_id=1, source_target_pairs={{0,16},{4,20},{8,24},{12,28},{16,0},{20,4},{24,8},{28,12},{1,17},{... | collective-permute-start | bytes 1351688 | tf_op jit(solution)/shard_map/ppermute | solution.py:30
  601.4 31.9 %all-to-all-start.3 = ((bf16[4,160,640]{2,1,0:T(8,128)(2,1)}), bf16[4,160,640]{2,1,0:T(8,128)(2,1)S(1)}, u32[]{:S(2)}, u32[]{:S(2)}) async-start(bf16[4,160,640]{2,1,0:T(8,128)(2,1)} %bitcast.178), calls=%async_computation.5 | async-start | bytes 1638400 | tf_op jit(solution)/shard_map/all_to_all | solution.py:1166
  (132 other events, 1424.3 us)
Sparse Core Ops, SparseCore 0:
  99.3 65.9 all-gather.4
  166.9 42.1 all-gather.6
  431.8 42.5 reduce-scatter.2
  476.6 61.4 reduce-scatter.4

commit v4 on v3

--- a/solution.py
+++ b/solution.py
@@ -1338,7 +1338,10 @@
         [(heads_low, 0, 2 * core_heads), (vraw_low, 0, core_heads)],
         [(qk_w, 0, 2 * core_heads), (value_w, 0, core_heads)],
     )
-    vo_sent, heads_low, in_part, ug_back, block_out = tie((vo_sent, heads_low, in_part, ug_back, block_out))
+    (grad_down,) = unit_return(1, down_back)
+    vo_sent, heads_low, in_part, ug_back, block_out, grad_down = tie(
+        (vo_sent, heads_low, in_part, ug_back, block_out, grad_down)
+    )
     att_term = att_rate_term[:1] + swap(att_rate_term[:1], 1)
     vo_messages, heads_low, in_part, att_term = tie((spread_turn(*vo_sent), heads_low, in_part, att_term))
     qk_extra = jnp.concatenate(
@@ -1354,11 +1357,10 @@
     vo_turned, in_rows, qk_messages = tie((vo_turned, in_rows, qk_messages))
     qk_sent = attn_send(qk_messages)
     returned_in = from_sequence(in_rows)
+    qk_sent, vo_turned = tie((qk_sent, vo_turned))
     vo_got = attn_scatter(vo_sent, vo_turned)
-    qk_sent, down_back, ug_back = tie((qk_sent, down_back, ug_back))
     qk_turned = attn_turn(spread_turn(*qk_sent))
-    (grad_down,) = unit_return(1, down_back)
-    qk_turned, returned_in, vo_got, grad_down = tie((qk_turned, returned_in, vo_got, grad_down))
+    qk_turned, returned_in, ug_back = tie((qk_turned, returned_in, ug_back))
     qk_got = attn_scatter(qk_sent, qk_turned)
     grad_up, grad_gate = unit_return(2, ug_back)
     in_grad = by_micro(*returned_in)

time: 670 us -> 657 us (0.981)
  waiting for transfers between devices: 140 us -> 130 us
    ppermute x23, waiting for transfers between devices: 75.6 us -> 65.3 us  [across(): lax.ppermute(value, ALL, [(a * count + b, c * count + d) for (a, b), (c,...]
    reduce_scatter x1, waiting for transfers between devices: 8.29 us -> 1.04 us  [per_device(): ug_back = lax.psum_scatter(ug_blocks, 'tensor', scatter_dimension=0)]
    unnamed x173 -> x177, local copies, waits for them, and re-layouts: 41.7 us -> 41.5 us
  transfers between devices with their start and end apart: 79 -> 79, of which waited for: 26 -> 26; matrix products, arithmetic and copies ran while one was open for 7% -> 8% of each run, Pallas kernels for 39% -> 39%
where the time goes in v4:
time: 657 us; the launch traced here: 649 us
  Pallas kernels  294 us (45%)
  waiting for transfers between devices  130 us (20%)
  starting transfers between devices  110 us (17%)
  local copies, waits for them, and re-layouts  64.2 us (10%)
  other arithmetic  34.7 us (5%)
  between operations  15.9 us (2%)
    ppermute x23, waiting for transfers between devices, across(): lax.ppermute(value, ALL, [(a * count + b, c * count + d) for (a, b), (c,...  65.3 us
    ppermute x48, waiting for transfers between devices, swap(): return lax.ppermute(value, DP, [(i, i ^ bit) for i in range(count)])  55.8 us
    pallas_call x4, Pallas kernels, rows_product(): pl.pallas_call(kernel, grid=(sum(steps),), in_specs=[pl.BlockSpec((n, dep...  49 us
    ppermute x23, starting transfers between devices, across(): lax.ppermute(value, ALL, [(a * count + b, c * count + d) for (a, b), (c,...  47.2 us
    ppermute x48, starting transfers between devices, swap(): return lax.ppermute(value, DP, [(i, i ^ bit) for i in range(count)])  45.7 us
    pallas_call x3, Pallas kernels, mlp_backward(): pl.pallas_call(kernel, grid=(steps,), in_specs=chunk_specs(blocks, depth)...  44.6 us
    unnamed x177, local copies, waits for them, and re-layouts  41.5 us
    pallas_call x1, Pallas kernels, attend_backward(): pl.pallas_call(kernel, grid=(pairs,), in_specs=[block, keys, block, block...  28.8 us
  transfers between devices with their start and end apart: 79, of which 26 were waited for; matrix products, arithmetic and copies ran while one was open for 8% of the time, Pallas kernels for 39%

profile of v4, /device:TPU:0, one launch (start us, length us, event | category | flops | bytes accessed | tf_op | source)
XLA Modules:
  0.0 648.7 jit_solution(8739736834336997607)
XLA Ops:
  35.4 11.8 %collective-permute-done.9 = bf16[2,176,640]{2,1,0:T(8,128)(2,1)S(1)} collective-permute-done((bf16[2,176,640]{2,1,0:T(8,128)(2,1)}, bf16[2,176,640]{2,1,0:T(8,128)(2,1)S(1)}, u32[]{:S(2)}, u32[]{:S(2)}) %collective-permute-start.9) | collective-permute-done | bytes 450592 | tf_op jit(solution)/shard_map/ppermute | solution.py:1039
  60.0 7.0 %collective-permute-start.17 = (bf16[128,1280]{1,0:T(8,128)(2,1)S(1)}, bf16[128,1280]{1,0:T(8,128)(2,1)S(1)}, u32[]{:S(2)}, u32[]{:S(2)}) collective-permute-start(bf16[128,1280]{1,0:T(8,128)(2,1)S(1)} %dynamic-slice_bitcast_fusion.6), channel_id=1, source_target_pairs={{0,2},{1,6},{2,0},{3,4},{4,3},{5,7},{6,1},{7,5},{8,10},{9,14},{10,... | collective-permute-start | bytes 983048 | tf_op jit(solution)/shard_map/ppermute | solution.py:1039
  71.2 9.6 %collective-permute-done.17 = bf16[128,1280]{1,0:T(8,128)(2,1)S(1)} collective-permute-done((bf16[128,1280]{1,0:T(8,128)(2,1)S(1)}, bf16[128,1280]{1,0:T(8,128)(2,1)S(1)}, u32[]{:S(2)}, u32[]{:S(2)}) %collective-permute-start.17) | collective-permute-done | bytes 327712 | tf_op jit(solution)/shard_map/ppermute | solution.py:1039
  117.1 11.6 %shard_map.258 = (bf16[1024,1280]{1,0:T(8,128)(2,1)S(1)}, bf16[1024,1280]{1,0:T(8,128)(2,1)S(1)}) custom-call(bf16[1024,1280]{1,0:T(8,128)(2,1)} %bitcast.132, bf16[1280,1280]{1,0:T(8,128)(2,1)} %bitcast.166, f32[1,1280]{1,0:T(1,128)S(1)} %broadcast_in_dim.116.gain_ref), custom_call_target="tpu_custom_call" | custom-call | flops 1 | bytes 1 | tf_op jit(solution)/shard_map/pallas_call | solution.py:163
  130.3 15.6 %shard_map.260 = (bf16[1024,640]{1,0:T(8,128)(2,1)S(1)}, f32[5,8,1024]{2,1,0:T(8,128)S(1)}) custom-call(bf16[1024,1280]{1,0:T(8,128)(2,1)S(1)} %get-tuple-element.239.q_ref.k_ref, bf16[1024,1280]{1,0:T(8,128)(2,1)S(1)} %get-tuple-element.239.q_ref.k_ref, bf16[1024,640]{1,0:T(8,128)(2,1)S(1)} %shard_map.259.v_ref, f32[1,1024]{1,0:T(1,128)S(1)} %bitcast.158, ...), custom_call_target="tpu_custom_call" | custom-call | flops 1 | bytes 1 | tf_op jit(solution)/shard_map/pallas_call | solution.py:225
  157.4 5.1 shard_map.264
  172.0 5.5 shard_map.265
  179.2 8.0 %shard_map.266 = (bf16[2048,1280]{1,0:T(8,128)(2,1)}, bf16[2048,1280]{1,0:T(8,128)(2,1)}, bf16[512,1280]{1,0:T(8,128)(2,1)S(1)}, bf16[512,1280]{1,0:T(8,128)(2,1)S(1)}, bf16[512,1280]{1,0:T(8,128)(2,1)S(1)}) custom-call(bf16[512,1280]{1,0:T(8,128)(2,1)} %get-tuple-element.252.refs_0_, bf16[1280,1280]{1,0:T(8,128)(2,1)} %bitcast.125, ...), custom_call_target="tpu_custom_call" | custom-call | flops 1 | bytes 1 | tf_op jit(solution)/shard_map/pallas_call | solution.py:653
  188.3 8.8 %collective-permute-done.25.refs_1_ = bf16[512,1280]{1,0:T(8,128)(2,1)S(1)} collective-permute-done((bf16[512,1280]{1,0:T(8,128)(2,1)}, bf16[512,1280]{1,0:T(8,128)(2,1)S(1)}, u32[]{:S(2)}, u32[]{:S(2)}) %collective-permute-start.25) | collective-permute-done | bytes 1310752 | tf_op jit(solution)/shard_map/ppermute | solution.py:30
  202.1 11.3 %shard_map.267 = (bf16[2048,1280]{1,0:T(8,128)(2,1)}, bf16[2048,1280]{1,0:T(8,128)(2,1)}, bf16[1024,1280]{1,0:T(8,128)(2,1)S(1)}, bf16[1024,1280]{1,0:T(8,128)(2,1)}, bf16[1024,1280]{1,0:T(8,128)(2,1)}) custom-call(bf16[512,1280]{1,0:T(8,128)(2,1)S(1)} %collective-permute-done.24.refs_0_, ...), custom_call_target="tpu_custom_call", output_to_operand_aliasing={{0}: (5, {}), {1}: (6, {})} | custom-call | flops 1 | bytes 1 | tf_op jit(solution)/shard_map/pallas_call | solution.py:653
  216.9 8.1 %shard_map.271 = (bf16[2048,1280]{1,0:T(8,128)(2,1)}, bf16[2048,1280]{1,0:T(8,128)(2,1)}, bf16[512,1280]{1,0:T(8,128)(2,1)S(1)}, bf16[512,1280]{1,0:T(8,128)(2,1)S(1)}, bf16[512,1280]{1,0:T(8,128)(2,1)S(1)}) custom-call(bf16[256,1280]{1,0:T(8,128)(2,1)} %collective-permute-done.28.refs_0_, ...), custom_call_target="tpu_custom_call", output_to_operand_aliasing={{0}: (5, {}), {1}: (6, {})} | custom-call | flops 1 | bytes 1 | tf_op jit(solution)/shard_map/pallas_call | solution.py:653
  228.7 6.1 shard_map.270
  247.0 28.0 %collective-permute-done.34.refs_7_ = bf16[256,1280]{1,0:T(8,128)(2,1)S(1)} collective-permute-done((bf16[256,1280]{1,0:T(8,128)(2,1)S(1)}, bf16[256,1280]{1,0:T(8,128)(2,1)S(1)}, u32[]{:S(2)}, u32[]{:S(2)}) %collective-permute-start.34) | collective-permute-done | bytes 655392 | tf_op jit(solution)/shard_map/ppermute | solution.py:1039
  279.8 12.8 %collective-permute-done.36.refs_4_ = bf16[256,1280]{1,0:T(8,128)(2,1)S(1)} collective-permute-done((bf16[256,1280]{1,0:T(8,128)(2,1)}, bf16[256,1280]{1,0:T(8,128)(2,1)S(1)}, u32[]{:S(2)}, u32[]{:S(2)}) %collective-permute-start.36) | collective-permute-done | bytes 655392 | tf_op jit(solution)/shard_map/ppermute | solution.py:30
  294.0 6.7 %shard_map.273 = (bf16[512,1280]{1,0:T(8,128)(2,1)S(1)}, f32[512,1280]{1,0:T(8,128)}, bf16[512,1280]{1,0:T(8,128)(2,1)S(1)}, f32[8,1280]{1,0:T(8,128)S(1)}) custom-call(s32[1]{0:T(128)} %bitcast.32.early_ref, bf16[512,1280]{1,0:T(8,128)(2,1)} %copy-done.27, bf16[512,1280]{1,0:T(8,128)(2,1)} %copy-done.69, bf16[512,1280]{1,0:T(8,128)(2,1)} %copy-done.70, ...), custom_call_target="tpu_custom_call" | custom-call | flops 1 | bytes 1 | tf_op jit(solution)/shard_map/pallas_call | solution.py:561
  306.5 6.9 %collective-permute-start.41 = (bf16[256,1280]{1,0:T(8,128)(2,1)}, bf16[256,1280]{1,0:T(8,128)(2,1)}, u32[]{:S(2)}, u32[]{:S(2)}) collective-permute-start(bf16[256,1280]{1,0:T(8,128)(2,1)} %get-tuple-element.493), channel_id=1, source_target_pairs={{0,0},{4,1},{2,2},{6,3},{1,4},{5,5},{3,6},{7,7},{8,8},{12,9},{10,1... | collective-permute-start | bytes 1966088 | tf_op jit(solution)/shard_map/ppermute | solution.py:1039
  313.5 12.3 %shard_map.274 = (bf16[2048,1280]{1,0:T(8,128)(2,1)}, bf16[2048,1280]{1,0:T(8,128)(2,1)}, bf16[2048,1280]{1,0:T(8,128)(2,1)}, bf16[512,1280]{1,0:T(8,128)(2,1)S(1)}, f32[8,1280]{1,0:T(8,128)S(1)}) custom-call(bf16[512,1280]{1,0:T(8,128)(2,1)S(1)} %get-tuple-element.286.refs_0_, bf16[1280,1280]{1,0:T(8,128)(2,1)} %bitcast.120, ...), custom_call_target="tpu_custom_call" | custom-call | flops 1 | bytes 1 | tf_op jit(solution)/shard_map/pallas_call | solution.py:726
  334.3 19.5 %shard_map.275 = (bf16[2048,1280]{1,0:T(8,128)(2,1)}, bf16[2048,1280]{1,0:T(8,128)(2,1)}, bf16[2048,1280]{1,0:T(8,128)(2,1)}, bf16[1024,1280]{1,0:T(8,128)(2,1)S(1)}, f32[8,1280]{1,0:T(8,128)S(1)}) custom-call(bf16[512,1280]{1,0:T(8,128)(2,1)S(1)} %collective-permute-done.37.refs_0_, ...), custom_call_target="tpu_custom_call", output_to_operand_aliasing={{0}: (8, {}), {1}: (9, {}), {2}: (10, {})} | custom-call | flops 1 | bytes 1 | tf_op jit(solution)/shard_map/pallas_call | solution.py:726
  353.8 12.8 %shard_map.276 = (bf16[2048,1280]{1,0:T(8,128)(2,1)}, bf16[2048,1280]{1,0:T(8,128)(2,1)}, bf16[2048,1280]{1,0:T(8,128)(2,1)}, bf16[512,1280]{1,0:T(8,128)(2,1)S(1)}, f32[8,1280]{1,0:T(8,128)S(1)}) custom-call(bf16[256,1280]{1,0:T(8,128)(2,1)} %collective-permute-done.39.refs_0_, ...), custom_call_target="tpu_custom_call", output_to_operand_aliasing={{0}: (8, {}), {1}: (9, {}), {2}: (10, {})} | custom-call | flops 1 | bytes 1 | tf_op jit(solution)/shard_map/pallas_call | solution.py:726
  370.6 12.5 %shard_map.277 = bf16[1280,1280]{1,0:T(8,128)(2,1)S(1)} custom-call(bf16[2048,1280]{1,0:T(8,128)(2,1)} %get-tuple-element.313.refs_0_, bf16[2048,1280]{1,0:T(8,128)(2,1)} %get-tuple-element.314.refs_1_), custom_call_target="tpu_custom_call" | custom-call | flops 1 | bytes 1 | tf_op jit(solution)/shard_map/pallas_call | solution.py:426
  388.2 21.1 %shard_map.279 = bf16[1280,2560]{1,0:T(8,128)(2,1)} custom-call(bf16[2048,1280]{1,0:T(8,128)(2,1)S(1)} %bitcast.136, bf16[2048,1280]{1,0:T(8,128)(2,1)} %get-tuple-element.318.refs_1_, bf16[2048,1280]{1,0:T(8,128)(2,1)} %get-tuple-element.319.refs_2_), custom_call_target="tpu_custom_call" | custom-call | flops 1 | bytes 1 | tf_op jit(solution)/shard_map/pallas_call | solution.py:426
  415.0 5.7 shard_map.280
  422.6 5.8 shard_map.281
  434.1 7.5 %shard_map.282 = (f32[512,1280]{1,0:T(8,128)}, bf16[512,1280]{1,0:T(8,128)(2,1)S(1)}, f32[8,1280]{1,0:T(8,128)S(1)}) custom-call(bf16[512,1280]{1,0:T(8,128)(2,1)S(1)} %copy-done.52, bf16[512,1280]{1,0:T(8,128)(2,1)S(1)} %collective-permute-done.43.refs_1_, bf16[512,1280]{1,0:T(8,128)(2,1)} %collective-permute-done.44.refs_2_, ...), custom_call_target="tpu_custom_call" | custom-call | flops 1 | bytes 1 | tf_op jit(solution)/shard_map/pallas_call | solution.py:606
  448.0 5.6 shard_map.284
  459.1 28.8 %shard_map.286 = (bf16[1024,1280]{1,0:T(8,128)(2,1)}, bf16[1024,640]{1,0:T(8,128)(2,1)S(1)}, f32[8,640]{1,0:T(8,128)S(1)}) custom-call(bf16[1024,1280]{1,0:T(8,128)(2,1)} %copy-done.4, bf16[1024,1280]{1,0:T(8,128)(2,1)} %copy-done.4, bf16[1024,640]{1,0:T(8,128)(2,1)S(1)} %copy-done.15, bf16[1024,1280]{1,0:T(8,128)(2,1)} %copy-done.23, ...), custom_call_target="tpu_custom_call" | custom-call | flops 1 | bytes 1 | tf_op jit(solution)/shard_map/pallas_call | solution.py:325
  491.6 9.3 %shard_map.287 = bf16[1280,1280]{1,0:T(8,128)(2,1)} custom-call(bf16[1024,1280]{1,0:T(8,128)(2,1)S(1)} %bitcast.133, bf16[1024,1280]{1,0:T(8,128)(2,1)} %bitcast.138, bf16[1024,640]{1,0:T(8,128)(2,1)S(1)} %copy-done.29, bf16[1024,640]{1,0:T(8,128)(2,1)S(1)} %copy-done.18), custom_call_target="tpu_custom_call" | custom-call | flops 1 | bytes 1 | tf_op jit(solution)/shard_map/pallas_call | solution.py:426
  519.9 8.5 %shard_map.289 = bf16[1024,1280]{1,0:T(8,128)(2,1)S(1)} custom-call(bf16[1024,1280]{1,0:T(8,128)(2,1)} %get-tuple-element.378.refs_0_.refs_1_, bf16[1024,640]{1,0:T(8,128)(2,1)S(1)} %copy-done.30, bf16[1280,1280]{1,0:T(8,128)(2,1)} %bitcast.167, bf16[1280,640]{1,0:T(8,128)(2,1)S(1)} %bitcast.146), custom_call_target="tpu_custom_call" | custom-call | flops 1 | bytes 1 | tf_op jit(solution)/shard_map/pallas_call | solution.py:364
  529.9 5.3 all-to-all-done.2.block_ref
  548.1 6.2 shard_map.292
  567.6 16.1 %collective-permute-done.57.first_ref = bf16[2,176,1280]{2,1,0:T(8,128)(2,1)S(1)} collective-permute-done((bf16[2,176,1280]{2,1,0:T(8,128)(2,1)S(1)}, bf16[2,176,1280]{2,1,0:T(8,128)(2,1)S(1)}, u32[]{:S(2)}, u32[]{:S(2)}) %collective-permute-start.57) | collective-permute-done | bytes 901152 | tf_op jit(solution)/shard_map/ppermute | solution.py:30
  618.3 13.2 %collective-permute-done.69 = bf16[176,640]{1,0:T(8,128)(2,1)S(1)} collective-permute-done((bf16[176,640]{1,0:T(8,128)(2,1)S(1)}, bf16[176,640]{1,0:T(8,128)(2,1)S(1)}, u32[]{:S(2)}, u32[]{:S(2)}) %collective-permute-start.69) | collective-permute-done | bytes 225312 | tf_op jit(solution)/shard_map/ppermute | solution.py:1039
  (520 shorter events, 279.7 us)
Async XLA Ops:
  25.0 22.2 %collective-permute-start.9 = (bf16[2,176,640]{2,1,0:T(8,128)(2,1)}, bf16[2,176,640]{2,1,0:T(8,128)(2,1)S(1)}, u32[]{:S(2)}, u32[]{:S(2)}) collective-permute-start(bf16[2,176,640]{2,1,0:T(8,128)(2,1)} %pad_maximum_fusion.6), channel_id=1, source_target_pairs={{1,0},{2,1},{3,2},{0,3},{7,4},{4,5},{5,6},{6,7},{9,8},{10,9},{11,1... | collective-permute-start | bytes 1351688 | tf_op jit(solution)/shard_map/ppermute | solution.py:1039
  50.5 31.1 %collective-permute-start.14 = (bf16[2,160,640]{2,1,0:T(8,128)(2,1)S(1)}, bf16[2,160,640]{2,1,0:T(8,128)(2,1)S(1)}, u32[]{:S(2)}, u32[]{:S(2)}) collective-permute-start(bf16[2,160,640]{2,1,0:T(8,128)(2,1)S(1)} %get-tuple-element.225.refs_0_), channel_id=1, source_target_pairs={{0,16},{4,20},{8,24},{12,28},{16,0},{20,4},{24,8},{28,12},{1,17},{... | collective-permute-start | bytes 1228808 | tf_op jit(solution)/shard_map/ppermute | solution.py:30
  52.1 32.5 %collective-permute-start.13 = (bf16[2,160,640]{2,1,0:T(8,128)(2,1)S(1)}, bf16[2,160,640]{2,1,0:T(8,128)(2,1)}, u32[]{:S(2)}, u32[]{:S(2)}) collective-permute-start(bf16[2,160,640]{2,1,0:T(8,128)(2,1)S(1)} %get-tuple-element.225.refs_0_), channel_id=1, source_target_pairs={{0,8},{4,12},{8,0},{12,4},{16,24},{20,28},{24,16},{28,20},{1,9},{5... | collective-permute-start | bytes 1228808 | tf_op jit(solution)/shard_map/ppermute | solution.py:30
  53.6 45.6 %all-to-all-start = ((bf16[4,160,640]{2,1,0:T(8,128)(2,1)}), bf16[4,160,640]{2,1,0:T(8,128)(2,1)}, u32[]{:S(2)}, u32[]{:S(2)}) async-start(bf16[4,160,640]{2,1,0:T(8,128)(2,1)} %shard_map.254), calls=%async_computation | async-start | bytes 1638400 | tf_op jit(solution)/shard_map/all_to_all | solution.py:1194
  57.8 107.6 %all-gather.5.cloned.1.call-start = ((), (), s32[]{:S(2)}) async-start(), calls=%async_computation.8 | async-start | bytes 4096000 | tf_op jit(solution)/shard_map/all_gather | solution.py:1209
  101.4 46.1 %collective-permute-start.22 = (bf16[2,160,640]{2,1,0:T(8,128)(2,1)}, bf16[2,160,640]{2,1,0:T(8,128)(2,1)}, u32[]{:S(2)}, u32[]{:S(2)}) collective-permute-start(bf16[2,160,640]{2,1,0:T(8,128)(2,1)} %get-tuple-element.246.refs_0_), channel_id=1, source_target_pairs={{0,24},{4,28},{8,16},{12,20},{16,8},{20,12},{24,0},{28,4},{1,25},{... | collective-permute-start | bytes 1228808 | tf_op jit(solution)/shard_map/ppermute | solution.py:30
  104.0 43.5 %collective-permute-start.21 = (bf16[2,160,640]{2,1,0:T(8,128)(2,1)}, bf16[2,160,640]{2,1,0:T(8,128)(2,1)}, u32[]{:S(2)}, u32[]{:S(2)}) collective-permute-start(bf16[2,160,640]{2,1,0:T(8,128)(2,1)} %get-tuple-element.246.refs_0_), channel_id=1, source_target_pairs={{0,16},{4,20},{8,24},{12,28},{16,0},{20,4},{24,8},{28,12},{1,17},{... | collective-permute-start | bytes 1228808 | tf_op jit(solution)/shard_map/ppermute | solution.py:30
  104.5 42.9 %collective-permute-start.20 = (bf16[2,160,640]{2,1,0:T(8,128)(2,1)}, bf16[2,160,640]{2,1,0:T(8,128)(2,1)}, u32[]{:S(2)}, u32[]{:S(2)}) collective-permute-start(bf16[2,160,640]{2,1,0:T(8,128)(2,1)} %get-tuple-element.246.refs_0_), channel_id=1, source_target_pairs={{0,8},{4,12},{8,0},{12,4},{16,24},{20,28},{24,16},{28,20},{1,9},{5... | collective-permute-start | bytes 1228808 | tf_op jit(solution)/shard_map/ppermute | solution.py:30
  107.5 40.0 %all-to-all-start.1 = ((bf16[4,160,384]{2,1,0:T(8,128)(2,1)}), bf16[4,160,384]{2,1,0:T(8,128)(2,1)}, u32[]{:S(2)}, u32[]{:S(2)}) async-start(bf16[4,160,384]{2,1,0:T(8,128)(2,1)} %shard_map.261), calls=%async_computation.1 | async-start | bytes 983040 | tf_op jit(solution)/shard_map/all_to_all | solution.py:1203
  111.6 103.2 %all-gather.7.cloned.1.call-start = ((), (), s32[]{:S(2)}) async-start(), calls=%async_computation.9 | async-start | bytes 2457600 | tf_op jit(solution)/shard_map/all_gather | solution.py:1230
  165.4 323.6 %reduce-scatter.3.cloned.1.call-start = ((), (), s32[]{:S(2)}) async-start(), calls=%async_computation.6 | async-start | bytes 2457600 | tf_op jit(solution)/shard_map/reduce_scatter | solution.py:1318
  165.7 31.5 %collective-permute-start.25 = (bf16[512,1280]{1,0:T(8,128)(2,1)}, bf16[512,1280]{1,0:T(8,128)(2,1)S(1)}, u32[]{:S(2)}, u32[]{:S(2)}) collective-permute-start(bf16[512,1280]{1,0:T(8,128)(2,1)} %get-tuple-element.252.refs_0_), channel_id=1, source_target_pairs={{0,16},{4,20},{8,24},{12,28},{16,0},{20,4},{24,8},{28,12},{1,17},{... | collective-permute-start | bytes 3932168 | tf_op jit(solution)/shard_map/ppermute | solution.py:30
  167.2 31.1 %collective-permute-start.24 = (bf16[512,1280]{1,0:T(8,128)(2,1)}, bf16[512,1280]{1,0:T(8,128)(2,1)S(1)}, u32[]{:S(2)}, u32[]{:S(2)}) collective-permute-start(bf16[512,1280]{1,0:T(8,128)(2,1)} %get-tuple-element.252.refs_0_), channel_id=1, source_target_pairs={{0,8},{4,12},{8,0},{12,4},{16,24},{20,28},{24,16},{28,20},{1,9},{5... | collective-permute-start | bytes 3932168 | tf_op jit(solution)/shard_map/ppermute | solution.py:30
  241.9 33.1 %collective-permute-start.31 = (bf16[512,1280]{1,0:T(8,128)(2,1)S(1)}, bf16[512,1280]{1,0:T(8,128)(2,1)S(1)}, u32[]{:S(2)}, u32[]{:S(2)}) collective-permute-start(bf16[512,1280]{1,0:T(8,128)(2,1)S(1)} %pad_maximum_fusion), channel_id=1, source_target_pairs={{0,8},{4,12},{8,0},{12,4},{16,24},{20,28},{24,16},{28,20},{1,9},{5... | collective-permute-start | bytes 3932168 | tf_op jit(solution)/shard_map/ppermute | solution.py:30
  243.4 31.6 %collective-permute-start.32 = (bf16[512,1280]{1,0:T(8,128)(2,1)S(1)}, bf16[512,1280]{1,0:T(8,128)(2,1)S(1)}, u32[]{:S(2)}, u32[]{:S(2)}) collective-permute-start(bf16[512,1280]{1,0:T(8,128)(2,1)S(1)} %pad_maximum_fusion.1), channel_id=1, source_target_pairs={{0,16},{4,20},{8,24},{12,28},{16,0},{20,4},{24,8},{28,12},{1,17},{... | collective-permute-start | bytes 3932168 | tf_op jit(solution)/shard_map/ppermute | solution.py:30
  245.0 30.1 %collective-permute-start.34 = (bf16[256,1280]{1,0:T(8,128)(2,1)S(1)}, bf16[256,1280]{1,0:T(8,128)(2,1)S(1)}, u32[]{:S(2)}, u32[]{:S(2)}) collective-permute-start(bf16[256,1280]{1,0:T(8,128)(2,1)S(1)} %get-tuple-element.494), channel_id=1, source_target_pairs={{0,2},{1,6},{2,0},{3,4},{4,3},{5,7},{6,1},{7,5},{8,10},{9,14},{10,... | collective-permute-start | bytes 1966088 | tf_op jit(solution)/shard_map/ppermute | solution.py:1039
  246.1 28.9 %collective-permute-start.33 = (bf16[256,1280]{1,0:T(8,128)(2,1)S(1)}, bf16[256,1280]{1,0:T(8,128)(2,1)S(1)}, u32[]{:S(2)}, u32[]{:S(2)}) collective-permute-start(bf16[256,1280]{1,0:T(8,128)(2,1)S(1)} %get-tuple-element.495), channel_id=1, source_target_pairs={{0,0},{1,4},{2,2},{3,6},{4,1},{5,5},{6,3},{7,7},{8,8},{9,12},{10,1... | collective-permute-start | bytes 1966088 | tf_op jit(solution)/shard_map/ppermute | solution.py:1039
  300.7 28.2 %collective-permute-start.38 = (bf16[512,1280]{1,0:T(8,128)(2,1)S(1)}, bf16[512,1280]{1,0:T(8,128)(2,1)S(1)}, u32[]{:S(2)}, u32[]{:S(2)}) collective-permute-start(bf16[512,1280]{1,0:T(8,128)(2,1)S(1)} %get-tuple-element.286.refs_0_), channel_id=1, source_target_pairs={{0,16},{4,20},{8,24},{12,28},{16,0},{20,4},{24,8},{28,12},{1,17},{... | collective-permute-start | bytes 3932168 | tf_op jit(solution)/shard_map/ppermute | solution.py:30
  302.1 28.2 %collective-permute-start.37 = (bf16[512,1280]{1,0:T(8,128)(2,1)S(1)}, bf16[512,1280]{1,0:T(8,128)(2,1)S(1)}, u32[]{:S(2)}, u32[]{:S(2)}) collective-permute-start(bf16[512,1280]{1,0:T(8,128)(2,1)S(1)} %get-tuple-element.286.refs_0_), channel_id=1, source_target_pairs={{0,8},{4,12},{8,0},{12,4},{16,24},{20,28},{24,16},{28,20},{1,9},{5... | collective-permute-start | bytes 3932168 | tf_op jit(solution)/shard_map/ppermute | solution.py:30
  304.7 49.1 %collective-permute-start.42 = (bf16[256,1280]{1,0:T(8,128)(2,1)}, bf16[256,1280]{1,0:T(8,128)(2,1)}, u32[]{:S(2)}, u32[]{:S(2)}) collective-permute-start(bf16[256,1280]{1,0:T(8,128)(2,1)} %get-tuple-element.492), channel_id=1, source_target_pairs={{2,0},{6,1},{0,2},{4,3},{3,4},{7,5},{1,6},{5,7},{10,8},{14,9},{8,1... | collective-permute-start | bytes 1966088 | tf_op jit(solution)/shard_map/ppermute | solution.py:1039
  306.5 47.3 %collective-permute-start.41 = (bf16[256,1280]{1,0:T(8,128)(2,1)}, bf16[256,1280]{1,0:T(8,128)(2,1)}, u32[]{:S(2)}, u32[]{:S(2)}) collective-permute-start(bf16[256,1280]{1,0:T(8,128)(2,1)} %get-tuple-element.493), channel_id=1, source_target_pairs={{0,0},{4,1},{2,2},{6,3},{1,4},{5,5},{3,6},{7,7},{8,8},{12,9},{10,1... | collective-permute-start | bytes 1966088 | tf_op jit(solution)/shard_map/ppermute | solution.py:1039
  367.1 42.3 %collective-permute-start.43 = (bf16[512,1280]{1,0:T(8,128)(2,1)S(1)}, bf16[512,1280]{1,0:T(8,128)(2,1)S(1)}, u32[]{:S(2)}, u32[]{:S(2)}) collective-permute-start(bf16[512,1280]{1,0:T(8,128)(2,1)S(1)} %pad_maximum_fusion.2), channel_id=1, source_target_pairs={{0,8},{4,12},{8,0},{12,4},{16,24},{20,28},{24,16},{28,20},{1,9},{5... | collective-permute-start | bytes 3932168 | tf_op jit(solution)/shard_map/ppermute | solution.py:30
  367.6 41.8 %collective-permute-start.44 = (bf16[512,1280]{1,0:T(8,128)(2,1)S(1)}, bf16[512,1280]{1,0:T(8,128)(2,1)}, u32[]{:S(2)}, u32[]{:S(2)}) collective-permute-start(bf16[512,1280]{1,0:T(8,128)(2,1)S(1)} %pad_maximum_fusion.3), channel_id=1, source_target_pairs={{0,16},{4,20},{8,24},{12,28},{16,0},{20,4},{24,8},{28,12},{1,17},{... | collective-permute-start | bytes 3932168 | tf_op jit(solution)/shard_map/ppermute | solution.py:30
  369.3 40.0 %collective-permute-start.45 = (f32[3,1280]{1,0:T(4,128)S(1)}, f32[3,1280]{1,0:T(4,128)S(1)}, u32[]{:S(2)}, u32[]{:S(2)}) collective-permute-start(f32[3,1280]{1,0:T(4,128)S(1)} %pad_maximum_fusion.13), channel_id=1, source_target_pairs={{0,4},{4,0},{8,12},{12,8},{16,20},{20,16},{24,28},{28,24},{1,5},{5... | collective-permute-start | bytes 46088 | tf_op jit(solution)/shard_map/ppermute | solution.py:30
  431.8 106.5 %reduce-scatter.5.cloned.1.call-start = ((), (), s32[]{:S(2)}) async-start(), calls=%async_computation.7 | async-start | bytes 4096000 | tf_op jit(solution)/shard_map/reduce_scatter | solution.py:1326
  506.8 30.5 %collective-permute-start.51 = (bf16[2,176,1280]{2,1,0:T(8,128)(2,1)}, bf16[2,176,1280]{2,1,0:T(8,128)(2,1)S(1)}, u32[]{:S(2)}, u32[]{:S(2)}) collective-permute-start(bf16[2,176,1280]{2,1,0:T(8,128)(2,1)} %get-tuple-element.356), channel_id=1, source_target_pairs={{0,8},{4,12},{8,0},{12,4},{16,24},{20,28},{24,16},{28,20},{1,9},{5... | collective-permute-start | bytes 2703368 | tf_op jit(solution)/shard_map/ppermute | solution.py:30
  507.7 29.6 %collective-permute-start.52 = (bf16[2,176,1280]{2,1,0:T(8,128)(2,1)}, bf16[2,176,1280]{2,1,0:T(8,128)(2,1)}, u32[]{:S(2)}, u32[]{:S(2)}) collective-permute-start(bf16[2,176,1280]{2,1,0:T(8,128)(2,1)} %get-tuple-element.357), channel_id=1, source_target_pairs={{0,16},{4,20},{8,24},{12,28},{16,0},{20,4},{24,8},{28,12},{1,17},{... | collective-permute-start | bytes 2703368 | tf_op jit(solution)/shard_map/ppermute | solution.py:30
  512.2 23.1 %all-to-all-start.2 = ((bf16[4,160,384]{2,1,0:T(8,128)(2,1)}), bf16[4,160,384]{2,1,0:T(8,128)(2,1)}, u32[]{:S(2)}, u32[]{:S(2)}) async-start(bf16[4,160,384]{2,1,0:T(8,128)(2,1)} %bitcast.179), calls=%async_computation.4 | async-start | bytes 983040 | tf_op jit(solution)/shard_map/all_to_all | solution.py:1166
  563.1 31.8 %collective-permute-start.62 = (bf16[256,1280]{1,0:T(8,128)(2,1)S(1)}, bf16[256,1280]{1,0:T(8,128)(2,1)}, u32[]{:S(2)}, u32[]{:S(2)}) collective-permute-start(bf16[256,1280]{1,0:T(8,128)(2,1)S(1)} %get-tuple-element.488), channel_id=1, source_target_pairs={{2,0},{6,1},{0,2},{4,3},{3,4},{7,5},{1,6},{5,7},{10,8},{14,9},{8,1... | collective-permute-start | bytes 1966088 | tf_op jit(solution)/shard_map/ppermute | solution.py:1039
  565.9 29.9 %collective-permute-start.61 = (bf16[256,1280]{1,0:T(8,128)(2,1)S(1)}, bf16[256,1280]{1,0:T(8,128)(2,1)}, u32[]{:S(2)}, u32[]{:S(2)}) collective-permute-start(bf16[256,1280]{1,0:T(8,128)(2,1)S(1)} %get-tuple-element.489), channel_id=1, source_target_pairs={{0,0},{4,1},{2,2},{6,3},{1,4},{5,5},{3,6},{7,7},{8,8},{12,9},{10,1... | collective-permute-start | bytes 1966088 | tf_op jit(solution)/shard_map/ppermute | solution.py:1039
  599.7 40.7 %all-to-all-start.3 = ((bf16[4,160,640]{2,1,0:T(8,128)(2,1)}), bf16[4,160,640]{2,1,0:T(8,128)(2,1)S(1)}, u32[]{:S(2)}, u32[]{:S(2)}) async-start(bf16[4,160,640]{2,1,0:T(8,128)(2,1)} %bitcast.178), calls=%async_computation.5 | async-start | bytes 1638400 | tf_op jit(solution)/shard_map/all_to_all | solution.py:1166
  608.1 23.4 %collective-permute-start.69 = (bf16[176,640]{1,0:T(8,128)(2,1)S(1)}, bf16[176,640]{1,0:T(8,128)(2,1)S(1)}, u32[]{:S(2)}, u32[]{:S(2)}) collective-permute-start(bf16[176,640]{1,0:T(8,128)(2,1)S(1)} %get-tuple-element.408), channel_id=1, source_target_pairs={{0,4},{1,5},{2,6},{3,7},{4,2},{5,3},{6,0},{7,1},{8,12},{9,13},{10,... | collective-permute-start | bytes 675848 | tf_op jit(solution)/shard_map/ppermute | solution.py:1039
  (134 other events, 1473.9 us)
Sparse Core Ops, SparseCore 0:
  99.3 65.9 all-gather.4
  166.9 42.1 all-gather.6
  432.0 42.5 reduce-scatter.2
  476.7 61.5 reduce-scatter.4

commit v5 on v4

--- a/solution.py
+++ b/solution.py
@@ -149,7 +149,7 @@
     n, depth = rows.shape
     width = weight.shape[1]
     tile = 2 * LANES
-    block = 512
+    block = n
 
     def kernel(rows_ref, weight_ref, gain_ref, out_ref, raw_ref):
         means = head_means(tile)

time: 657 us -> 657 us (level)
  no operation moved by 1% of the time
where the time goes in v5:
time: 657 us; the launch traced here: 649 us
  Pallas kernels  291 us (44%)
  waiting for transfers between devices  134 us (20%)
  starting transfers between devices  109 us (17%)
  local copies, waits for them, and re-layouts  64.2 us (10%)
  other arithmetic  34.7 us (5%)
  between operations  15.9 us (2%)
    ppermute x23, waiting for transfers between devices, across(): lax.ppermute(value, ALL, [(a * count + b, c * count + d) for (a, b), (c,...  65.8 us
    ppermute x48, waiting for transfers between devices, swap(): return lax.ppermute(value, DP, [(i, i ^ bit) for i in range(count)])  55.8 us
    pallas_call x4, Pallas kernels, rows_product(): pl.pallas_call(kernel, grid=(sum(steps),), in_specs=[pl.BlockSpec((n, dep...  49 us
    ppermute x23, starting transfers between devices, across(): lax.ppermute(value, ALL, [(a * count + b, c * count + d) for (a, b), (c,...  47.2 us
    ppermute x48, starting transfers between devices, swap(): return lax.ppermute(value, DP, [(i, i ^ bit) for i in range(count)])  45.7 us
    pallas_call x3, Pallas kernels, mlp_backward(): pl.pallas_call(kernel, grid=(steps,), in_specs=chunk_specs(blocks, depth)...  44.6 us
    unnamed x177, local copies, waits for them, and re-layouts  41.5 us
    pallas_call x1, Pallas kernels, attend_backward(): pl.pallas_call(kernel, grid=(pairs,), in_specs=[block, keys, block, block...  28.8 us
  transfers between devices with their start and end apart: 79, of which 26 were waited for; matrix products, arithmetic and copies ran while one was open for 8% of the time, Pallas kernels for 39%

profile of v5, /device:TPU:0, one launch (start us, length us, event | category | flops | bytes accessed | tf_op | source)
XLA Modules:
  0.0 648.9 jit_solution(15635452623729274850)
XLA Ops:
  35.4 11.8 %collective-permute-done.9 = bf16[2,176,640]{2,1,0:T(8,128)(2,1)S(1)} collective-permute-done((bf16[2,176,640]{2,1,0:T(8,128)(2,1)}, bf16[2,176,640]{2,1,0:T(8,128)(2,1)S(1)}, u32[]{:S(2)}, u32[]{:S(2)}) %collective-permute-start.9) | collective-permute-done | bytes 450592 | tf_op jit(solution)/shard_map/ppermute | solution.py:1039
  60.0 7.0 %collective-permute-start.17 = (bf16[128,1280]{1,0:T(8,128)(2,1)S(1)}, bf16[128,1280]{1,0:T(8,128)(2,1)S(1)}, u32[]{:S(2)}, u32[]{:S(2)}) collective-permute-start(bf16[128,1280]{1,0:T(8,128)(2,1)S(1)} %dynamic-slice_bitcast_fusion.6), channel_id=1, source_target_pairs={{0,2},{1,6},{2,0},{3,4},{4,3},{5,7},{6,1},{7,5},{8,10},{9,14},{10,... | collective-permute-start | bytes 983048 | tf_op jit(solution)/shard_map/ppermute | solution.py:1039
  71.2 9.6 %collective-permute-done.17 = bf16[128,1280]{1,0:T(8,128)(2,1)S(1)} collective-permute-done((bf16[128,1280]{1,0:T(8,128)(2,1)S(1)}, bf16[128,1280]{1,0:T(8,128)(2,1)S(1)}, u32[]{:S(2)}, u32[]{:S(2)}) %collective-permute-start.17) | collective-permute-done | bytes 327712 | tf_op jit(solution)/shard_map/ppermute | solution.py:1039
  117.1 8.4 %shard_map.258 = (bf16[1024,1280]{1,0:T(8,128)(2,1)S(1)}, bf16[1024,1280]{1,0:T(8,128)(2,1)S(1)}) custom-call(bf16[1024,1280]{1,0:T(8,128)(2,1)} %bitcast.132, bf16[1280,1280]{1,0:T(8,128)(2,1)} %bitcast.166, f32[1,1280]{1,0:T(1,128)S(1)} %broadcast_in_dim.116.gain_ref), custom_call_target="tpu_custom_call" | custom-call | flops 1 | bytes 1 | tf_op jit(solution)/shard_map/pallas_call | solution.py:163
  127.1 15.6 %shard_map.260 = (bf16[1024,640]{1,0:T(8,128)(2,1)S(1)}, f32[5,8,1024]{2,1,0:T(8,128)S(1)}) custom-call(bf16[1024,1280]{1,0:T(8,128)(2,1)S(1)} %get-tuple-element.239.q_ref.k_ref, bf16[1024,1280]{1,0:T(8,128)(2,1)S(1)} %get-tuple-element.239.q_ref.k_ref, bf16[1024,640]{1,0:T(8,128)(2,1)S(1)} %shard_map.259.v_ref, f32[1,1024]{1,0:T(1,128)S(1)} %bitcast.158, ...), custom_call_target="tpu_custom_call" | custom-call | flops 1 | bytes 1 | tf_op jit(solution)/shard_map/pallas_call | solution.py:225
  159.3 6.0 all-gather.5.cloned.1.call-done
  172.0 5.5 shard_map.265
  179.2 8.0 %shard_map.266 = (bf16[2048,1280]{1,0:T(8,128)(2,1)}, bf16[2048,1280]{1,0:T(8,128)(2,1)}, bf16[512,1280]{1,0:T(8,128)(2,1)S(1)}, bf16[512,1280]{1,0:T(8,128)(2,1)S(1)}, bf16[512,1280]{1,0:T(8,128)(2,1)S(1)}) custom-call(bf16[512,1280]{1,0:T(8,128)(2,1)} %get-tuple-element.252.refs_0_, bf16[1280,1280]{1,0:T(8,128)(2,1)} %bitcast.125, ...), custom_call_target="tpu_custom_call" | custom-call | flops 1 | bytes 1 | tf_op jit(solution)/shard_map/pallas_call | solution.py:653
  188.3 8.8 %collective-permute-done.25.refs_1_ = bf16[512,1280]{1,0:T(8,128)(2,1)S(1)} collective-permute-done((bf16[512,1280]{1,0:T(8,128)(2,1)}, bf16[512,1280]{1,0:T(8,128)(2,1)S(1)}, u32[]{:S(2)}, u32[]{:S(2)}) %collective-permute-start.25) | collective-permute-done | bytes 1310752 | tf_op jit(solution)/shard_map/ppermute | solution.py:30
  202.1 11.3 %shard_map.267 = (bf16[2048,1280]{1,0:T(8,128)(2,1)}, bf16[2048,1280]{1,0:T(8,128)(2,1)}, bf16[1024,1280]{1,0:T(8,128)(2,1)S(1)}, bf16[1024,1280]{1,0:T(8,128)(2,1)}, bf16[1024,1280]{1,0:T(8,128)(2,1)}) custom-call(bf16[512,1280]{1,0:T(8,128)(2,1)S(1)} %collective-permute-done.24.refs_0_, ...), custom_call_target="tpu_custom_call", output_to_operand_aliasing={{0}: (5, {}), {1}: (6, {})} | custom-call | flops 1 | bytes 1 | tf_op jit(solution)/shard_map/pallas_call | solution.py:653
  216.9 8.1 %shard_map.271 = (bf16[2048,1280]{1,0:T(8,128)(2,1)}, bf16[2048,1280]{1,0:T(8,128)(2,1)}, bf16[512,1280]{1,0:T(8,128)(2,1)S(1)}, bf16[512,1280]{1,0:T(8,128)(2,1)S(1)}, bf16[512,1280]{1,0:T(8,128)(2,1)S(1)}) custom-call(bf16[256,1280]{1,0:T(8,128)(2,1)} %collective-permute-done.28.refs_0_, ...), custom_call_target="tpu_custom_call", output_to_operand_aliasing={{0}: (5, {}), {1}: (6, {})} | custom-call | flops 1 | bytes 1 | tf_op jit(solution)/shard_map/pallas_call | solution.py:653
  228.7 6.1 shard_map.270
  246.9 28.1 %collective-permute-done.34.refs_7_ = bf16[256,1280]{1,0:T(8,128)(2,1)S(1)} collective-permute-done((bf16[256,1280]{1,0:T(8,128)(2,1)S(1)}, bf16[256,1280]{1,0:T(8,128)(2,1)S(1)}, u32[]{:S(2)}, u32[]{:S(2)}) %collective-permute-start.34) | collective-permute-done | bytes 655392 | tf_op jit(solution)/shard_map/ppermute | solution.py:1039
  279.8 12.9 %collective-permute-done.36.refs_4_ = bf16[256,1280]{1,0:T(8,128)(2,1)S(1)} collective-permute-done((bf16[256,1280]{1,0:T(8,128)(2,1)}, bf16[256,1280]{1,0:T(8,128)(2,1)S(1)}, u32[]{:S(2)}, u32[]{:S(2)}) %collective-permute-start.36) | collective-permute-done | bytes 655392 | tf_op jit(solution)/shard_map/ppermute | solution.py:30
  294.0 6.7 %shard_map.273 = (bf16[512,1280]{1,0:T(8,128)(2,1)S(1)}, f32[512,1280]{1,0:T(8,128)}, bf16[512,1280]{1,0:T(8,128)(2,1)S(1)}, f32[8,1280]{1,0:T(8,128)S(1)}) custom-call(s32[1]{0:T(128)} %bitcast.32.early_ref, bf16[512,1280]{1,0:T(8,128)(2,1)} %copy-done.27, bf16[512,1280]{1,0:T(8,128)(2,1)} %copy-done.69, bf16[512,1280]{1,0:T(8,128)(2,1)} %copy-done.70, ...), custom_call_target="tpu_custom_call" | custom-call | flops 1 | bytes 1 | tf_op jit(solution)/shard_map/pallas_call | solution.py:561
  306.5 6.9 %collective-permute-start.41 = (bf16[256,1280]{1,0:T(8,128)(2,1)}, bf16[256,1280]{1,0:T(8,128)(2,1)}, u32[]{:S(2)}, u32[]{:S(2)}) collective-permute-start(bf16[256,1280]{1,0:T(8,128)(2,1)} %get-tuple-element.493), channel_id=1, source_target_pairs={{0,0},{4,1},{2,2},{6,3},{1,4},{5,5},{3,6},{7,7},{8,8},{12,9},{10,1... | collective-permute-start | bytes 1966088 | tf_op jit(solution)/shard_map/ppermute | solution.py:1039
  313.5 12.3 %shard_map.274 = (bf16[2048,1280]{1,0:T(8,128)(2,1)}, bf16[2048,1280]{1,0:T(8,128)(2,1)}, bf16[2048,1280]{1,0:T(8,128)(2,1)}, bf16[512,1280]{1,0:T(8,128)(2,1)S(1)}, f32[8,1280]{1,0:T(8,128)S(1)}) custom-call(bf16[512,1280]{1,0:T(8,128)(2,1)S(1)} %get-tuple-element.286.refs_0_, bf16[1280,1280]{1,0:T(8,128)(2,1)} %bitcast.120, ...), custom_call_target="tpu_custom_call" | custom-call | flops 1 | bytes 1 | tf_op jit(solution)/shard_map/pallas_call | solution.py:726
  334.3 19.5 %shard_map.275 = (bf16[2048,1280]{1,0:T(8,128)(2,1)}, bf16[2048,1280]{1,0:T(8,128)(2,1)}, bf16[2048,1280]{1,0:T(8,128)(2,1)}, bf16[1024,1280]{1,0:T(8,128)(2,1)S(1)}, f32[8,1280]{1,0:T(8,128)S(1)}) custom-call(bf16[512,1280]{1,0:T(8,128)(2,1)S(1)} %collective-permute-done.37.refs_0_, ...), custom_call_target="tpu_custom_call", output_to_operand_aliasing={{0}: (8, {}), {1}: (9, {}), {2}: (10, {})} | custom-call | flops 1 | bytes 1 | tf_op jit(solution)/shard_map/pallas_call | solution.py:726
  353.8 12.8 %shard_map.276 = (bf16[2048,1280]{1,0:T(8,128)(2,1)}, bf16[2048,1280]{1,0:T(8,128)(2,1)}, bf16[2048,1280]{1,0:T(8,128)(2,1)}, bf16[512,1280]{1,0:T(8,128)(2,1)S(1)}, f32[8,1280]{1,0:T(8,128)S(1)}) custom-call(bf16[256,1280]{1,0:T(8,128)(2,1)} %collective-permute-done.39.refs_0_, ...), custom_call_target="tpu_custom_call", output_to_operand_aliasing={{0}: (8, {}), {1}: (9, {}), {2}: (10, {})} | custom-call | flops 1 | bytes 1 | tf_op jit(solution)/shard_map/pallas_call | solution.py:726
  370.7 12.5 %shard_map.277 = bf16[1280,1280]{1,0:T(8,128)(2,1)S(1)} custom-call(bf16[2048,1280]{1,0:T(8,128)(2,1)} %get-tuple-element.313.refs_0_, bf16[2048,1280]{1,0:T(8,128)(2,1)} %get-tuple-element.314.refs_1_), custom_call_target="tpu_custom_call" | custom-call | flops 1 | bytes 1 | tf_op jit(solution)/shard_map/pallas_call | solution.py:426
  388.3 21.1 %shard_map.279 = bf16[1280,2560]{1,0:T(8,128)(2,1)} custom-call(bf16[2048,1280]{1,0:T(8,128)(2,1)S(1)} %bitcast.136, bf16[2048,1280]{1,0:T(8,128)(2,1)} %get-tuple-element.318.refs_1_, bf16[2048,1280]{1,0:T(8,128)(2,1)} %get-tuple-element.319.refs_2_), custom_call_target="tpu_custom_call" | custom-call | flops 1 | bytes 1 | tf_op jit(solution)/shard_map/pallas_call | solution.py:426
  415.0 5.7 shard_map.280
  422.6 5.8 shard_map.281
  434.2 7.5 %shard_map.282 = (f32[512,1280]{1,0:T(8,128)}, bf16[512,1280]{1,0:T(8,128)(2,1)S(1)}, f32[8,1280]{1,0:T(8,128)S(1)}) custom-call(bf16[512,1280]{1,0:T(8,128)(2,1)S(1)} %copy-done.52, bf16[512,1280]{1,0:T(8,128)(2,1)S(1)} %collective-permute-done.43.refs_1_, bf16[512,1280]{1,0:T(8,128)(2,1)} %collective-permute-done.44.refs_2_, ...), custom_call_target="tpu_custom_call" | custom-call | flops 1 | bytes 1 | tf_op jit(solution)/shard_map/pallas_call | solution.py:606
  448.0 5.6 shard_map.284
  459.1 28.8 %shard_map.286 = (bf16[1024,1280]{1,0:T(8,128)(2,1)}, bf16[1024,640]{1,0:T(8,128)(2,1)S(1)}, f32[8,640]{1,0:T(8,128)S(1)}) custom-call(bf16[1024,1280]{1,0:T(8,128)(2,1)} %copy-done.4, bf16[1024,1280]{1,0:T(8,128)(2,1)} %copy-done.4, bf16[1024,640]{1,0:T(8,128)(2,1)S(1)} %copy-done.15, bf16[1024,1280]{1,0:T(8,128)(2,1)} %copy-done.23, ...), custom_call_target="tpu_custom_call" | custom-call | flops 1 | bytes 1 | tf_op jit(solution)/shard_map/pallas_call | solution.py:325
  491.6 9.3 %shard_map.287 = bf16[1280,1280]{1,0:T(8,128)(2,1)} custom-call(bf16[1024,1280]{1,0:T(8,128)(2,1)S(1)} %bitcast.133, bf16[1024,1280]{1,0:T(8,128)(2,1)} %bitcast.138, bf16[1024,640]{1,0:T(8,128)(2,1)S(1)} %copy-done.29, bf16[1024,640]{1,0:T(8,128)(2,1)S(1)} %copy-done.18), custom_call_target="tpu_custom_call" | custom-call | flops 1 | bytes 1 | tf_op jit(solution)/shard_map/pallas_call | solution.py:426
  519.9 8.5 %shard_map.289 = bf16[1024,1280]{1,0:T(8,128)(2,1)S(1)} custom-call(bf16[1024,1280]{1,0:T(8,128)(2,1)} %get-tuple-element.378.refs_0_.refs_1_, bf16[1024,640]{1,0:T(8,128)(2,1)S(1)} %copy-done.30, bf16[1280,1280]{1,0:T(8,128)(2,1)} %bitcast.167, bf16[1280,640]{1,0:T(8,128)(2,1)S(1)} %bitcast.146), custom_call_target="tpu_custom_call" | custom-call | flops 1 | bytes 1 | tf_op jit(solution)/shard_map/pallas_call | solution.py:364
  530.0 5.3 all-to-all-done.2.block_ref
  548.0 6.2 shard_map.292
  567.9 15.7 %collective-permute-done.57.first_ref = bf16[2,176,1280]{2,1,0:T(8,128)(2,1)S(1)} collective-permute-done((bf16[2,176,1280]{2,1,0:T(8,128)(2,1)S(1)}, bf16[2,176,1280]{2,1,0:T(8,128)(2,1)S(1)}, u32[]{:S(2)}, u32[]{:S(2)}) %collective-permute-start.57) | collective-permute-done | bytes 901152 | tf_op jit(solution)/shard_map/ppermute | solution.py:30
  617.9 13.8 %collective-permute-done.69 = bf16[176,640]{1,0:T(8,128)(2,1)S(1)} collective-permute-done((bf16[176,640]{1,0:T(8,128)(2,1)S(1)}, bf16[176,640]{1,0:T(8,128)(2,1)S(1)}, u32[]{:S(2)}, u32[]{:S(2)}) %collective-permute-start.69) | collective-permute-done | bytes 225312 | tf_op jit(solution)/shard_map/ppermute | solution.py:1039
  (520 shorter events, 281.8 us)
Async XLA Ops:
  25.0 22.2 %collective-permute-start.9 = (bf16[2,176,640]{2,1,0:T(8,128)(2,1)}, bf16[2,176,640]{2,1,0:T(8,128)(2,1)S(1)}, u32[]{:S(2)}, u32[]{:S(2)}) collective-permute-start(bf16[2,176,640]{2,1,0:T(8,128)(2,1)} %pad_maximum_fusion.6), channel_id=1, source_target_pairs={{1,0},{2,1},{3,2},{0,3},{7,4},{4,5},{5,6},{6,7},{9,8},{10,9},{11,1... | collective-permute-start | bytes 1351688 | tf_op jit(solution)/shard_map/ppermute | solution.py:1039
  50.5 31.1 %collective-permute-start.14 = (bf16[2,160,640]{2,1,0:T(8,128)(2,1)S(1)}, bf16[2,160,640]{2,1,0:T(8,128)(2,1)S(1)}, u32[]{:S(2)}, u32[]{:S(2)}) collective-permute-start(bf16[2,160,640]{2,1,0:T(8,128)(2,1)S(1)} %get-tuple-element.225.refs_0_), channel_id=1, source_target_pairs={{0,16},{4,20},{8,24},{12,28},{16,0},{20,4},{24,8},{28,12},{1,17},{... | collective-permute-start | bytes 1228808 | tf_op jit(solution)/shard_map/ppermute | solution.py:30
  52.1 32.5 %collective-permute-start.13 = (bf16[2,160,640]{2,1,0:T(8,128)(2,1)S(1)}, bf16[2,160,640]{2,1,0:T(8,128)(2,1)}, u32[]{:S(2)}, u32[]{:S(2)}) collective-permute-start(bf16[2,160,640]{2,1,0:T(8,128)(2,1)S(1)} %get-tuple-element.225.refs_0_), channel_id=1, source_target_pairs={{0,8},{4,12},{8,0},{12,4},{16,24},{20,28},{24,16},{28,20},{1,9},{5... | collective-permute-start | bytes 1228808 | tf_op jit(solution)/shard_map/ppermute | solution.py:30
  53.6 45.6 %all-to-all-start = ((bf16[4,160,640]{2,1,0:T(8,128)(2,1)}), bf16[4,160,640]{2,1,0:T(8,128)(2,1)}, u32[]{:S(2)}, u32[]{:S(2)}) async-start(bf16[4,160,640]{2,1,0:T(8,128)(2,1)} %shard_map.254), calls=%async_computation | async-start | bytes 1638400 | tf_op jit(solution)/shard_map/all_to_all | solution.py:1194
  57.8 107.6 %all-gather.5.cloned.1.call-start = ((), (), s32[]{:S(2)}) async-start(), calls=%async_computation.8 | async-start | bytes 4096000 | tf_op jit(solution)/shard_map/all_gather | solution.py:1209
  101.4 42.9 %collective-permute-start.22 = (bf16[2,160,640]{2,1,0:T(8,128)(2,1)}, bf16[2,160,640]{2,1,0:T(8,128)(2,1)}, u32[]{:S(2)}, u32[]{:S(2)}) collective-permute-start(bf16[2,160,640]{2,1,0:T(8,128)(2,1)} %get-tuple-element.246.refs_0_), channel_id=1, source_target_pairs={{0,24},{4,28},{8,16},{12,20},{16,8},{20,12},{24,0},{28,4},{1,25},{... | collective-permute-start | bytes 1228808 | tf_op jit(solution)/shard_map/ppermute | solution.py:30
  104.0 40.3 %collective-permute-start.21 = (bf16[2,160,640]{2,1,0:T(8,128)(2,1)}, bf16[2,160,640]{2,1,0:T(8,128)(2,1)}, u32[]{:S(2)}, u32[]{:S(2)}) collective-permute-start(bf16[2,160,640]{2,1,0:T(8,128)(2,1)} %get-tuple-element.246.refs_0_), channel_id=1, source_target_pairs={{0,16},{4,20},{8,24},{12,28},{16,0},{20,4},{24,8},{28,12},{1,17},{... | collective-permute-start | bytes 1228808 | tf_op jit(solution)/shard_map/ppermute | solution.py:30
  104.5 39.7 %collective-permute-start.20 = (bf16[2,160,640]{2,1,0:T(8,128)(2,1)}, bf16[2,160,640]{2,1,0:T(8,128)(2,1)}, u32[]{:S(2)}, u32[]{:S(2)}) collective-permute-start(bf16[2,160,640]{2,1,0:T(8,128)(2,1)} %get-tuple-element.246.refs_0_), channel_id=1, source_target_pairs={{0,8},{4,12},{8,0},{12,4},{16,24},{20,28},{24,16},{28,20},{1,9},{5... | collective-permute-start | bytes 1228808 | tf_op jit(solution)/shard_map/ppermute | solution.py:30
  107.5 36.8 %all-to-all-start.1 = ((bf16[4,160,384]{2,1,0:T(8,128)(2,1)}), bf16[4,160,384]{2,1,0:T(8,128)(2,1)}, u32[]{:S(2)}, u32[]{:S(2)}) async-start(bf16[4,160,384]{2,1,0:T(8,128)(2,1)} %shard_map.261), calls=%async_computation.1 | async-start | bytes 983040 | tf_op jit(solution)/shard_map/all_to_all | solution.py:1203
  111.6 103.2 %all-gather.7.cloned.1.call-start = ((), (), s32[]{:S(2)}) async-start(), calls=%async_computation.9 | async-start | bytes 2457600 | tf_op jit(solution)/shard_map/all_gather | solution.py:1230
  165.4 323.6 %reduce-scatter.3.cloned.1.call-start = ((), (), s32[]{:S(2)}) async-start(), calls=%async_computation.6 | async-start | bytes 2457600 | tf_op jit(solution)/shard_map/reduce_scatter | solution.py:1318
  165.7 31.5 %collective-permute-start.25 = (bf16[512,1280]{1,0:T(8,128)(2,1)}, bf16[512,1280]{1,0:T(8,128)(2,1)S(1)}, u32[]{:S(2)}, u32[]{:S(2)}) collective-permute-start(bf16[512,1280]{1,0:T(8,128)(2,1)} %get-tuple-element.252.refs_0_), channel_id=1, source_target_pairs={{0,16},{4,20},{8,24},{12,28},{16,0},{20,4},{24,8},{28,12},{1,17},{... | collective-permute-start | bytes 3932168 | tf_op jit(solution)/shard_map/ppermute | solution.py:30
  167.2 31.1 %collective-permute-start.24 = (bf16[512,1280]{1,0:T(8,128)(2,1)}, bf16[512,1280]{1,0:T(8,128)(2,1)S(1)}, u32[]{:S(2)}, u32[]{:S(2)}) collective-permute-start(bf16[512,1280]{1,0:T(8,128)(2,1)} %get-tuple-element.252.refs_0_), channel_id=1, source_target_pairs={{0,8},{4,12},{8,0},{12,4},{16,24},{20,28},{24,16},{28,20},{1,9},{5... | collective-permute-start | bytes 3932168 | tf_op jit(solution)/shard_map/ppermute | solution.py:30
  241.9 33.1 %collective-permute-start.31 = (bf16[512,1280]{1,0:T(8,128)(2,1)S(1)}, bf16[512,1280]{1,0:T(8,128)(2,1)S(1)}, u32[]{:S(2)}, u32[]{:S(2)}) collective-permute-start(bf16[512,1280]{1,0:T(8,128)(2,1)S(1)} %pad_maximum_fusion), channel_id=1, source_target_pairs={{0,8},{4,12},{8,0},{12,4},{16,24},{20,28},{24,16},{28,20},{1,9},{5... | collective-permute-start | bytes 3932168 | tf_op jit(solution)/shard_map/ppermute | solution.py:30
  243.4 31.6 %collective-permute-start.32 = (bf16[512,1280]{1,0:T(8,128)(2,1)S(1)}, bf16[512,1280]{1,0:T(8,128)(2,1)S(1)}, u32[]{:S(2)}, u32[]{:S(2)}) collective-permute-start(bf16[512,1280]{1,0:T(8,128)(2,1)S(1)} %pad_maximum_fusion.1), channel_id=1, source_target_pairs={{0,16},{4,20},{8,24},{12,28},{16,0},{20,4},{24,8},{28,12},{1,17},{... | collective-permute-start | bytes 3932168 | tf_op jit(solution)/shard_map/ppermute | solution.py:30
  245.0 30.0 %collective-permute-start.34 = (bf16[256,1280]{1,0:T(8,128)(2,1)S(1)}, bf16[256,1280]{1,0:T(8,128)(2,1)S(1)}, u32[]{:S(2)}, u32[]{:S(2)}) collective-permute-start(bf16[256,1280]{1,0:T(8,128)(2,1)S(1)} %get-tuple-element.494), channel_id=1, source_target_pairs={{0,2},{1,6},{2,0},{3,4},{4,3},{5,7},{6,1},{7,5},{8,10},{9,14},{10,... | collective-permute-start | bytes 1966088 | tf_op jit(solution)/shard_map/ppermute | solution.py:1039
  246.1 28.9 %collective-permute-start.33 = (bf16[256,1280]{1,0:T(8,128)(2,1)S(1)}, bf16[256,1280]{1,0:T(8,128)(2,1)S(1)}, u32[]{:S(2)}, u32[]{:S(2)}) collective-permute-start(bf16[256,1280]{1,0:T(8,128)(2,1)S(1)} %get-tuple-element.495), channel_id=1, source_target_pairs={{0,0},{1,4},{2,2},{3,6},{4,1},{5,5},{6,3},{7,7},{8,8},{9,12},{10,1... | collective-permute-start | bytes 1966088 | tf_op jit(solution)/shard_map/ppermute | solution.py:1039
  300.7 28.3 %collective-permute-start.38 = (bf16[512,1280]{1,0:T(8,128)(2,1)S(1)}, bf16[512,1280]{1,0:T(8,128)(2,1)S(1)}, u32[]{:S(2)}, u32[]{:S(2)}) collective-permute-start(bf16[512,1280]{1,0:T(8,128)(2,1)S(1)} %get-tuple-element.286.refs_0_), channel_id=1, source_target_pairs={{0,16},{4,20},{8,24},{12,28},{16,0},{20,4},{24,8},{28,12},{1,17},{... | collective-permute-start | bytes 3932168 | tf_op jit(solution)/shard_map/ppermute | solution.py:30
  302.1 28.2 %collective-permute-start.37 = (bf16[512,1280]{1,0:T(8,128)(2,1)S(1)}, bf16[512,1280]{1,0:T(8,128)(2,1)S(1)}, u32[]{:S(2)}, u32[]{:S(2)}) collective-permute-start(bf16[512,1280]{1,0:T(8,128)(2,1)S(1)} %get-tuple-element.286.refs_0_), channel_id=1, source_target_pairs={{0,8},{4,12},{8,0},{12,4},{16,24},{20,28},{24,16},{28,20},{1,9},{5... | collective-permute-start | bytes 3932168 | tf_op jit(solution)/shard_map/ppermute | solution.py:30
  304.7 49.1 %collective-permute-start.42 = (bf16[256,1280]{1,0:T(8,128)(2,1)}, bf16[256,1280]{1,0:T(8,128)(2,1)}, u32[]{:S(2)}, u32[]{:S(2)}) collective-permute-start(bf16[256,1280]{1,0:T(8,128)(2,1)} %get-tuple-element.492), channel_id=1, source_target_pairs={{2,0},{6,1},{0,2},{4,3},{3,4},{7,5},{1,6},{5,7},{10,8},{14,9},{8,1... | collective-permute-start | bytes 1966088 | tf_op jit(solution)/shard_map/ppermute | solution.py:1039
  306.5 47.3 %collective-permute-start.41 = (bf16[256,1280]{1,0:T(8,128)(2,1)}, bf16[256,1280]{1,0:T(8,128)(2,1)}, u32[]{:S(2)}, u32[]{:S(2)}) collective-permute-start(bf16[256,1280]{1,0:T(8,128)(2,1)} %get-tuple-element.493), channel_id=1, source_target_pairs={{0,0},{4,1},{2,2},{6,3},{1,4},{5,5},{3,6},{7,7},{8,8},{12,9},{10,1... | collective-permute-start | bytes 1966088 | tf_op jit(solution)/shard_map/ppermute | solution.py:1039
  367.1 42.3 %collective-permute-start.43 = (bf16[512,1280]{1,0:T(8,128)(2,1)S(1)}, bf16[512,1280]{1,0:T(8,128)(2,1)S(1)}, u32[]{:S(2)}, u32[]{:S(2)}) collective-permute-start(bf16[512,1280]{1,0:T(8,128)(2,1)S(1)} %pad_maximum_fusion.2), channel_id=1, source_target_pairs={{0,8},{4,12},{8,0},{12,4},{16,24},{20,28},{24,16},{28,20},{1,9},{5... | collective-permute-start | bytes 3932168 | tf_op jit(solution)/shard_map/ppermute | solution.py:30
  367.6 41.8 %collective-permute-start.44 = (bf16[512,1280]{1,0:T(8,128)(2,1)S(1)}, bf16[512,1280]{1,0:T(8,128)(2,1)}, u32[]{:S(2)}, u32[]{:S(2)}) collective-permute-start(bf16[512,1280]{1,0:T(8,128)(2,1)S(1)} %pad_maximum_fusion.3), channel_id=1, source_target_pairs={{0,16},{4,20},{8,24},{12,28},{16,0},{20,4},{24,8},{28,12},{1,17},{... | collective-permute-start | bytes 3932168 | tf_op jit(solution)/shard_map/ppermute | solution.py:30
  369.3 40.0 %collective-permute-start.45 = (f32[3,1280]{1,0:T(4,128)S(1)}, f32[3,1280]{1,0:T(4,128)S(1)}, u32[]{:S(2)}, u32[]{:S(2)}) collective-permute-start(f32[3,1280]{1,0:T(4,128)S(1)} %pad_maximum_fusion.13), channel_id=1, source_target_pairs={{0,4},{4,0},{8,12},{12,8},{16,20},{20,16},{24,28},{28,24},{1,5},{5... | collective-permute-start | bytes 46088 | tf_op jit(solution)/shard_map/ppermute | solution.py:30
  431.9 106.4 %reduce-scatter.5.cloned.1.call-start = ((), (), s32[]{:S(2)}) async-start(), calls=%async_computation.7 | async-start | bytes 4096000 | tf_op jit(solution)/shard_map/reduce_scatter | solution.py:1326
  506.8 30.5 %collective-permute-start.51 = (bf16[2,176,1280]{2,1,0:T(8,128)(2,1)}, bf16[2,176,1280]{2,1,0:T(8,128)(2,1)S(1)}, u32[]{:S(2)}, u32[]{:S(2)}) collective-permute-start(bf16[2,176,1280]{2,1,0:T(8,128)(2,1)} %get-tuple-element.356), channel_id=1, source_target_pairs={{0,8},{4,12},{8,0},{12,4},{16,24},{20,28},{24,16},{28,20},{1,9},{5... | collective-permute-start | bytes 2703368 | tf_op jit(solution)/shard_map/ppermute | solution.py:30
  507.7 29.6 %collective-permute-start.52 = (bf16[2,176,1280]{2,1,0:T(8,128)(2,1)}, bf16[2,176,1280]{2,1,0:T(8,128)(2,1)}, u32[]{:S(2)}, u32[]{:S(2)}) collective-permute-start(bf16[2,176,1280]{2,1,0:T(8,128)(2,1)} %get-tuple-element.357), channel_id=1, source_target_pairs={{0,16},{4,20},{8,24},{12,28},{16,0},{20,4},{24,8},{28,12},{1,17},{... | collective-permute-start | bytes 2703368 | tf_op jit(solution)/shard_map/ppermute | solution.py:30
  512.2 23.1 %all-to-all-start.2 = ((bf16[4,160,384]{2,1,0:T(8,128)(2,1)}), bf16[4,160,384]{2,1,0:T(8,128)(2,1)}, u32[]{:S(2)}, u32[]{:S(2)}) async-start(bf16[4,160,384]{2,1,0:T(8,128)(2,1)} %bitcast.179), calls=%async_computation.4 | async-start | bytes 983040 | tf_op jit(solution)/shard_map/all_to_all | solution.py:1166
  563.0 31.8 %collective-permute-start.62 = (bf16[256,1280]{1,0:T(8,128)(2,1)S(1)}, bf16[256,1280]{1,0:T(8,128)(2,1)}, u32[]{:S(2)}, u32[]{:S(2)}) collective-permute-start(bf16[256,1280]{1,0:T(8,128)(2,1)S(1)} %get-tuple-element.488), channel_id=1, source_target_pairs={{2,0},{6,1},{0,2},{4,3},{3,4},{7,5},{1,6},{5,7},{10,8},{14,9},{8,1... | collective-permute-start | bytes 1966088 | tf_op jit(solution)/shard_map/ppermute | solution.py:1039
  566.2 29.5 %collective-permute-start.61 = (bf16[256,1280]{1,0:T(8,128)(2,1)S(1)}, bf16[256,1280]{1,0:T(8,128)(2,1)}, u32[]{:S(2)}, u32[]{:S(2)}) collective-permute-start(bf16[256,1280]{1,0:T(8,128)(2,1)S(1)} %get-tuple-element.489), channel_id=1, source_target_pairs={{0,0},{4,1},{2,2},{6,3},{1,4},{5,5},{3,6},{7,7},{8,8},{12,9},{10,1... | collective-permute-start | bytes 1966088 | tf_op jit(solution)/shard_map/ppermute | solution.py:1039
  599.7 40.9 %all-to-all-start.3 = ((bf16[4,160,640]{2,1,0:T(8,128)(2,1)}), bf16[4,160,640]{2,1,0:T(8,128)(2,1)S(1)}, u32[]{:S(2)}, u32[]{:S(2)}) async-start(bf16[4,160,640]{2,1,0:T(8,128)(2,1)} %bitcast.178), calls=%async_computation.5 | async-start | bytes 1638400 | tf_op jit(solution)/shard_map/all_to_all | solution.py:1166
  608.0 23.7 %collective-permute-start.69 = (bf16[176,640]{1,0:T(8,128)(2,1)S(1)}, bf16[176,640]{1,0:T(8,128)(2,1)S(1)}, u32[]{:S(2)}, u32[]{:S(2)}) collective-permute-start(bf16[176,640]{1,0:T(8,128)(2,1)S(1)} %get-tuple-element.408), channel_id=1, source_target_pairs={{0,4},{1,5},{2,6},{3,7},{4,2},{5,3},{6,0},{7,1},{8,12},{9,13},{10,... | collective-permute-start | bytes 675848 | tf_op jit(solution)/shard_map/ppermute | solution.py:1039
  (134 other events, 1465.7 us)
Sparse Core Ops, SparseCore 0:
  99.3 65.9 all-gather.4
  166.9 42.1 all-gather.6
  432.0 42.4 reduce-scatter.2
  476.7 61.5 reduce-scatter.4
